TPU v7x, 32 devices: a whole 2x2x4 slice. The times are simulated.
32 devices in a mesh: band: 8 (over z, y), det: 4 (over x, core).
Axes of the slice: x: 2, y: 2, z: 4, core: 2. Of those that a mesh axis runs over, the one named last changes fastest.
Arguments:
- sky_coeffs: float32 [3, 2, 8, 2048], P(None, None, 'band', 'det'), may hold values from -6 to 6
- beam_coeffs: bfloat16 [4, 3, 2, 17, 2048], P('det'), may hold values from -2.5 to 2.5
- wigner_panel: bfloat16 [8, 17, 2048, 8], P('band', None, 'det'), may hold values from -0.125 to 0.125
- m_values: int32 [8], replicated, may hold values from 0 to 4095, as said below
- cycle_table: int32 [8, 3], replicated, may hold values from -1 to 7, as said below
- send_lists: int32 [4, 8, 8, 2], P('det'), may hold values from -1 to 12287, as said below
- sample_block: int32 [4, 32768], P('det', 'band'), may hold values from 0 to 15, as said below
- sample_phi: int32 [4, 32768], P('det', 'band'), may hold values from 0 to 126
- sample_psi: int32 [4, 32768], P('det', 'band'), may hold values from 0 to 31
- sample_frac: float32 [2, 4, 32768], P(None, 'det', 'band'), may hold values from 0 to 1
Outputs:
- timestream: float32 [4, 32768], P('det', 'band')
Inputs may be any that keep to these rules, and one draw needn't show every extreme that they name: `cycle_table`: each cycle stands in exactly one slot; -1 marks an empty slot; some cycle band fills all 3 slots, many hold none. `send_lists`: of one detector's entries from all bands to one owner, at most 8 are not -1, and every owner reaches 8; an entry from a band that holds no cycle is -1; an entry that is not -1 is slot * 4096 + start, with slot a filled slot of band src and start the block's first phi cell. `sample_block`: src * 2 + entry of an entry that is not -1 in the detector's list from band src to the sample's owner. `m_values`: distinct orders; 0 and 4095 among them.
All inputs are finite; a program needn't handle non-finite values.
Results may differ from a plain program's by a relative error of at most 0.0051.
Values may be sent and summed in bfloat16 or wider, within the bound.
No kernel may reach another device: no remote copies, remote signals or barrier semaphores. Data moves between devices by JAX's collectives and lax.ppermute only.
A program may use at most 64 MiB of HBM per device.

v0:
```python
import math

import jax
import jax.numpy as jnp
from jax import lax
from jax.sharding import PartitionSpec as P

BMAX = 8
MPRIME = 17
NPSI = 32
NPHI = 4096
BLOCK_PHI = 128


def psi_tables():
    cells = jnp.arange(NPSI, dtype=jnp.int32)
    orders = jnp.arange(MPRIME, dtype=jnp.int32) - BMAX
    turns = orders[:, None] * cells[None, :] % NPSI
    angle = 2.0 * math.pi / NPSI * turns.astype(jnp.float32)
    return (jnp.cos(angle), jnp.sin(angle))


def psi_items(incoming):
    highest = lax.Precision.HIGHEST
    cos_psi, sin_psi = psi_tables()
    real_part = jnp.einsum(
        "bimn,nj->bimj", incoming[:, :, 0], cos_psi, precision=highest
    ) - jnp.einsum("bimn,nj->bimj", incoming[:, :, 1], sin_psi, precision=highest)
    imag_part = jnp.einsum(
        "bimn,nj->bimj", incoming[:, :, 0], sin_psi, precision=highest
    ) + jnp.einsum("bimn,nj->bimj", incoming[:, :, 1], cos_psi, precision=highest)
    return jnp.stack([real_part, imag_part], 2).astype(jnp.bfloat16)


def phi_table(m_values, columns):
    turns = m_values[:, None] * columns[None, :] % NPHI
    angle = 2.0 * math.pi / NPHI * turns.astype(jnp.float32)
    return jnp.concatenate([jnp.cos(angle), -jnp.sin(angle)], 0).astype(jnp.bfloat16)


def cycle_cube(samples, table, scale):
    bands, items, parts, local_orders, cells = samples.shape
    rows = jnp.transpose(samples, (1, 4, 2, 0, 3)).reshape(
        items * cells, parts * bands * local_orders
    )
    values = jnp.dot(rows, table, preferred_element_type=jnp.float32) * scale
    return values.astype(jnp.bfloat16).reshape(items, cells, table.shape[1])


def interpolate(flat_cells, block_pos, cell_phi, cell_psi, frac_phi, frac_psi):
    psi_next = (cell_psi + 1) % NPSI
    base_index = block_pos * (NPSI * BLOCK_PHI)
    low_index = base_index + cell_psi * BLOCK_PHI + cell_phi
    high_index = base_index + psi_next * BLOCK_PHI + cell_phi
    value_ll = jnp.take(flat_cells, low_index).astype(jnp.float32)
    value_lh = jnp.take(flat_cells, low_index + 1).astype(jnp.float32)
    value_hl = jnp.take(flat_cells, high_index).astype(jnp.float32)
    value_hh = jnp.take(flat_cells, high_index + 1).astype(jnp.float32)
    low_row = (1.0 - frac_phi) * value_ll + frac_phi * value_lh
    high_row = (1.0 - frac_phi) * value_hl + frac_phi * value_hh
    return (1.0 - frac_psi) * low_row + frac_psi * high_row


def per_device(
    sky_coeffs,
    beam_coeffs,
    wigner_panel,
    m_values,
    cycle_table,
    send_lists,
    sample_block,
    sample_phi,
    sample_psi,
    sample_frac,
):
    highest = lax.Precision.HIGHEST
    orders_all = m_values.shape[0]
    scale = 2.0 / math.sqrt(orders_all * MPRIME)
    own_band = lax.axis_index("band")
    beams = lax.all_to_all(beam_coeffs, "det", split_axis=4, concat_axis=0, tiled=True).astype(
        jnp.float32
    )
    mix_real = jnp.einsum(
        "cmk,dcnk->dmnk", sky_coeffs[:, 0], beams[:, :, 0], precision=highest
    ) + jnp.einsum("cmk,dcnk->dmnk", sky_coeffs[:, 1], beams[:, :, 1], precision=highest)
    mix_imag = jnp.einsum(
        "cmk,dcnk->dmnk", sky_coeffs[:, 1], beams[:, :, 0], precision=highest
    ) - jnp.einsum("cmk,dcnk->dmnk", sky_coeffs[:, 0], beams[:, :, 1], precision=highest)
    mixed = jnp.stack([mix_real, mix_imag], 1).astype(jnp.bfloat16)
    coeff = lax.psum_scatter(
        jnp.einsum("dsmnk,mnkr->dsmnr", mixed, wigner_panel, preferred_element_type=jnp.float32),
        "det",
        scatter_dimension=0,
        tiled=True,
    )[0]
    lists = send_lists[0]
    cycle_index = jnp.maximum(cycle_table, 0)
    table = phi_table(m_values, jnp.arange(NPHI, dtype=jnp.int32))
    payload = jnp.transpose(jnp.take(coeff, cycle_index, axis=3), (3, 4, 0, 1, 2))
    cube = cycle_cube(
        psi_items(lax.all_to_all(payload, "band", split_axis=0, concat_axis=0, tiled=True)),
        table,
        scale,
    )
    my_codes = jnp.maximum(lax.dynamic_index_in_dim(lists, own_band, 0, keepdims=False), 0)
    slot_index = my_codes // NPHI
    start_cell = my_codes % NPHI
    wrapped = jnp.concatenate([cube, cube[:, :, :BLOCK_PHI]], 2)

    def cut_block(slot_one, start_one):
        return lax.dynamic_slice(wrapped, (slot_one, 0, start_one), (1, NPSI, BLOCK_PHI))[0]

    outgoing = jax.vmap(jax.vmap(cut_block))(slot_index, start_cell)
    received = lax.all_to_all(outgoing, "band", split_axis=0, concat_axis=0, tiled=True)
    flat_cells = received.reshape(-1)
    block_pos = sample_block[0]
    values = interpolate(
        flat_cells, block_pos, sample_phi[0], sample_psi[0], sample_frac[0, 0], sample_frac[1, 0]
    )
    return values[None, :]


def solution(mesh):
    return jax.shard_map(
        per_device,
        mesh=mesh,
        in_specs=(
            P(None, None, "band", "det"),
            P("det", None, None, None, None),
            P("band", None, "det", None),
            P(),
            P(),
            P("det", None, None, None),
            P("det", "band"),
            P("det", "band"),
            P("det", "band"),
            P(None, "det", "band"),
        ),
        out_specs=P("det", "band"),
        check_vma=False,
    )
```

profile of v0, /device:TPU:0, one launch (start us, length us, event | category | flops | bytes accessed | tf_op | source)
XLA Modules:
  0.0 214.6 jit_solution(8219433095090991698)
XLA Ops:
  6.5 7.2 %copy.50 = bf16[1,3,2,17,2048]{3,2,1,0,4:T(2,128)(2,1)S(1)} copy(bf16[1,3,2,17,2048]{4,2,3,1,0:T(2,128)(2,1)} %param.13) | data formatting | bytes 835584 | tf_op args[1]
  13.8 0.0 copy-start.6
  13.8 0.0 copy-start.5
  13.8 0.0 copy-start.7
  13.8 0.0 copy-start.2
  13.8 0.0 copy-start.3
  13.9 0.0 copy-start.1
  13.9 5.4 %reshape.300 = bf16[4,2,26112]{2,1,0:T(2,128)(2,1)} reshape(bf16[2048,1,3,2,17]{4,3,2,1,0:T(2,128)(2,1)S(1)} %bitcast.141) | data formatting | bytes 835584
  19.3 4.2 %all-to-all-start = ((bf16[4,2,26112]{2,1,0:T(2,128)(2,1)}), bf16[4,2,26112]{2,1,0:T(2,128)(2,1)}, u32[]{:S(2)}, u32[]{:S(2)}) async-start(bf16[4,2,26112]{2,1,0:T(2,128)(2,1)} %reshape.300), calls=%async_computation | async-start | bytes 835584 | tf_op jit(solution)/shard_map/all_to_all | solution.py:80
  23.5 0.1 copy.54
  23.6 0.1 reshape.259
  23.7 0.6 cosine_convert_fusion
  24.4 7.3 %all-to-all-done = bf16[4,2,26112]{2,1,0:T(2,128)(2,1)} async-done(((bf16[4,2,26112]{2,1,0:T(2,128)(2,1)}), bf16[4,2,26112]{2,1,0:T(2,128)(2,1)}, u32[]{:S(2)}, u32[]{:S(2)}) %all-to-all-start) | async-done | bytes 417824 | tf_op jit(solution)/shard_map/all_to_all | solution.py:80
  31.8 8.1 %reshape.301 = bf16[2048,1,3,2,17]{4,3,2,1,0:T(2,128)(2,1)S(1)} reshape(bf16[4,2,26112]{2,1,0:T(2,128)(2,1)} %all-to-all-done) | data formatting | bytes 835584
  39.8 6.1 %copy.51 = bf16[1,3,2,17,4,512]{5,4,3,1,2,0:T(4,128)(2,1)} copy(bf16[1,3,2,17,4,512]{3,2,1,5,4,0:T(2,128)(2,1)S(1)} %bitcast.140) | data formatting | bytes 835584 | tf_op jit(solution)/shard_map/all_to_all | solution.py:80
  45.9 1.6 fusion.7
  47.6 0.1 fusion.22
  47.6 0.1 fusion.23
  47.7 0.2 convolution_bitcast_fusion
  47.9 0.7 copy.52
  48.6 0.0 reduce-scatter.2.cloned.1.call-update
  48.7 0.7 fusion.53
  49.4 0.1 copy.49
  49.5 19.9 %reduce-scatter.2.cloned.1.call-done = f32[1,2,1,17,8]{3,4,2,1,0:T(8,128)} async-done(((f32[4,2,1,17,8]{3,4,2,1,0:T(8,128)}), f32[1,2,1,17,8]{3,4,2,1,0:T(8,128)}) %reduce-scatter.2.cloned.1.call-update) | async-done | bytes 1104 | tf_op jit(solution)/shard_map/reduce_scatter | solution.py:90
  69.3 0.7 copy.104
  70.0 0.6 gather_fusion
  70.6 0.7 select_bitcast_fusion
  71.3 5.5 %all-to-all-start.1 = ((f32[8,3,2,1,17]{4,2,3,1,0:T(2,128)}), f32[8,3,2,1,17]{4,2,3,1,0:T(2,128)S(1)}, u32[]{:S(2)}, u32[]{:S(2)}) async-start(f32[8,3,2,1,17]{4,2,3,1,0:T(2,128)} %select_bitcast_fusion), calls=%async_computation.2 | async-start | bytes 49152 | tf_op jit(solution)/shard_map/all_to_all | solution.py:101
  76.8 0.1 copy.59
  76.9 0.1 reshape.266
  77.0 6.5 %all-to-all-done.1 = f32[8,3,2,1,17]{4,2,3,1,0:T(2,128)S(1)} async-done(((f32[8,3,2,1,17]{4,2,3,1,0:T(2,128)}), f32[8,3,2,1,17]{4,2,3,1,0:T(2,128)S(1)}, u32[]{:S(2)}, u32[]{:S(2)}) %all-to-all-start.1) | async-done | bytes 3296 | tf_op jit(solution)/shard_map/all_to_all | solution.py:101
  83.5 0.3 fusion.39
  83.8 0.3 fusion.35
  84.0 0.3 fusion.4
  84.3 0.3 fusion.3
  84.6 0.1 reshape.220
  84.7 0.4 fusion
  85.1 0.1 pad_maximum_fusion
  85.2 4.6 %copy.60 = bf16[3,32,4224]{1,0,2:T(4,128)(2,1)} copy(bf16[3,32,4224]{2,1,0:T(8,128)(2,1)S(1)} %pad_maximum_fusion) | data formatting | bytes 1622016 | tf_op jit(solution)/shard_map/concatenate | solution.py:108
  89.8 3.0 %gather_fusion.1 = bf16[16,32,128]{1,0,2:T(8,128)(2,1)S(1)} fusion(bf16[3,32,4224]{1,0,2:T(4,128)(2,1)} %copy.60, s32[16]{0:T(128)S(1)} %reshape.266), kind=kCustom, calls=%fused_computation.5 | custom fusion | bytes 262336 | tf_op jit(solution)/shard_map/vmap(vmap())/gather | solution.py:111
  92.9 1.0 copy.61
  93.9 3.4 %all-to-all-start.2 = ((bf16[8,2,32,128]{3,2,1,0:T(8,128)(2,1)}), bf16[8,2,32,128]{3,2,1,0:T(8,128)(2,1)S(1)}, u32[]{:S(2)}, u32[]{:S(2)}) async-start(bf16[8,2,32,128]{3,2,1,0:T(8,128)(2,1)} %copy.61), calls=%async_computation.3 | async-start | bytes 262144 | tf_op jit(solution)/shard_map/all_to_all | solution.py:114
  97.4 7.2 %all-to-all-done.2 = bf16[8,2,32,128]{3,2,1,0:T(8,128)(2,1)S(1)} async-done(((bf16[8,2,32,128]{3,2,1,0:T(8,128)(2,1)}), bf16[8,2,32,128]{3,2,1,0:T(8,128)(2,1)S(1)}, u32[]{:S(2)}, u32[]{:S(2)}) %all-to-all-start.2) | async-done | bytes 131104 | tf_op jit(solution)/shard_map/all_to_all | solution.py:114
  104.6 25.6 %gather_fusion.4 = bf16[4096]{0:T(1024)(128)(2,1)S(1)} fusion(bf16[65536]{0:T(1024)(128)(2,1)S(1)} %bitcast.136, s32[4096]{0:T(1024)S(1)} %get-tuple-element.31), kind=kCustom, calls=%fused_computation.2.clone | custom fusion | bytes 32768 | tf_op jit(solution)/shard_map/jit(_take)/gather | solution.py:57
  130.2 25.6 %gather_fusion.2 = bf16[4096]{0:T(1024)(128)(2,1)S(1)} fusion(bf16[65536]{0:T(1024)(128)(2,1)S(1)} %bitcast.137, s32[4096]{0:T(1024)S(1)} %get-tuple-element.30), kind=kCustom, calls=%fused_computation.clone | custom fusion | bytes 32768 | tf_op jit(solution)/shard_map/jit(_take)/gather | solution.py:55
  155.9 25.6 %gather_fusion.3 = bf16[4096]{0:T(1024)(128)(2,1)S(1)} fusion(bf16[65536]{0:T(1024)(128)(2,1)S(1)} %bitcast.138, s32[4096]{0:T(1024)S(1)} %get-tuple-element.16), kind=kCustom, calls=%fused_computation.1.clone | custom fusion | bytes 32768 | tf_op jit(solution)/shard_map/jit(_take)/gather | solution.py:56
  181.5 25.6 %gather_fusion.5 = bf16[4096]{0:T(1024)(128)(2,1)S(1)} fusion(bf16[65536]{0:T(1024)(128)(2,1)S(1)} %bitcast.139, s32[4096]{0:T(1024)S(1)} %get-tuple-element.12), kind=kCustom, calls=%fused_computation.3.clone | custom fusion | bytes 32768 | tf_op jit(solution)/shard_map/jit(_take)/gather | solution.py:58
  207.1 0.6 multiply_add_fusion
  (26 shorter events, 0.2 us)
Async XLA Ops:
  6.5 41.2 %copy-start = (bf16[1,17,512,8]{2,3,1,0:T(8,128)(2,1)S(1)}, bf16[1,17,512,8]{2,3,1,0:T(8,128)(2,1)}, u32[]{:S(2)}) copy-start(bf16[1,17,512,8]{2,3,1,0:T(8,128)(2,1)} %param.14) | copy-start | bytes 417796
  13.8 9.7 %copy-start.6 = (s32[8,3]{0,1:T(4,128)S(1)}, s32[8,3]{0,1:T(4,128)}, u32[]{:S(2)}) copy-start(s32[8,3]{0,1:T(4,128)} %param.16) | copy-start | bytes 292
  13.8 9.7 %copy-start.5 = (f32[3,2,1,512]{3,2,1,0:T(1,128)S(1)}, f32[3,2,1,512]{3,2,1,0:T(1,128)}, u32[]{:S(2)}) copy-start(f32[3,2,1,512]{3,2,1,0:T(1,128)} %param.12) | copy-start | bytes 36868
  13.8 9.9 %copy-start.7 = (s32[8]{0:T(128)S(1)}, s32[8]{0:T(128)}, u32[]{:S(2)}) copy-start(s32[8]{0:T(128)} %param.15) | copy-start | bytes 100
  13.8 10.5 %copy-start.2 = (s32[1,4096]{1,0:T(1,128)S(1)}, s32[1,4096]{1,0:T(1,128)}, u32[]{:S(2)}) copy-start(s32[1,4096]{1,0:T(1,128)} %param.20) | copy-start | bytes 49156
  13.8 10.5 %copy-start.3 = (s32[1,4096]{1,0:T(1,128)S(1)}, s32[1,4096]{1,0:T(1,128)}, u32[]{:S(2)}) copy-start(s32[1,4096]{1,0:T(1,128)} %param.18) | copy-start | bytes 49156
  13.9 10.5 %copy-start.1 = (f32[2,1,4096]{2,1,0:T(1,128)S(1)}, f32[2,1,4096]{2,1,0:T(1,128)}, u32[]{:S(2)}) copy-start(f32[2,1,4096]{2,1,0:T(1,128)} %param.21) | copy-start | bytes 98308
  19.3 12.5 %all-to-all-start = ((bf16[4,2,26112]{2,1,0:T(2,128)(2,1)}), bf16[4,2,26112]{2,1,0:T(2,128)(2,1)}, u32[]{:S(2)}, u32[]{:S(2)}) async-start(bf16[4,2,26112]{2,1,0:T(2,128)(2,1)} %reshape.300), calls=%async_computation | async-start | bytes 835584 | tf_op jit(solution)/shard_map/all_to_all | solution.py:80
  23.5 45.9 %reduce-scatter.2.cloned.1.call-start = ((), (), s32[]{:S(2)}) async-start(), calls=%async_computation.4 | async-start | bytes 40960 | tf_op jit(solution)/shard_map/reduce_scatter | solution.py:90
  71.3 12.1 %all-to-all-start.1 = ((f32[8,3,2,1,17]{4,2,3,1,0:T(2,128)}), f32[8,3,2,1,17]{4,2,3,1,0:T(2,128)S(1)}, u32[]{:S(2)}, u32[]{:S(2)}) async-start(f32[8,3,2,1,17]{4,2,3,1,0:T(2,128)} %select_bitcast_fusion), calls=%async_computation.2 | async-start | bytes 49152 | tf_op jit(solution)/shard_map/all_to_all | solution.py:101
  89.8 7.5 %copy-start.4 = (s32[1,4096]{1,0:T(1,128)S(1)}, s32[1,4096]{1,0:T(1,128)}, u32[]{:S(2)}) copy-start(s32[1,4096]{1,0:T(1,128)} %param.19) | copy-start | bytes 49156
  93.9 10.7 %all-to-all-start.2 = ((bf16[8,2,32,128]{3,2,1,0:T(8,128)(2,1)}), bf16[8,2,32,128]{3,2,1,0:T(8,128)(2,1)S(1)}, u32[]{:S(2)}, u32[]{:S(2)}) async-start(bf16[8,2,32,128]{3,2,1,0:T(8,128)(2,1)} %copy.61), calls=%async_computation.3 | async-start | bytes 262144 | tf_op jit(solution)/shard_map/all_to_all | solution.py:114
Sparse Core Ops, SparseCore 0:
  48.8 20.4 reduce-scatter.1
where the time goes:
time: 215 us
  local copies, waits for them, and re-layouts  141 us (66%)
  waiting for transfers between devices  40.9 us (19%)
  between operations  13.7 us (6%)
  starting transfers between devices  13.1 us (6%)
  other arithmetic  4.56 us (2%)
    gather x1, local copies, waits for them, and re-layouts, interpolate(): value_ll = jnp.take(flat_cells, low_index).astype(jnp.float32)  25.6 us
    gather x1, local copies, waits for them, and re-layouts, interpolate(): value_lh = jnp.take(flat_cells, low_index + 1).astype(jnp.float32)  25.6 us
    gather x1, local copies, waits for them, and re-layouts, interpolate(): value_hh = jnp.take(flat_cells, high_index + 1).astype(jnp.float32)  25.6 us
    gather x1, local copies, waits for them, and re-layouts, interpolate(): value_hl = jnp.take(flat_cells, high_index).astype(jnp.float32)  25.6 us
    unnamed x20, local copies, waits for them, and re-layouts  20.7 us
    reduce_scatter x1, waiting for transfers between devices, per_device(): lax.psum_scatter(jnp.einsum('dsmnk,mnkr->dsmnr', mixed, wigner_panel, pre...  19.9 us
    all_to_all x1, waiting for transfers between devices, per_device(): lax.all_to_all(beam_coeffs, 'det', split_axis=4, concat_axis=0, tiled=True)  7.34 us
    all_to_all x1, waiting for transfers between devices, per_device(): lax.all_to_all(outgoing, 'band', split_axis=0, concat_axis=0, tiled=True)  7.22 us
  transfers between devices with their start and end apart: 4, of which 4 were waited for; matrix products, arithmetic and copies ran while one was open for 1% of the time, Pallas kernels for 0%

commit v1 on v0

--- a/solution.py
+++ b/solution.py
@@ -3,6 +3,8 @@
 import jax
 import jax.numpy as jnp
 from jax import lax
+from jax.experimental import pallas as pl
+from jax.experimental.pallas import tpu as pltpu
 from jax.sharding import PartitionSpec as P
 
 BMAX = 8
@@ -10,6 +12,8 @@
 NPSI = 32
 NPHI = 4096
 BLOCK_PHI = 128
+LANES = 128
+ROWS = 24
 
 
 def psi_tables():
@@ -61,7 +65,7 @@
     return (1.0 - frac_psi) * low_row + frac_psi * high_row
 
 
-def per_device(
+def by_blocks(
     sky_coeffs,
     beam_coeffs,
     wigner_panel,
@@ -120,7 +124,247 @@
     return values[None, :]
 
 
+def smem():
+    return pl.BlockSpec(memory_space=pltpu.SMEM)
+
+
+def vmem():
+    return pl.BlockSpec(memory_space=pltpu.VMEM)
+
+
+def cos_sin(turns, whole):
+    quarter = whole // 4
+    quadrant = (turns + quarter // 2) // quarter
+    rest = turns - quadrant * quarter
+    x = rest.astype(jnp.float32) * (2.0 * math.pi / whole)
+    y = x * x
+    sine = x * (1.0 + y * (-1.0 / 6 + y * (1.0 / 120 + y * (-1.0 / 5040 + y * (1.0 / 362880)))))
+    cosine = 1.0 + y * (
+        -0.5 + y * (1.0 / 24 + y * (-1.0 / 720 + y * (1.0 / 40320 - y * (1.0 / 3628800))))
+    )
+    quadrant = quadrant & 3
+    odd = (quadrant & 1) == 1
+    c = jnp.where(odd, sine, cosine)
+    s = jnp.where(odd, cosine, sine)
+    c = jnp.where((quadrant == 1) | (quadrant == 2), -c, c)
+    s = jnp.where(quadrant >= 2, -s, s)
+    return c, s
+
+
+def beam_kernel(place, own, other, out):
+    chunk = out.shape[4] // 2
+    for side, ref in enumerate((own, other)):
+        for part in range(2):
+            owner = place[0] ^ (2 * part)
+            lanes = pl.ds(pl.multiple_of(owner * chunk, chunk), chunk)
+            for c in range(ref.shape[0]):
+                block = ref[c, :, :, lanes].astype(jnp.float32)
+                for s in range(2):
+                    out[side, c, s, 0:MPRIME, part * chunk : (part + 1) * chunk] = block[:, s, :]
+    out[:, :, :, MPRIME:, :] = jnp.zeros_like(out[:, :, :, MPRIME:, :])
+
+
+def sample_kernel(
+    place, m_values, cycle_table, lists, block, phi, psi, frac, phase, low, high, tables
+):
+    orders = m_values.shape[0]
+    slots = cycle_table.shape[0] // orders
+    scale = 2.0 / math.sqrt(orders * MPRIME)
+    band = place[1]
+    blocks = block[...]
+    start = jnp.zeros_like(blocks)
+    cycle = jnp.zeros_like(blocks)
+    entries = lists.shape[0] // (orders * orders)
+    for source in range(orders):
+        for entry in range(entries):
+            code = jnp.maximum(lists[(source * orders + band) * entries + entry], 0)
+            here = blocks == source * entries + entry
+            start = jnp.where(here, code & (NPHI - 1), start)
+            cycle = jnp.where(here, cycle_table[source * slots + lax.div(code, NPHI)], cycle)
+    cell = psi[...]
+    low[...] = cycle * NPSI + cell
+    high[...] = cycle * NPSI + ((cell + 1) & (NPSI - 1))
+    first = (start + phi[...]) & (NPHI - 1)
+    row = lax.broadcasted_iota(jnp.int32, (orders, LANES), 0)
+    m = jnp.zeros((orders, LANES), jnp.int32)
+    for k in range(orders):
+        m = jnp.where(row == k, m_values[band ^ k], m)
+    for g in range(blocks.shape[0]):
+        turns = (m * first[g : g + 1, :]) & (NPHI - 1)
+        c0, s0 = cos_sin(turns, NPHI)
+        c1, s1 = cos_sin((turns + m) & (NPHI - 1), NPHI)
+        c0, s0, c1, s1 = (v.astype(jnp.bfloat16).astype(jnp.float32) for v in (c0, s0, c1, s1))
+        f = frac[0, g : g + 1, :]
+        e = 1.0 - f
+        phase[g, 0] = (e * c0 + f * c1) * scale
+        phase[g, 1] = (e * s0 + f * s1) * (-scale)
+    shape = tables.shape[1:]
+    lane = lax.broadcasted_iota(jnp.int32, shape, 1) & (NPSI - 1)
+    line = lax.broadcasted_iota(jnp.int32, shape, 0)
+    imag = line >= ROWS
+    n = jnp.where(imag, line - ROWS, line)
+    c, s = cos_sin(((n - BMAX) * lane) & (NPSI - 1), NPSI)
+    tables[0] = jnp.where(imag, -s, c)
+    tables[1] = jnp.where(imag, c, s)
+
+
+def rows_kernel(beams, sky_own, sky_other, w_own, w_other, tables, mine, theirs):
+    chunk = w_own.shape[1]
+    cycles = w_own.shape[0] // MPRIME
+    total = None
+    for part, (sky, w) in enumerate(((sky_own, w_own), (sky_other, w_other))):
+        lanes = slice(part * chunk, (part + 1) * chunk)
+        pieces = []
+        for side in range(2):
+            real = jnp.zeros((ROWS, chunk), jnp.float32)
+            imag = jnp.zeros((ROWS, chunk), jnp.float32)
+            for c in range(sky.shape[0]):
+                sr, si = sky[c, 0], sky[c, 1]
+                br, bi = beams[side, c, 0, :, lanes], beams[side, c, 1, :, lanes]
+                real += sr * br + si * bi
+                imag += si * br - sr * bi
+            pieces += [real, imag]
+        mixed = jnp.concatenate(pieces, 0).astype(jnp.bfloat16)
+        term = lax.dot_general(
+            mixed, w[...], (((1,), (1,)), ((), ())), preferred_element_type=jnp.float32
+        )
+        total = term if total is None else total + term
+    line = lax.broadcasted_iota(jnp.int32, total.shape, 0)
+    column = lax.broadcasted_iota(jnp.int32, total.shape, 1)
+    kept = jnp.where(lax.rem(line, ROWS) == lax.div(column, cycles), total, 0.0)
+    wide = (w_own.shape[0], cycles * NPSI)
+    spread = (
+        lax.rem(lax.broadcasted_iota(jnp.int32, wide, 0), cycles)
+        == lax.div(lax.broadcasted_iota(jnp.int32, wide, 1), NPSI)
+    ).astype(jnp.bfloat16)
+    coeff = jnp.zeros((total.shape[0], wide[1]), jnp.float32)
+    for _ in range(3):
+        piece = kept.astype(jnp.bfloat16)
+        kept = kept - piece.astype(jnp.float32)
+        coeff += jnp.dot(piece, spread, preferred_element_type=jnp.float32)
+    for side, out in enumerate((mine, theirs)):
+        own = coeff[side * 2 * ROWS : (side + 1) * 2 * ROWS]
+        for s in range(2):
+            out[s : s + 1, :] = jnp.sum(own * tables[s], 0, keepdims=True)
+
+
+def final_kernel(*refs):
+    *parts, phase, low, high, frac, out = refs
+    width = parts[0].shape[2]
+    rows = [part[k, :, :].astype(jnp.float32) for part in parts for k in range(part.shape[0])]
+    planes = [jnp.concatenate([row[s : s + 1] for row in rows], 0) for s in range(2)]
+    tiles = [[plane[:, t : t + LANES] for t in range(0, width, LANES)] for plane in planes]
+
+    def pick(table, index):
+        value = None
+        inside = index & (LANES - 1)
+        for t, tile in enumerate(table):
+            found = jnp.take_along_axis(tile, inside, axis=1, mode="promise_in_bounds")
+            value = found if value is None else jnp.where(index >= t * LANES, found, value)
+        return value
+
+    for g in range(out.shape[0]):
+        shape = (len(rows), LANES)
+        at_low = jnp.broadcast_to(low[g : g + 1, :], shape)
+        at_high = jnp.broadcast_to(high[g : g + 1, :], shape)
+        f = frac[1, g : g + 1, :]
+        e = 1.0 - f
+        real = e * pick(tiles[0], at_low) + f * pick(tiles[0], at_high)
+        imag = e * pick(tiles[1], at_low) + f * pick(tiles[1], at_high)
+        total = real * phase[g, 0] + imag * phase[g, 1]
+        out[g : g + 1, :] = jnp.sum(total, 0, keepdims=True)
+
+
+def call(kernel, out_shape, in_specs, flops):
+    return pl.pallas_call(
+        kernel,
+        out_shape=out_shape,
+        in_specs=in_specs,
+        out_specs=jax.tree.map(lambda _: vmem(), out_shape),
+        cost_estimate=pl.CostEstimate(flops=flops, bytes_accessed=1 << 20, transcendentals=0),
+        compiler_params=pltpu.CompilerParams(vmem_limit_bytes=24 << 20),
+    )
+
+
+def by_samples(
+    sky_coeffs,
+    beam_coeffs,
+    wigner_panel,
+    m_values,
+    cycle_table,
+    send_lists,
+    sample_block,
+    sample_phi,
+    sample_psi,
+    sample_frac,
+):
+    f32 = jnp.float32
+    bands = lax.axis_size("band")
+    band, det = lax.axis_index("band"), lax.axis_index("det")
+    place = jnp.stack([det, band])
+    chunk, cycles = wigner_panel.shape[2:]
+    groups = sample_block.shape[1] // LANES
+    psi_width = cycles * NPSI
+
+    def swap(x, axis, bit):
+        return lax.ppermute(x, axis, [(i, i ^ bit) for i in range(lax.axis_size(axis))])
+
+    panel = jnp.transpose(wigner_panel[0], (0, 2, 1)).reshape(MPRIME * cycles, chunk)
+    beam = jnp.transpose(beam_coeffs[0], (0, 2, 1, 3))
+    panel_other = swap(panel, "det", 2)
+    sky_other = swap(sky_coeffs, "det", 2)
+    beam_other = swap(beam, "det", 1)
+
+    phase, low, high, tables = call(
+        sample_kernel,
+        (
+            jax.ShapeDtypeStruct((groups, 2, bands, LANES), f32),
+            jax.ShapeDtypeStruct((groups, LANES), jnp.int32),
+            jax.ShapeDtypeStruct((groups, LANES), jnp.int32),
+            jax.ShapeDtypeStruct((2, 2 * ROWS, psi_width), f32),
+        ),
+        [smem()] * 4 + [vmem()] * 4,
+        1 << 22,
+    )(
+        place,
+        m_values,
+        cycle_table.reshape(-1),
+        send_lists.reshape(-1),
+        sample_block.reshape(groups, LANES),
+        sample_phi.reshape(groups, LANES),
+        sample_psi.reshape(groups, LANES),
+        sample_frac.reshape(2, groups, LANES),
+    )
+    beams = call(
+        beam_kernel,
+        jax.ShapeDtypeStruct((2, beam.shape[0], 2, ROWS, 2 * chunk), f32),
+        [smem(), vmem(), vmem()],
+        1 << 22,
+    )(place, beam, beam_other)
+    mine, theirs = call(
+        rows_kernel,
+        (jax.ShapeDtypeStruct((2, psi_width), f32), jax.ShapeDtypeStruct((2, psi_width), f32)),
+        [vmem()] * 6,
+        1 << 22,
+    )(beams, sky_coeffs, sky_other, panel, panel_other, tables)
+    rows = (mine + swap(theirs, "det", 1)).astype(jnp.bfloat16)
+    pair = jnp.stack([rows, swap(rows, "band", 1)])
+    parts = [pair] + [swap(pair, "band", k) for k in range(2, bands, 2)]
+    values = call(
+        final_kernel,
+        jax.ShapeDtypeStruct((groups, LANES), f32),
+        [vmem()] * (len(parts) + 4),
+        1 << 22,
+    )(*parts, phase, low, high, sample_frac.reshape(2, groups, LANES))
+    return values.reshape(1, -1)
+
+
 def solution(mesh):
+    def per_device(*args):
+        cycles = args[2].shape[3]
+        small = mesh.shape["band"] <= 8 and cycles <= 8
+        return (by_samples if small else by_blocks)(*args)
+
     return jax.shard_map(
         per_device,
         mesh=mesh,

time: 215 us -> 28.8 us (0.13)
  local copies, waits for them, and re-layouts: 141 us -> 6.36 us
  waiting for transfers between devices: 40.9 us -> 8.07 us
  between operations: 13.7 us -> 0.1 us
  other arithmetic: 4.56 us -> 0.09 us
  Pallas kernels: 0 us -> 3.84 us
  starting transfers between devices: 13.1 us -> 9.87 us
    gather x6 -> x0, local copies, waits for them, and re-layouts: 106 us -> none  [the longest x1 25.6 us: interpolate(): value_ll = jnp.take(flat_cells, low_index).astype(jnp.float32)]
    all_to_all x3 -> x0, waiting for transfers between devices: 21 us -> none  [the longest x1 7.34 us: per_device(): lax.all_to_all(beam_coeffs, 'det', split_axis=4, concat_axis=0, tiled=True)]
    reduce_scatter x1 -> x0, waiting for transfers between devices: 19.9 us -> none  [per_device(): lax.psum_scatter(jnp.einsum('dsmnk,mnkr->dsmnr', mixed, wigner_panel, pre...]
    unnamed x20, local copies, waits for them, and re-layouts: 20.7 us -> 6.14 us
    all_to_all x3 -> x0, starting transfers between devices: 13.1 us -> none  [the longest x1 5.51 us: per_device(): lax.all_to_all(payload, 'band', split_axis=0, concat_axis=0, tiled=True)]
    ppermute x0 -> x8, starting transfers between devices: none -> 9.87 us  [swap(): lax.ppermute(x, axis, [(i, i ^ bit) for i in range(lax.axis_size(axis))])]
    ppermute x0 -> x8, waiting for transfers between devices: none -> 8.07 us  [swap(): lax.ppermute(x, axis, [(i, i ^ bit) for i in range(lax.axis_size(axis))])]
    all_to_all x1 -> x0, local copies, waits for them, and re-layouts: 6.12 us -> none  [per_device(): lax.all_to_all(beam_coeffs, 'det', split_axis=4, concat_axis=0, tiled=True)]
  transfers between devices with their start and end apart: 4 -> 8, of which waited for: 4 -> 4; matrix products, arithmetic and copies ran while one was open for 1% -> 7% of each run, Pallas kernels for 0% -> 7%
where the time goes in v1:
time: 28.8 us; the launch traced here: 28.3 us
  starting transfers between devices  9.87 us (34%)
  waiting for transfers between devices  8.07 us (28%)
  local copies, waits for them, and re-layouts  6.36 us (22%)
  Pallas kernels  3.84 us (13%)
    ppermute x8, starting transfers between devices, swap(): lax.ppermute(x, axis, [(i, i ^ bit) for i in range(lax.axis_size(axis))])  9.87 us
    ppermute x8, waiting for transfers between devices, swap(): lax.ppermute(x, axis, [(i, i ^ bit) for i in range(lax.axis_size(axis))])  8.07 us
    unnamed x20, local copies, waits for them, and re-layouts  6.14 us
    pallas_call x1, Pallas kernels, by_samples(): call(final_kernel, jax.ShapeDtypeStruct((groups, LANES), f32), [vmem()] *...  1.29 us
    pallas_call x1, Pallas kernels, by_samples(): call(sample_kernel, (jax.ShapeDtypeStruct((groups, 2, bands, LANES), f32)...  1.26 us
    pallas_call x1, Pallas kernels, by_samples(): call(beam_kernel, jax.ShapeDtypeStruct((2, beam.shape[0], 2, ROWS, 2 * ch...  0.82 us
  transfers between devices with their start and end apart: 8, of which 4 were waited for; matrix products, arithmetic and copies ran while one was open for 7% of the time, Pallas kernels for 7%

profile of v1, /device:TPU:0, one launch (start us, length us, event | category | flops | bytes accessed | tf_op | source)
XLA Modules:
  0.0 28.3 jit_solution(17895789505433036030)
XLA Ops:
  0.0 0.0 copy-start.1
  0.0 0.5 %collective-permute-start = (bf16[3,17,2,2048]{3,2,1,0:T(2,128)(2,1)}, bf16[3,17,2,2048]{3,2,1,0:T(2,128)(2,1)S(1)}, u32[]{:S(2)}, u32[]{:S(2)}) collective-permute-start(bf16[3,17,2,2048]{3,2,1,0:T(2,128)(2,1)} %bitcast.19), channel_id=1, source_target_pairs={{0,1},{1,0},{2,3},{3,2},{4,5},{5,4},{6,7},{7,6},{8,9},{9,8},{10,11... | collective-permute-start | bytes 1253384 | tf_op jit(solution)/shard_map/ppermute | solution.py:310
  0.5 2.5 %collective-permute-start.2 = (bf16[136,512]{1,0:T(8,128)(2,1)}, bf16[136,512]{1,0:T(8,128)(2,1)S(1)}, u32[]{:S(2)}, u32[]{:S(2)}) collective-permute-start(bf16[136,512]{1,0:T(8,128)(2,1)} %bitcast.21), channel_id=1, source_target_pairs={{0,2},{1,3},{2,0},{3,1},{4,6},{5,7},{6,4},{7,5},{8,10},{9,11},{10,... | collective-permute-start | bytes 417800 | tf_op jit(solution)/shard_map/ppermute | solution.py:310
  3.0 0.1 collective-permute-start.1
  3.1 0.1 pad_add_fusion.place
  3.2 0.8 %copy.13 = s32[8,3]{1,0:T(8,128)S(1)} copy(s32[8,3]{0,1:T(4,128)} %param.14) | data formatting | bytes 192 | tf_op args[4]
  3.9 0.1 reshape.26.cycle_table
  4.0 0.8 %copy.14 = s32[1,8,8,2]{3,2,1,0:T(8,128)S(1)} copy(s32[1,8,8,2]{2,3,1,0:T(2,128)} %param.15) | data formatting | bytes 1024 | tf_op args[5]
  4.8 0.1 reshape.27.lists
  5.0 0.0 copy-start.2
  5.0 0.8 %copy-done.2 = f32[2,1,4096]{2,1,0:T(1,128)S(1)} copy-done((f32[2,1,4096]{2,1,0:T(1,128)S(1)}, f32[2,1,4096]{2,1,0:T(1,128)}, u32[]{:S(2)}) %copy-start.2) | copy-done | bytes 32792
  5.7 0.0 copy-start.4
  5.7 0.7 %copy-done.4 = s32[1,4096]{1,0:T(1,128)S(1)} copy-done((s32[1,4096]{1,0:T(1,128)S(1)}, s32[1,4096]{1,0:T(1,128)}, u32[]{:S(2)}) %copy-start.4) | copy-done | bytes 16408
  6.5 0.0 copy-start.5
  6.5 0.7 %copy-done.5 = s32[1,4096]{1,0:T(1,128)S(1)} copy-done((s32[1,4096]{1,0:T(1,128)S(1)}, s32[1,4096]{1,0:T(1,128)}, u32[]{:S(2)}) %copy-start.5) | copy-done | bytes 16408
  7.2 0.0 copy-start.6
  7.2 0.7 %copy-done.6 = s32[1,4096]{1,0:T(1,128)S(1)} copy-done((s32[1,4096]{1,0:T(1,128)S(1)}, s32[1,4096]{1,0:T(1,128)}, u32[]{:S(2)}) %copy-start.6) | copy-done | bytes 16408
  7.9 0.0 copy-start.8
  7.9 0.7 %copy-done.8 = s32[8]{0:T(128)S(1)} copy-done((s32[8]{0:T(128)S(1)}, s32[8]{0:T(128)}, u32[]{:S(2)}) %copy-start.8) | copy-done | bytes 56
  8.5 0.0 copy-start.7
  8.6 1.3 %shard_map.101 = (f32[32,2,8,128]{3,2,1,0:T(8,128)S(1)}, s32[32,128]{1,0:T(8,128)S(1)}, s32[32,128]{1,0:T(8,128)S(1)}, f32[2,48,256]{2,1,0:T(8,128)S(1)}) custom-call(s32[2]{0:T(128)S(1)} %pad_add_fusion.place, s32[8]{0:T(128)S(1)} %copy-done.8, s32[24]{0:T(128)S(1)} %reshape.26.cycle_table, s32[128]{0:T(128)S(1)} %reshape.27.lists, s32[32,128]{1,0:T(8,128)S(1)} %bitcast.25, ...), custom_call_target="tpu_custom_call" | custom-call | flops 4194304 | bytes 1048576 | tf_op jit(solution)/shard_map/pallas_call | solution.py:318
  9.8 0.0 collective-permute-done.other
  9.8 0.0 copy-start
  9.8 1.0 %copy-done = bf16[1,3,2,17,2048]{4,2,3,1,0:T(2,128)(2,1)S(1)} copy-done((bf16[1,3,2,17,2048]{4,2,3,1,0:T(2,128)(2,1)S(1)}, bf16[1,3,2,17,2048]{4,2,3,1,0:T(2,128)(2,1)}, u32[]{:S(2)}) %copy-start) | copy-done | bytes 417816
  10.8 0.8 %shard_map.100.beams = f32[2,3,2,24,1024]{4,3,2,1,0:T(8,128)S(1)} custom-call(s32[2]{0:T(128)S(1)} %pad_add_fusion.place, bf16[3,17,2,2048]{3,2,1,0:T(2,128)(2,1)S(1)} %bitcast.20, bf16[3,17,2,2048]{3,2,1,0:T(2,128)(2,1)S(1)} %collective-permute-done.other), custom_call_target="tpu_custom_call" | custom-call | flops 4194304 | bytes 1048576 | tf_op jit(solution)/shard_map/pallas_call | solution.py:338
  11.7 0.0 copy-start.3
  11.7 0.0 collective-permute-done.1.sky_other
  11.7 0.0 collective-permute-done.2.w_other
  11.7 0.0 copy-done.1
  11.7 0.0 copy-done.7
  11.7 0.5 %shard_map.102 = (f32[2,256]{1,0:T(2,128)S(1)}, f32[2,256]{1,0:T(2,128)S(1)}) custom-call(f32[2,3,2,24,1024]{4,3,2,1,0:T(8,128)S(1)} %shard_map.100.beams, f32[3,2,1,512]{3,2,1,0:T(1,128)S(1)} %copy-done.7, f32[3,2,1,512]{3,2,1,0:T(1,128)S(1)} %collective-permute-done.1.sky_other, bf16[136,512]{1,0:T(8,128)(2,1)S(1)} %bitcast.22, ...), custom_call_target="tpu_custom_call" | custom-call | flops 4194304 | bytes 1048576 | tf_op jit(solution)/shard_map/pallas_call | solution.py:344
  12.2 0.2 collective-permute-start.3
  12.4 1.1 %collective-permute-done.3 = f32[2,256]{1,0:T(2,128)S(1)} collective-permute-done((f32[2,256]{1,0:T(2,128)S(1)}, f32[2,256]{1,0:T(2,128)S(1)}, u32[]{:S(2)}, u32[]{:S(2)}) %collective-permute-start.3) | collective-permute-done | bytes 2080 | tf_op jit(solution)/shard_map/ppermute | solution.py:310
  13.4 1.9 %collective-permute-start.4 = (bf16[2,256]{1,0:T(2,128)(2,1)S(1)}, bf16[2,256]{1,0:T(2,128)(2,1)S(1)}, u32[]{:S(2)}, u32[]{:S(2)}) collective-permute-start(bf16[2,256]{1,0:T(2,128)(2,1)S(1)} %add_convert_fusion), channel_id=1, source_target_pairs={{0,4},{4,0},{8,12},{12,8},{16,20},{20,16},{24,28},{28,24},{1,5},{5... | collective-permute-start | bytes 3080 | tf_op jit(solution)/shard_map/ppermute | solution.py:310
  15.4 1.6 %collective-permute-done.4 = bf16[2,256]{1,0:T(2,128)(2,1)S(1)} collective-permute-done((bf16[2,256]{1,0:T(2,128)(2,1)S(1)}, bf16[2,256]{1,0:T(2,128)(2,1)S(1)}, u32[]{:S(2)}, u32[]{:S(2)}) %collective-permute-start.4) | collective-permute-done | bytes 1056 | tf_op jit(solution)/shard_map/ppermute | solution.py:310
  17.0 2.1 %collective-permute-start.5 = (bf16[2,2,256]{2,1,0:T(2,128)(2,1)S(1)}, bf16[2,2,256]{2,1,0:T(2,128)(2,1)S(1)}, u32[]{:S(2)}, u32[]{:S(2)}) collective-permute-start(bf16[2,2,256]{2,1,0:T(2,128)(2,1)S(1)} %pad_maximum_fusion.refs_0_), channel_id=1, source_target_pairs={{0,8},{4,12},{8,0},{12,4},{16,24},{20,28},{24,16},{28,20},{1,9},{5... | collective-permute-start | bytes 6152 | tf_op jit(solution)/shard_map/ppermute | solution.py:310
  19.1 2.6 %collective-permute-start.6 = (bf16[2,2,256]{2,1,0:T(2,128)(2,1)S(1)}, bf16[2,2,256]{2,1,0:T(2,128)(2,1)S(1)}, u32[]{:S(2)}, u32[]{:S(2)}) collective-permute-start(bf16[2,2,256]{2,1,0:T(2,128)(2,1)S(1)} %pad_maximum_fusion.refs_0_), channel_id=1, source_target_pairs={{0,16},{4,20},{8,24},{12,28},{16,0},{20,4},{24,8},{28,12},{1,17},{... | collective-permute-start | bytes 6152 | tf_op jit(solution)/shard_map/ppermute | solution.py:310
  21.7 0.0 collective-permute-start.7
  21.7 0.0 collective-permute-done.5.refs_1_
  21.7 1.9 %collective-permute-done.6.refs_2_ = bf16[2,2,256]{2,1,0:T(2,128)(2,1)S(1)} collective-permute-done((bf16[2,2,256]{2,1,0:T(2,128)(2,1)S(1)}, bf16[2,2,256]{2,1,0:T(2,128)(2,1)S(1)}, u32[]{:S(2)}, u32[]{:S(2)}) %collective-permute-start.6) | collective-permute-done | bytes 2080 | tf_op jit(solution)/shard_map/ppermute | solution.py:310
  23.6 3.5 %collective-permute-done.7.refs_3_ = bf16[2,2,256]{2,1,0:T(2,128)(2,1)S(1)} collective-permute-done((bf16[2,2,256]{2,1,0:T(2,128)(2,1)S(1)}, bf16[2,2,256]{2,1,0:T(2,128)(2,1)S(1)}, u32[]{:S(2)}, u32[]{:S(2)}) %collective-permute-start.7) | collective-permute-done | bytes 2080 | tf_op jit(solution)/shard_map/ppermute | solution.py:310
  27.0 0.0 copy-done.3
  27.0 1.3 %shard_map.103 = f32[32,128]{1,0:T(8,128)} custom-call(bf16[2,2,256]{2,1,0:T(2,128)(2,1)S(1)} %pad_maximum_fusion.refs_0_, bf16[2,2,256]{2,1,0:T(2,128)(2,1)S(1)} %collective-permute-done.5.refs_1_, bf16[2,2,256]{2,1,0:T(2,128)(2,1)S(1)} %collective-permute-done.6.refs_2_, bf16[2,2,256]{2,1,0:T(2,128)(2,1)S(1)} %collective-permute-done.7.refs_3_, ...), custom_call_target="tpu_custom_call" | custom-call | flops 4194304 | bytes 1048576 | tf_op jit(solution)/shard_map/pallas_call | solution.py:353
  (2 shorter events, 0.0 us)
Async XLA Ops:
  0.0 11.7 %copy-start.1 = (bf16[1,17,512,8]{2,3,1,0:T(8,128)(2,1)S(1)}, bf16[1,17,512,8]{2,3,1,0:T(8,128)(2,1)}, u32[]{:S(2)}) copy-start(bf16[1,17,512,8]{2,3,1,0:T(8,128)(2,1)} %param.12) | copy-start | bytes 417796
  0.0 9.8 %collective-permute-start = (bf16[3,17,2,2048]{3,2,1,0:T(2,128)(2,1)}, bf16[3,17,2,2048]{3,2,1,0:T(2,128)(2,1)S(1)}, u32[]{:S(2)}, u32[]{:S(2)}) collective-permute-start(bf16[3,17,2,2048]{3,2,1,0:T(2,128)(2,1)} %bitcast.19), channel_id=1, source_target_pairs={{0,1},{1,0},{2,3},{3,2},{4,5},{5,4},{6,7},{7,6},{8,9},{9,8},{10,11... | collective-permute-start | bytes 1253384 | tf_op jit(solution)/shard_map/ppermute | solution.py:310
  0.5 11.2 %collective-permute-start.2 = (bf16[136,512]{1,0:T(8,128)(2,1)}, bf16[136,512]{1,0:T(8,128)(2,1)S(1)}, u32[]{:S(2)}, u32[]{:S(2)}) collective-permute-start(bf16[136,512]{1,0:T(8,128)(2,1)} %bitcast.21), channel_id=1, source_target_pairs={{0,2},{1,3},{2,0},{3,1},{4,6},{5,7},{6,4},{7,5},{8,10},{9,11},{10,... | collective-permute-start | bytes 417800 | tf_op jit(solution)/shard_map/ppermute | solution.py:310
  3.0 8.7 %collective-permute-start.1 = (f32[3,2,1,512]{3,2,1,0:T(1,128)}, f32[3,2,1,512]{3,2,1,0:T(1,128)S(1)}, u32[]{:S(2)}, u32[]{:S(2)}) collective-permute-start(f32[3,2,1,512]{3,2,1,0:T(1,128)} %sky_own.1), channel_id=1, source_target_pairs={{0,2},{1,3},{2,0},{3,1},{4,6},{5,7},{6,4},{7,5},{8,10},{9,11},{10,... | collective-permute-start | bytes 36872 | tf_op jit(solution)/shard_map/ppermute | solution.py:310
  5.0 0.8 %copy-start.2 = (f32[2,1,4096]{2,1,0:T(1,128)S(1)}, f32[2,1,4096]{2,1,0:T(1,128)}, u32[]{:S(2)}) copy-start(f32[2,1,4096]{2,1,0:T(1,128)} %param.19) | copy-start | bytes 98308
  5.7 0.7 %copy-start.4 = (s32[1,4096]{1,0:T(1,128)S(1)}, s32[1,4096]{1,0:T(1,128)}, u32[]{:S(2)}) copy-start(s32[1,4096]{1,0:T(1,128)} %param.16) | copy-start | bytes 49156
  6.5 0.7 %copy-start.5 = (s32[1,4096]{1,0:T(1,128)S(1)}, s32[1,4096]{1,0:T(1,128)}, u32[]{:S(2)}) copy-start(s32[1,4096]{1,0:T(1,128)} %param.17) | copy-start | bytes 49156
  7.2 0.7 %copy-start.6 = (s32[1,4096]{1,0:T(1,128)S(1)}, s32[1,4096]{1,0:T(1,128)}, u32[]{:S(2)}) copy-start(s32[1,4096]{1,0:T(1,128)} %param.18) | copy-start | bytes 49156
  7.9 0.7 %copy-start.8 = (s32[8]{0:T(128)S(1)}, s32[8]{0:T(128)}, u32[]{:S(2)}) copy-start(s32[8]{0:T(128)} %m_values.1) | copy-start | bytes 100
  8.5 3.2 %copy-start.7 = (f32[3,2,1,512]{3,2,1,0:T(1,128)S(1)}, f32[3,2,1,512]{3,2,1,0:T(1,128)}, u32[]{:S(2)}) copy-start(f32[3,2,1,512]{3,2,1,0:T(1,128)} %sky_own.1) | copy-start | bytes 36868
  9.8 1.0 %copy-start = (bf16[1,3,2,17,2048]{4,2,3,1,0:T(2,128)(2,1)S(1)}, bf16[1,3,2,17,2048]{4,2,3,1,0:T(2,128)(2,1)}, u32[]{:S(2)}) copy-start(bf16[1,3,2,17,2048]{4,2,3,1,0:T(2,128)(2,1)} %param.11) | copy-start | bytes 1253380
  11.7 15.4 %copy-start.3 = (f32[2,1,4096]{2,1,0:T(1,128)S(1)}, f32[2,1,4096]{2,1,0:T(1,128)}, u32[]{:S(2)}) copy-start(f32[2,1,4096]{2,1,0:T(1,128)} %param.19) | copy-start | bytes 98308
  12.2 1.2 %collective-permute-start.3 = (f32[2,256]{1,0:T(2,128)S(1)}, f32[2,256]{1,0:T(2,128)S(1)}, u32[]{:S(2)}, u32[]{:S(2)}) collective-permute-start(f32[2,256]{1,0:T(2,128)S(1)} %get-tuple-element.13), channel_id=1, source_target_pairs={{0,1},{1,0},{2,3},{3,2},{4,5},{5,4},{6,7},{7,6},{8,9},{9,8},{10,11... | collective-permute-start | bytes 6152 | tf_op jit(solution)/shard_map/ppermute | solution.py:310
  13.4 3.6 %collective-permute-start.4 = (bf16[2,256]{1,0:T(2,128)(2,1)S(1)}, bf16[2,256]{1,0:T(2,128)(2,1)S(1)}, u32[]{:S(2)}, u32[]{:S(2)}) collective-permute-start(bf16[2,256]{1,0:T(2,128)(2,1)S(1)} %add_convert_fusion), channel_id=1, source_target_pairs={{0,4},{4,0},{8,12},{12,8},{16,20},{20,16},{24,28},{28,24},{1,5},{5... | collective-permute-start | bytes 3080 | tf_op jit(solution)/shard_map/ppermute | solution.py:310
  17.0 4.7 %collective-permute-start.5 = (bf16[2,2,256]{2,1,0:T(2,128)(2,1)S(1)}, bf16[2,2,256]{2,1,0:T(2,128)(2,1)S(1)}, u32[]{:S(2)}, u32[]{:S(2)}) collective-permute-start(bf16[2,2,256]{2,1,0:T(2,128)(2,1)S(1)} %pad_maximum_fusion.refs_0_), channel_id=1, source_target_pairs={{0,8},{4,12},{8,0},{12,4},{16,24},{20,28},{24,16},{28,20},{1,9},{5... | collective-permute-start | bytes 6152 | tf_op jit(solution)/shard_map/ppermute | solution.py:310
  19.1 4.5 %collective-permute-start.6 = (bf16[2,2,256]{2,1,0:T(2,128)(2,1)S(1)}, bf16[2,2,256]{2,1,0:T(2,128)(2,1)S(1)}, u32[]{:S(2)}, u32[]{:S(2)}) collective-permute-start(bf16[2,2,256]{2,1,0:T(2,128)(2,1)S(1)} %pad_maximum_fusion.refs_0_), channel_id=1, source_target_pairs={{0,16},{4,20},{8,24},{12,28},{16,0},{20,4},{24,8},{28,12},{1,17},{... | collective-permute-start | bytes 6152 | tf_op jit(solution)/shard_map/ppermute | solution.py:310
  21.7 5.4 %collective-permute-start.7 = (bf16[2,2,256]{2,1,0:T(2,128)(2,1)S(1)}, bf16[2,2,256]{2,1,0:T(2,128)(2,1)S(1)}, u32[]{:S(2)}, u32[]{:S(2)}) collective-permute-start(bf16[2,2,256]{2,1,0:T(2,128)(2,1)S(1)} %pad_maximum_fusion.refs_0_), channel_id=1, source_target_pairs={{0,24},{4,28},{8,16},{12,20},{16,8},{20,12},{24,0},{28,4},{1,25},{... | collective-permute-start | bytes 6152 | tf_op jit(solution)/shard_map/ppermute | solution.py:310

commit v2 on v1

--- a/solution.py
+++ b/solution.py
@@ -128,6 +128,10 @@
     return pl.BlockSpec(memory_space=pltpu.SMEM)
 
 
+def hbm():
+    return pl.BlockSpec(memory_space=pltpu.HBM)
+
+
 def vmem():
     return pl.BlockSpec(memory_space=pltpu.VMEM)
 
@@ -151,44 +155,58 @@
     return c, s
 
 
-def beam_kernel(place, own, other, out):
-    chunk = out.shape[4] // 2
-    for side, ref in enumerate((own, other)):
-        for part in range(2):
-            owner = place[0] ^ (2 * part)
-            lanes = pl.ds(pl.multiple_of(owner * chunk, chunk), chunk)
-            for c in range(ref.shape[0]):
-                block = ref[c, :, :, lanes].astype(jnp.float32)
-                for s in range(2):
-                    out[side, c, s, 0:MPRIME, part * chunk : (part + 1) * chunk] = block[:, s, :]
-    out[:, :, :, MPRIME:, :] = jnp.zeros_like(out[:, :, :, MPRIME:, :])
+def beam_kernel(place, source, out):
+    chunk = out.shape[3] // 2
+    for part in range(2):
+        owner = place[0] ^ (2 * part)
+        lanes = pl.ds(pl.multiple_of(owner * chunk, chunk), chunk)
+        for c in range(out.shape[0]):
+            block = source[c, :, :, lanes].astype(jnp.float32)
+            for s in range(2):
+                out[c, s, 0:MPRIME, part * chunk : (part + 1) * chunk] = block[:, s, :]
+    out[:, :, MPRIME:, :] = jnp.zeros_like(out[:, :, MPRIME:, :])
+
+
+def beam_copy_kernel(place, source, out, held, sem):
+    copy = pltpu.make_async_copy(source, held, sem)
+    copy.start()
+    copy.wait()
+    beam_kernel(place, held, out)
 
 
 def sample_kernel(
-    place, m_values, cycle_table, lists, block, phi, psi, frac, phase, low, high, tables
+    place, m_values, cycle_table, lists, *refs
 ):
+    sources, (phase, low, high), (block, phi, psi, frac, sems) = refs[:4], refs[4:7], refs[7:]
+    copies = [
+        pltpu.make_async_copy(source, held, sems.at[i])
+        for i, (source, held) in enumerate(zip(sources, (block, phi, psi, frac)))
+    ]
+    for copy in copies:
+        copy.start()
     orders = m_values.shape[0]
-    slots = cycle_table.shape[0] // orders
+    row = lax.broadcasted_iota(jnp.int32, (orders, LANES), 0)
+    m = jnp.zeros((orders, LANES), jnp.int32)
+    for k in range(orders):
+        m = jnp.where(row == k, m_values[place[1] ^ k], m)
+    for copy in copies:
+        copy.wait()
     scale = 2.0 / math.sqrt(orders * MPRIME)
     band = place[1]
     blocks = block[...]
     start = jnp.zeros_like(blocks)
     cycle = jnp.zeros_like(blocks)
-    entries = lists.shape[0] // (orders * orders)
-    for source in range(orders):
+    sources, entries = lists.shape[:2]
+    for source in range(sources):
         for entry in range(entries):
-            code = jnp.maximum(lists[(source * orders + band) * entries + entry], 0)
+            code = jnp.maximum(lists[source, entry, band], 0)
             here = blocks == source * entries + entry
             start = jnp.where(here, code & (NPHI - 1), start)
-            cycle = jnp.where(here, cycle_table[source * slots + lax.div(code, NPHI)], cycle)
+            cycle = jnp.where(here, cycle_table[lax.div(code, NPHI), source], cycle)
     cell = psi[...]
     low[...] = cycle * NPSI + cell
     high[...] = cycle * NPSI + ((cell + 1) & (NPSI - 1))
     first = (start + phi[...]) & (NPHI - 1)
-    row = lax.broadcasted_iota(jnp.int32, (orders, LANES), 0)
-    m = jnp.zeros((orders, LANES), jnp.int32)
-    for k in range(orders):
-        m = jnp.where(row == k, m_values[band ^ k], m)
     for g in range(blocks.shape[0]):
         turns = (m * first[g : g + 1, :]) & (NPHI - 1)
         c0, s0 = cos_sin(turns, NPHI)
@@ -198,29 +216,31 @@
         e = 1.0 - f
         phase[g, 0] = (e * c0 + f * c1) * scale
         phase[g, 1] = (e * s0 + f * s1) * (-scale)
-    shape = tables.shape[1:]
+
+
+def psi_weights(width):
+    shape = (2 * ROWS, width)
     lane = lax.broadcasted_iota(jnp.int32, shape, 1) & (NPSI - 1)
     line = lax.broadcasted_iota(jnp.int32, shape, 0)
     imag = line >= ROWS
     n = jnp.where(imag, line - ROWS, line)
     c, s = cos_sin(((n - BMAX) * lane) & (NPSI - 1), NPSI)
-    tables[0] = jnp.where(imag, -s, c)
-    tables[1] = jnp.where(imag, c, s)
-
-
-def rows_kernel(beams, sky_own, sky_other, w_own, w_other, tables, mine, theirs):
+    return jnp.where(imag, -s, c), jnp.where(imag, c, s)
+
+
+def rows_kernel(beam_own, beam_other, sky_own, sky_other, w_own, w_other, out):
     chunk = w_own.shape[1]
     cycles = w_own.shape[0] // MPRIME
     total = None
     for part, (sky, w) in enumerate(((sky_own, w_own), (sky_other, w_other))):
         lanes = slice(part * chunk, (part + 1) * chunk)
         pieces = []
-        for side in range(2):
+        for beam in (beam_own, beam_other):
             real = jnp.zeros((ROWS, chunk), jnp.float32)
             imag = jnp.zeros((ROWS, chunk), jnp.float32)
             for c in range(sky.shape[0]):
                 sr, si = sky[c, 0], sky[c, 1]
-                br, bi = beams[side, c, 0, :, lanes], beams[side, c, 1, :, lanes]
+                br, bi = beam[c, 0, :, lanes], beam[c, 1, :, lanes]
                 real += sr * br + si * bi
                 imag += si * br - sr * bi
             pieces += [real, imag]
@@ -242,10 +262,11 @@
         piece = kept.astype(jnp.bfloat16)
         kept = kept - piece.astype(jnp.float32)
         coeff += jnp.dot(piece, spread, preferred_element_type=jnp.float32)
-    for side, out in enumerate((mine, theirs)):
-        own = coeff[side * 2 * ROWS : (side + 1) * 2 * ROWS]
+    weights = psi_weights(wide[1])
+    for side in range(2):
+        held = coeff[side * 2 * ROWS : (side + 1) * 2 * ROWS]
         for s in range(2):
-            out[s : s + 1, :] = jnp.sum(own * tables[s], 0, keepdims=True)
+            out[side, s : s + 1, :] = jnp.sum(held * weights[s], 0, keepdims=True)
 
 
 def final_kernel(*refs):
@@ -275,12 +296,13 @@
         out[g : g + 1, :] = jnp.sum(total, 0, keepdims=True)
 
 
-def call(kernel, out_shape, in_specs, flops):
+def call(kernel, out_shape, in_specs, flops, scratch=()):
     return pl.pallas_call(
         kernel,
         out_shape=out_shape,
         in_specs=in_specs,
         out_specs=jax.tree.map(lambda _: vmem(), out_shape),
+        scratch_shapes=scratch,
         cost_estimate=pl.CostEstimate(flops=flops, bytes_accessed=1 << 20, transcendentals=0),
         compiler_params=pltpu.CompilerParams(vmem_limit_bytes=24 << 20),
     )
@@ -306,50 +328,63 @@
     groups = sample_block.shape[1] // LANES
     psi_width = cycles * NPSI
 
-    def swap(x, axis, bit):
-        return lax.ppermute(x, axis, [(i, i ^ bit) for i in range(lax.axis_size(axis))])
+    sizes = (bands, lax.axis_size("det"))
+
+    def swap(x, band_bits, det_bits):
+        pairs = [
+            (b * sizes[1] + d, (b ^ band_bits) * sizes[1] + (d ^ det_bits))
+            for b in range(sizes[0])
+            for d in range(sizes[1])
+        ]
+        return lax.ppermute(x, ("band", "det"), pairs)
 
     panel = jnp.transpose(wigner_panel[0], (0, 2, 1)).reshape(MPRIME * cycles, chunk)
     beam = jnp.transpose(beam_coeffs[0], (0, 2, 1, 3))
-    panel_other = swap(panel, "det", 2)
-    sky_other = swap(sky_coeffs, "det", 2)
-    beam_other = swap(beam, "det", 1)
-
-    phase, low, high, tables = call(
+    panel_other = swap(panel, 0, 2)
+    sky_other = swap(sky_coeffs, 0, 2)
+    beam, place = lax.optimization_barrier((beam, place))
+    beam_other = swap(beam, 0, 1)
+    split = jax.ShapeDtypeStruct((beam.shape[0], 2, ROWS, 2 * chunk), f32)
+    beam_own = call(
+        beam_copy_kernel,
+        split,
+        [smem(), hbm()],
+        1 << 22,
+        [pltpu.VMEM(beam.shape, beam.dtype), pltpu.SemaphoreType.DMA],
+    )(place, beam)
+    beam_other = call(beam_kernel, split, [smem(), vmem()], 1 << 22)(place, beam_other)
+    sums = call(rows_kernel, jax.ShapeDtypeStruct((2, 2, psi_width), f32), [vmem()] * 6, 1 << 22)(
+        beam_own, beam_other, sky_coeffs, sky_other, panel, panel_other
+    )
+    rows = (sums + swap(sums, 0, 1)[::-1]).astype(jnp.bfloat16)
+    rows_y = swap(rows, 1, 1)
+    block, phi, psi, frac, _ = lax.optimization_barrier(
+        (sample_block, sample_phi, sample_psi, sample_frac, rows)
+    )
+    held = [pltpu.VMEM((groups, LANES), jnp.int32)] * 3 + [pltpu.VMEM((2, groups, LANES), f32)]
+    phase, low, high = call(
         sample_kernel,
         (
             jax.ShapeDtypeStruct((groups, 2, bands, LANES), f32),
             jax.ShapeDtypeStruct((groups, LANES), jnp.int32),
             jax.ShapeDtypeStruct((groups, LANES), jnp.int32),
-            jax.ShapeDtypeStruct((2, 2 * ROWS, psi_width), f32),
         ),
-        [smem()] * 4 + [vmem()] * 4,
+        [smem()] * 4 + [hbm()] * 4,
         1 << 22,
+        held + [pltpu.SemaphoreType.DMA((4,))],
     )(
         place,
         m_values,
-        cycle_table.reshape(-1),
-        send_lists.reshape(-1),
-        sample_block.reshape(groups, LANES),
-        sample_phi.reshape(groups, LANES),
-        sample_psi.reshape(groups, LANES),
-        sample_frac.reshape(2, groups, LANES),
-    )
-    beams = call(
-        beam_kernel,
-        jax.ShapeDtypeStruct((2, beam.shape[0], 2, ROWS, 2 * chunk), f32),
-        [smem(), vmem(), vmem()],
-        1 << 22,
-    )(place, beam, beam_other)
-    mine, theirs = call(
-        rows_kernel,
-        (jax.ShapeDtypeStruct((2, psi_width), f32), jax.ShapeDtypeStruct((2, psi_width), f32)),
-        [vmem()] * 6,
-        1 << 22,
-    )(beams, sky_coeffs, sky_other, panel, panel_other, tables)
-    rows = (mine + swap(theirs, "det", 1)).astype(jnp.bfloat16)
-    pair = jnp.stack([rows, swap(rows, "band", 1)])
-    parts = [pair] + [swap(pair, "band", k) for k in range(2, bands, 2)]
+        cycle_table.T,
+        jnp.transpose(send_lists[0], (0, 2, 1)),
+        block.reshape(groups, LANES),
+        phi.reshape(groups, LANES),
+        psi.reshape(groups, LANES),
+        frac.reshape(2, groups, LANES),
+    )
+    pair = jnp.stack([rows[0], rows_y[1]])
+    pair_other = jnp.stack([rows[1], rows_y[0]])
+    parts = [pair] + [swap(pair_other, k, 1) for k in range(2, bands, 2)]
     values = call(
         final_kernel,
         jax.ShapeDtypeStruct((groups, LANES), f32),

time: 28.8 us -> 22.5 us (0.78)
  local copies, waits for them, and re-layouts: 6.36 us -> 1.66 us
  waiting for transfers between devices: 8.07 us -> 6.11 us
  Pallas kernels: 3.84 us -> 4.87 us
  starting transfers between devices: 9.87 us -> 9.38 us
    unnamed x20, local copies, waits for them, and re-layouts: 6.14 us -> 1.65 us
    ppermute x8, waiting for transfers between devices: 8.07 us -> 6.11 us  [swap(): return lax.ppermute(x, ('band', 'det'), pairs)]
    pallas_call x2 -> x3, Pallas kernels: 1.3 us -> 2.08 us  [the longest x1 0.91 us: by_samples(): call(beam_copy_kernel, split, [smem(), hbm()], 1 << 22, [pltpu.VMEM(beam....]
    ppermute x8, starting transfers between devices: 9.87 us -> 9.38 us  [swap(): return lax.ppermute(x, ('band', 'det'), pairs)]
  transfers between devices with their start and end apart: 8 -> 8, of which waited for: 4 -> 4; matrix products, arithmetic and copies ran while one was open for 7% -> 0% of each run, Pallas kernels for 7% -> 14%
where the time goes in v2:
time: 22.5 us; the launch traced here: 22.3 us
  starting transfers between devices  9.38 us (42%)
  waiting for transfers between devices  6.11 us (27%)
  Pallas kernels  4.87 us (22%)
  local copies, waits for them, and re-layouts  1.66 us (7%)
    ppermute x8, starting transfers between devices, swap(): return lax.ppermute(x, ('band', 'det'), pairs)  9.38 us
    ppermute x8, waiting for transfers between devices, swap(): return lax.ppermute(x, ('band', 'det'), pairs)  6.11 us
    unnamed x20, local copies, waits for them, and re-layouts  1.65 us
    pallas_call x1, Pallas kernels, by_samples(): call(sample_kernel, (jax.ShapeDtypeStruct((groups, 2, bands, LANES), f32)...  1.49 us
    pallas_call x1, Pallas kernels, by_samples(): call(final_kernel, jax.ShapeDtypeStruct((groups, LANES), f32), [vmem()] *...  1.29 us
    pallas_call x1, Pallas kernels, by_samples(): call(beam_copy_kernel, split, [smem(), hbm()], 1 << 22, [pltpu.VMEM(beam....  0.91 us
    pallas_call x1, Pallas kernels, by_samples(): call(beam_kernel, split, [smem(), vmem()], 1 << 22)(place, beam_other)  0.68 us
    pallas_call x1, Pallas kernels, by_samples(): call(rows_kernel, jax.ShapeDtypeStruct((2, 2, psi_width), f32), [vmem()]...  0.49 us
  transfers between devices with their start and end apart: 8, of which 4 were waited for; matrix products, arithmetic and copies ran while one was open for 0% of the time, Pallas kernels for 14%

profile of v2, /device:TPU:0, one launch (start us, length us, event | category | flops | bytes accessed | tf_op | source)
XLA Modules:
  0.0 22.3 jit_solution(12954048046975149732)
XLA Ops:
  0.0 0.0 copy-start.6
  0.0 0.1 pad_add_fusion.place
  0.1 0.5 %collective-permute-start = (bf16[3,17,2,2048]{3,2,1,0:T(2,128)(2,1)}, bf16[3,17,2,2048]{3,2,1,0:T(2,128)(2,1)S(1)}, u32[]{:S(2)}, u32[]{:S(2)}) collective-permute-start(bf16[3,17,2,2048]{3,2,1,0:T(2,128)(2,1)} %bitcast.20), channel_id=1, source_target_pairs={{0,1},{1,0},{2,3},{3,2},{4,5},{5,4},{6,7},{7,6},{8,9},{9,8},{10,11... | collective-permute-start | bytes 1253384 | tf_op jit(solution)/shard_map/ppermute | solution.py:339
  0.5 2.6 %collective-permute-start.2 = (bf16[136,512]{1,0:T(8,128)(2,1)}, bf16[136,512]{1,0:T(8,128)(2,1)S(1)}, u32[]{:S(2)}, u32[]{:S(2)}) collective-permute-start(bf16[136,512]{1,0:T(8,128)(2,1)} %bitcast.22), channel_id=1, source_target_pairs={{0,2},{1,3},{2,0},{3,1},{4,6},{5,7},{6,4},{7,5},{8,10},{9,11},{10,... | collective-permute-start | bytes 417800 | tf_op jit(solution)/shard_map/ppermute | solution.py:339
  3.1 0.0 copy-done.6
  3.1 0.5 %collective-permute-start.1 = (f32[3,2,1,512]{3,2,1,0:T(1,128)S(1)}, f32[3,2,1,512]{3,2,1,0:T(1,128)S(1)}, u32[]{:S(2)}, u32[]{:S(2)}) collective-permute-start(f32[3,2,1,512]{3,2,1,0:T(1,128)S(1)} %copy-done.6), channel_id=1, source_target_pairs={{0,2},{1,3},{2,0},{3,1},{4,6},{5,7},{6,4},{7,5},{8,10},{9,11},{10,... | collective-permute-start | bytes 36872 | tf_op jit(solution)/shard_map/ppermute | solution.py:339
  3.6 0.0 copy-start
  3.6 1.0 %copy-done = bf16[1,3,2,17,2048]{4,2,3,1,0:T(2,128)(2,1)S(1)} copy-done((bf16[1,3,2,17,2048]{4,2,3,1,0:T(2,128)(2,1)S(1)}, bf16[1,3,2,17,2048]{4,2,3,1,0:T(2,128)(2,1)}, u32[]{:S(2)}) %copy-start) | copy-done | bytes 417816
  4.7 0.9 %shard_map.100.beam_own = f32[3,2,24,1024]{3,2,1,0:T(8,128)S(1)} custom-call(s32[2]{0:T(128)S(1)} %pad_add_fusion.place, bf16[3,17,2,2048]{3,2,1,0:T(2,128)(2,1)S(1)} %bitcast.21), custom_call_target="tpu_custom_call" | custom-call | flops 4194304 | bytes 1048576 | tf_op jit(solution)/shard_map/pallas_call | solution.py:348
  5.6 0.0 copy-start.1
  5.6 0.0 collective-permute-done.source
  5.6 0.7 %shard_map.101.beam_other = f32[3,2,24,1024]{3,2,1,0:T(8,128)S(1)} custom-call(s32[2]{0:T(128)S(1)} %pad_add_fusion.place, bf16[3,17,2,2048]{3,2,1,0:T(2,128)(2,1)S(1)} %collective-permute-done.source), custom_call_target="tpu_custom_call" | custom-call | flops 4194304 | bytes 1048576 | tf_op jit(solution)/shard_map/pallas_call | solution.py:355
  6.3 1.6 %collective-permute-done.1.sky_other = f32[3,2,1,512]{3,2,1,0:T(1,128)S(1)} collective-permute-done((f32[3,2,1,512]{3,2,1,0:T(1,128)S(1)}, f32[3,2,1,512]{3,2,1,0:T(1,128)S(1)}, u32[]{:S(2)}, u32[]{:S(2)}) %collective-permute-start.1) | collective-permute-done | bytes 12320 | tf_op jit(solution)/shard_map/ppermute | solution.py:339
  7.8 0.0 collective-permute-done.2.w_other
  7.8 0.0 copy-done.1
  7.8 0.0 copy-start.2
  7.8 0.0 copy-start.4
  7.9 0.0 copy-start.5
  7.9 0.0 copy-start.8
  7.9 0.5 %shard_map.102 = f32[2,2,256]{2,1,0:T(2,128)S(1)} custom-call(f32[3,2,24,1024]{3,2,1,0:T(8,128)S(1)} %shard_map.100.beam_own, f32[3,2,24,1024]{3,2,1,0:T(8,128)S(1)} %shard_map.101.beam_other, f32[3,2,1,512]{3,2,1,0:T(1,128)S(1)} %copy-done.6, f32[3,2,1,512]{3,2,1,0:T(1,128)S(1)} %collective-permute-done.1.sky_other, bf16[136,512]{1,0:T(8,128)(2,1)S(1)} %bitcast.23, ...), custom_call_target="tpu_custom_call" | custom-call | flops 4194304 | bytes 1048576 | tf_op jit(solution)/shard_map/pallas_call | solution.py:356
  8.4 0.0 copy-start.3
  8.4 0.1 collective-permute-start.3
  8.5 1.2 %collective-permute-done.3 = f32[2,2,256]{2,1,0:T(2,128)S(1)} collective-permute-done((f32[2,2,256]{2,1,0:T(2,128)S(1)}, f32[2,2,256]{2,1,0:T(2,128)S(1)}, u32[]{:S(2)}, u32[]{:S(2)}) %collective-permute-start.3) | collective-permute-done | bytes 4128 | tf_op jit(solution)/shard_map/ppermute | solution.py:339
  9.6 0.0 copy-start.7
  9.6 1.6 %collective-permute-start.4 = (bf16[2,2,256]{2,1,0:T(2,128)(2,1)S(1)}, bf16[2,2,256]{2,1,0:T(2,128)(2,1)S(1)}, u32[]{:S(2)}, u32[]{:S(2)}) collective-permute-start(bf16[2,2,256]{2,1,0:T(2,128)(2,1)S(1)} %add_convert_fusion), channel_id=1, source_target_pairs={{0,5},{1,4},{2,7},{3,6},{4,1},{5,0},{6,3},{7,2},{8,13},{9,12},{10,... | collective-permute-start | bytes 6152 | tf_op jit(solution)/shard_map/ppermute | solution.py:339
  11.2 0.0 copy-start.9
  11.2 0.0 copy-done.2
  11.2 0.0 copy-done.4
  11.2 0.0 copy-done.5
  11.2 0.0 copy-done.8
  11.2 0.0 copy-done.3
  11.3 0.0 copy-done.7
  11.3 0.6 %copy-done.9 = s32[8]{0:T(128)S(1)} copy-done((s32[8]{0:T(128)S(1)}, s32[8]{0:T(128)}, u32[]{:S(2)}) %copy-start.9) | copy-done | bytes 56
  11.9 1.5 %shard_map.103 = (f32[32,2,8,128]{3,2,1,0:T(8,128)S(1)}, s32[32,128]{1,0:T(8,128)S(1)}, s32[32,128]{1,0:T(8,128)S(1)}) custom-call(s32[2]{0:T(128)S(1)} %pad_add_fusion.place, s32[8]{0:T(128)S(1)} %copy-done.9, s32[3,8]{1,0:T(4,128)S(1)} %bitcast.30, s32[8,2,8]{2,1,0:T(2,128)S(1)} %bitcast.29, s32[32,128]{1,0:T(8,128)S(1)} %bitcast.26, ...), custom_call_target="tpu_custom_call" | custom-call | flops 4194304 | bytes 1048576 | tf_op jit(solution)/shard_map/pallas_call | solution.py:365
  13.4 0.0 collective-permute-done.4
  13.4 3.7 %collective-permute-start.7 = (bf16[2,2,256]{2,1,0:T(2,128)(2,1)S(1)}, bf16[2,2,256]{2,1,0:T(2,128)(2,1)S(1)}, u32[]{:S(2)}, u32[]{:S(2)}) collective-permute-start(bf16[2,2,256]{2,1,0:T(2,128)(2,1)S(1)} %pad_maximum_fusion.1), channel_id=1, source_target_pairs={{0,25},{1,24},{2,27},{3,26},{4,29},{5,28},{6,31},{7,30},{8,17},{9,... | collective-permute-start | bytes 6152 | tf_op jit(solution)/shard_map/ppermute | solution.py:339
  17.1 0.0 collective-permute-start.6
  17.1 0.5 %collective-permute-start.5 = (bf16[2,2,256]{2,1,0:T(2,128)(2,1)S(1)}, bf16[2,2,256]{2,1,0:T(2,128)(2,1)S(1)}, u32[]{:S(2)}, u32[]{:S(2)}) collective-permute-start(bf16[2,2,256]{2,1,0:T(2,128)(2,1)S(1)} %pad_maximum_fusion.1), channel_id=1, source_target_pairs={{0,9},{1,8},{2,11},{3,10},{4,13},{5,12},{6,15},{7,14},{8,1},{9,0},... | collective-permute-start | bytes 6152 | tf_op jit(solution)/shard_map/ppermute | solution.py:339
  17.6 0.8 %collective-permute-done.7.refs_3_ = bf16[2,2,256]{2,1,0:T(2,128)(2,1)S(1)} collective-permute-done((bf16[2,2,256]{2,1,0:T(2,128)(2,1)S(1)}, bf16[2,2,256]{2,1,0:T(2,128)(2,1)S(1)}, u32[]{:S(2)}, u32[]{:S(2)}) %collective-permute-start.7) | collective-permute-done | bytes 2080 | tf_op jit(solution)/shard_map/ppermute | solution.py:339
  18.4 2.6 %collective-permute-done.6.refs_2_ = bf16[2,2,256]{2,1,0:T(2,128)(2,1)S(1)} collective-permute-done((bf16[2,2,256]{2,1,0:T(2,128)(2,1)S(1)}, bf16[2,2,256]{2,1,0:T(2,128)(2,1)S(1)}, u32[]{:S(2)}, u32[]{:S(2)}) %collective-permute-start.6) | collective-permute-done | bytes 2080 | tf_op jit(solution)/shard_map/ppermute | solution.py:339
  21.0 0.0 collective-permute-done.5.refs_1_
  21.0 1.3 %shard_map.104 = f32[32,128]{1,0:T(8,128)} custom-call(bf16[2,2,256]{2,1,0:T(2,128)(2,1)S(1)} %pad_maximum_fusion.refs_0_, bf16[2,2,256]{2,1,0:T(2,128)(2,1)S(1)} %collective-permute-done.5.refs_1_, bf16[2,2,256]{2,1,0:T(2,128)(2,1)S(1)} %collective-permute-done.6.refs_2_, bf16[2,2,256]{2,1,0:T(2,128)(2,1)S(1)} %collective-permute-done.7.refs_3_, ...), custom_call_target="tpu_custom_call" | custom-call | flops 4194304 | bytes 1048576 | tf_op jit(solution)/shard_map/pallas_call | solution.py:388
  (5 shorter events, 0.0 us)
Async XLA Ops:
  0.0 3.1 %copy-start.6 = (f32[3,2,1,512]{3,2,1,0:T(1,128)S(1)}, f32[3,2,1,512]{3,2,1,0:T(1,128)}, u32[]{:S(2)}) copy-start(f32[3,2,1,512]{3,2,1,0:T(1,128)} %sky_own.1) | copy-start | bytes 36868
  0.1 5.5 %collective-permute-start = (bf16[3,17,2,2048]{3,2,1,0:T(2,128)(2,1)}, bf16[3,17,2,2048]{3,2,1,0:T(2,128)(2,1)S(1)}, u32[]{:S(2)}, u32[]{:S(2)}) collective-permute-start(bf16[3,17,2,2048]{3,2,1,0:T(2,128)(2,1)} %bitcast.20), channel_id=1, source_target_pairs={{0,1},{1,0},{2,3},{3,2},{4,5},{5,4},{6,7},{7,6},{8,9},{9,8},{10,11... | collective-permute-start | bytes 1253384 | tf_op jit(solution)/shard_map/ppermute | solution.py:339
  0.5 7.3 %collective-permute-start.2 = (bf16[136,512]{1,0:T(8,128)(2,1)}, bf16[136,512]{1,0:T(8,128)(2,1)S(1)}, u32[]{:S(2)}, u32[]{:S(2)}) collective-permute-start(bf16[136,512]{1,0:T(8,128)(2,1)} %bitcast.22), channel_id=1, source_target_pairs={{0,2},{1,3},{2,0},{3,1},{4,6},{5,7},{6,4},{7,5},{8,10},{9,11},{10,... | collective-permute-start | bytes 417800 | tf_op jit(solution)/shard_map/ppermute | solution.py:339
  3.1 4.7 %collective-permute-start.1 = (f32[3,2,1,512]{3,2,1,0:T(1,128)S(1)}, f32[3,2,1,512]{3,2,1,0:T(1,128)S(1)}, u32[]{:S(2)}, u32[]{:S(2)}) collective-permute-start(f32[3,2,1,512]{3,2,1,0:T(1,128)S(1)} %copy-done.6), channel_id=1, source_target_pairs={{0,2},{1,3},{2,0},{3,1},{4,6},{5,7},{6,4},{7,5},{8,10},{9,11},{10,... | collective-permute-start | bytes 36872 | tf_op jit(solution)/shard_map/ppermute | solution.py:339
  3.6 1.0 %copy-start = (bf16[1,3,2,17,2048]{4,2,3,1,0:T(2,128)(2,1)S(1)}, bf16[1,3,2,17,2048]{4,2,3,1,0:T(2,128)(2,1)}, u32[]{:S(2)}) copy-start(bf16[1,3,2,17,2048]{4,2,3,1,0:T(2,128)(2,1)} %param.11) | copy-start | bytes 1253380
  5.6 2.3 %copy-start.1 = (bf16[1,17,512,8]{2,3,1,0:T(8,128)(2,1)S(1)}, bf16[1,17,512,8]{2,3,1,0:T(8,128)(2,1)}, u32[]{:S(2)}) copy-start(bf16[1,17,512,8]{2,3,1,0:T(8,128)(2,1)} %param.12) | copy-start | bytes 417796
  7.8 3.4 %copy-start.2 = (f32[2,1,4096]{2,1,0:T(1,128)S(1)}, f32[2,1,4096]{2,1,0:T(1,128)}, u32[]{:S(2)}) copy-start(f32[2,1,4096]{2,1,0:T(1,128)} %param.19) | copy-start | bytes 98308
  7.8 3.4 %copy-start.4 = (s32[1,4096]{1,0:T(1,128)S(1)}, s32[1,4096]{1,0:T(1,128)}, u32[]{:S(2)}) copy-start(s32[1,4096]{1,0:T(1,128)} %param.17) | copy-start | bytes 49156
  7.9 3.4 %copy-start.5 = (s32[1,4096]{1,0:T(1,128)S(1)}, s32[1,4096]{1,0:T(1,128)}, u32[]{:S(2)}) copy-start(s32[1,4096]{1,0:T(1,128)} %param.18) | copy-start | bytes 49156
  7.9 3.4 %copy-start.8 = (s32[8,3]{0,1:T(4,128)S(1)}, s32[8,3]{0,1:T(4,128)}, u32[]{:S(2)}) copy-start(s32[8,3]{0,1:T(4,128)} %param.14) | copy-start | bytes 292
  8.4 2.9 %copy-start.3 = (s32[1,4096]{1,0:T(1,128)S(1)}, s32[1,4096]{1,0:T(1,128)}, u32[]{:S(2)}) copy-start(s32[1,4096]{1,0:T(1,128)} %param.16) | copy-start | bytes 49156
  8.4 1.2 %collective-permute-start.3 = (f32[2,2,256]{2,1,0:T(2,128)S(1)}, f32[2,2,256]{2,1,0:T(2,128)S(1)}, u32[]{:S(2)}, u32[]{:S(2)}) collective-permute-start(f32[2,2,256]{2,1,0:T(2,128)S(1)} %shard_map.102), channel_id=1, source_target_pairs={{0,1},{1,0},{2,3},{3,2},{4,5},{5,4},{6,7},{7,6},{8,9},{9,8},{10,11... | collective-permute-start | bytes 12296 | tf_op jit(solution)/shard_map/ppermute | solution.py:339
  9.6 1.6 %copy-start.7 = (s32[1,8,8,2]{2,3,1,0:T(2,128)S(1)}, s32[1,8,8,2]{2,3,1,0:T(2,128)}, u32[]{:S(2)}) copy-start(s32[1,8,8,2]{2,3,1,0:T(2,128)} %param.15) | copy-start | bytes 1540
  9.6 3.7 %collective-permute-start.4 = (bf16[2,2,256]{2,1,0:T(2,128)(2,1)S(1)}, bf16[2,2,256]{2,1,0:T(2,128)(2,1)S(1)}, u32[]{:S(2)}, u32[]{:S(2)}) collective-permute-start(bf16[2,2,256]{2,1,0:T(2,128)(2,1)S(1)} %add_convert_fusion), channel_id=1, source_target_pairs={{0,5},{1,4},{2,7},{3,6},{4,1},{5,0},{6,3},{7,2},{8,13},{9,12},{10,... | collective-permute-start | bytes 6152 | tf_op jit(solution)/shard_map/ppermute | solution.py:339
  11.2 0.7 %copy-start.9 = (s32[8]{0:T(128)S(1)}, s32[8]{0:T(128)}, u32[]{:S(2)}) copy-start(s32[8]{0:T(128)} %m_values.1) | copy-start | bytes 100
  13.4 5.0 %collective-permute-start.7 = (bf16[2,2,256]{2,1,0:T(2,128)(2,1)S(1)}, bf16[2,2,256]{2,1,0:T(2,128)(2,1)S(1)}, u32[]{:S(2)}, u32[]{:S(2)}) collective-permute-start(bf16[2,2,256]{2,1,0:T(2,128)(2,1)S(1)} %pad_maximum_fusion.1), channel_id=1, source_target_pairs={{0,25},{1,24},{2,27},{3,26},{4,29},{5,28},{6,31},{7,30},{8,17},{9,... | collective-permute-start | bytes 6152 | tf_op jit(solution)/shard_map/ppermute | solution.py:339
  17.1 3.9 %collective-permute-start.6 = (bf16[2,2,256]{2,1,0:T(2,128)(2,1)S(1)}, bf16[2,2,256]{2,1,0:T(2,128)(2,1)S(1)}, u32[]{:S(2)}, u32[]{:S(2)}) collective-permute-start(bf16[2,2,256]{2,1,0:T(2,128)(2,1)S(1)} %pad_maximum_fusion.1), channel_id=1, source_target_pairs={{0,17},{1,16},{2,19},{3,18},{4,21},{5,20},{6,23},{7,22},{8,25},{9,... | collective-permute-start | bytes 6152 | tf_op jit(solution)/shard_map/ppermute | solution.py:339
  17.1 3.9 %collective-permute-start.5 = (bf16[2,2,256]{2,1,0:T(2,128)(2,1)S(1)}, bf16[2,2,256]{2,1,0:T(2,128)(2,1)S(1)}, u32[]{:S(2)}, u32[]{:S(2)}) collective-permute-start(bf16[2,2,256]{2,1,0:T(2,128)(2,1)S(1)} %pad_maximum_fusion.1), channel_id=1, source_target_pairs={{0,9},{1,8},{2,11},{3,10},{4,13},{5,12},{6,15},{7,14},{8,1},{9,0},... | collective-permute-start | bytes 6152 | tf_op jit(solution)/shard_map/ppermute | solution.py:339

commit v3 on v2

--- a/solution.py
+++ b/solution.py
@@ -136,23 +136,12 @@
     return pl.BlockSpec(memory_space=pltpu.VMEM)
 
 
-def cos_sin(turns, whole):
-    quarter = whole // 4
-    quadrant = (turns + quarter // 2) // quarter
-    rest = turns - quadrant * quarter
-    x = rest.astype(jnp.float32) * (2.0 * math.pi / whole)
+def cosine(turns, whole):
+    folded = jnp.abs((turns & (whole - 1)) - whole // 2) - whole // 4
+    x = folded.astype(jnp.float32) * (2.0 * math.pi / whole)
     y = x * x
-    sine = x * (1.0 + y * (-1.0 / 6 + y * (1.0 / 120 + y * (-1.0 / 5040 + y * (1.0 / 362880)))))
-    cosine = 1.0 + y * (
-        -0.5 + y * (1.0 / 24 + y * (-1.0 / 720 + y * (1.0 / 40320 - y * (1.0 / 3628800))))
-    )
-    quadrant = quadrant & 3
-    odd = (quadrant & 1) == 1
-    c = jnp.where(odd, sine, cosine)
-    s = jnp.where(odd, cosine, sine)
-    c = jnp.where((quadrant == 1) | (quadrant == 2), -c, c)
-    s = jnp.where(quadrant >= 2, -s, s)
-    return c, s
+    tail = 1.0 / 362880 - y * (1.0 / 39916800 - y * (1.0 / 6227020800))
+    return x * (1.0 + y * (-1.0 / 6 + y * (1.0 / 120 + y * (-1.0 / 5040 + y * tail))))
 
 
 def beam_kernel(place, source, out):
@@ -185,10 +174,13 @@
     for copy in copies:
         copy.start()
     orders = m_values.shape[0]
-    row = lax.broadcasted_iota(jnp.int32, (orders, LANES), 0)
-    m = jnp.zeros((orders, LANES), jnp.int32)
+    halves = phase.shape[0]
+    row = lax.broadcasted_iota(jnp.int32, phase.shape[2:], 0)
+    quarter = (row & 1) * (NPHI // 4)
+    m = [jnp.zeros_like(row) for _ in range(halves)]
     for k in range(orders):
-        m = jnp.where(row == k, m_values[place[1] ^ k], m)
+        half, line = divmod(k, orders // halves)
+        m[half] = jnp.where(row // 2 == line, m_values[place[1] ^ k], m[half])
     for copy in copies:
         copy.wait()
     scale = 2.0 / math.sqrt(orders * MPRIME)
@@ -208,14 +200,13 @@
     high[...] = cycle * NPSI + ((cell + 1) & (NPSI - 1))
     first = (start + phi[...]) & (NPHI - 1)
     for g in range(blocks.shape[0]):
-        turns = (m * first[g : g + 1, :]) & (NPHI - 1)
-        c0, s0 = cos_sin(turns, NPHI)
-        c1, s1 = cos_sin((turns + m) & (NPHI - 1), NPHI)
-        c0, s0, c1, s1 = (v.astype(jnp.bfloat16).astype(jnp.float32) for v in (c0, s0, c1, s1))
         f = frac[0, g : g + 1, :]
         e = 1.0 - f
-        phase[g, 0] = (e * c0 + f * c1) * scale
-        phase[g, 1] = (e * s0 + f * s1) * (-scale)
+        for half in range(halves):
+            turns = m[half] * first[g : g + 1, :] + quarter
+            at = cosine(turns, NPHI).astype(jnp.bfloat16).astype(jnp.float32)
+            after = cosine(turns + m[half], NPHI).astype(jnp.bfloat16).astype(jnp.float32)
+            phase[half, g] = (e * at + f * after) * scale
 
 
 def psi_weights(width):
@@ -224,7 +215,8 @@
     line = lax.broadcasted_iota(jnp.int32, shape, 0)
     imag = line >= ROWS
     n = jnp.where(imag, line - ROWS, line)
-    c, s = cos_sin(((n - BMAX) * lane) & (NPSI - 1), NPSI)
+    turns = (n - BMAX) * lane
+    c, s = cosine(turns, NPSI), cosine(turns - NPSI // 4, NPSI)
     return jnp.where(imag, -s, c), jnp.where(imag, c, s)
 
 
@@ -269,31 +261,46 @@
             out[side, s : s + 1, :] = jnp.sum(held * weights[s], 0, keepdims=True)
 
 
-def final_kernel(*refs):
-    *parts, phase, low, high, frac, out = refs
-    width = parts[0].shape[2]
-    rows = [part[k, :, :].astype(jnp.float32) for part in parts for k in range(part.shape[0])]
-    planes = [jnp.concatenate([row[s : s + 1] for row in rows], 0) for s in range(2)]
-    tiles = [[plane[:, t : t + LANES] for t in range(0, width, LANES)] for plane in planes]
-
-    def pick(table, index):
+def half_sum(part, phase, low, high, frac, g):
+    tiles = [part[:, t : t + LANES] for t in range(0, part.shape[1], LANES)]
+
+    def pick(index):
+        index = jnp.broadcast_to(index, (part.shape[0], LANES))
+        inside = index & (LANES - 1)
         value = None
-        inside = index & (LANES - 1)
-        for t, tile in enumerate(table):
+        for t, tile in enumerate(tiles):
             found = jnp.take_along_axis(tile, inside, axis=1, mode="promise_in_bounds")
             value = found if value is None else jnp.where(index >= t * LANES, found, value)
         return value
 
+    at_low, at_high = pick(low[g : g + 1, :]), pick(high[g : g + 1, :])
+    return (at_low + frac[1, g : g + 1, :] * (at_high - at_low)) * phase[g]
+
+
+def first_half_kernel(held, phase, low, high, frac, out):
+    part = jnp.concatenate([held[k, 0].astype(jnp.float32) for k in range(held.shape[0])], 0)
     for g in range(out.shape[0]):
-        shape = (len(rows), LANES)
-        at_low = jnp.broadcast_to(low[g : g + 1, :], shape)
-        at_high = jnp.broadcast_to(high[g : g + 1, :], shape)
-        f = frac[1, g : g + 1, :]
-        e = 1.0 - f
-        real = e * pick(tiles[0], at_low) + f * pick(tiles[0], at_high)
-        imag = e * pick(tiles[1], at_low) + f * pick(tiles[1], at_high)
-        total = real * phase[g, 0] + imag * phase[g, 1]
-        out[g : g + 1, :] = jnp.sum(total, 0, keepdims=True)
+        out[g] = half_sum(part, phase.at[0], low, high, frac, g)
+
+
+def row_sums(tiles):
+    row = lax.broadcasted_iota(jnp.int32, tiles[0].shape, 0)
+    for step in (1, 2, 4):
+        upper = (row & step) != 0
+        tiles = [
+            jnp.where(upper, b, a) + pltpu.roll(jnp.where(upper, a, b), step, 0)
+            for a, b in zip(tiles[::2], tiles[1::2])
+        ]
+    return tiles[0]
+
+
+def second_half_kernel(received, first, phase, low, high, frac, out):
+    part = jnp.concatenate([received[k].astype(jnp.float32) for k in range(received.shape[0])], 0)
+    for g in range(0, out.shape[0], 8):
+        totals = [
+            first[k] + half_sum(part, phase.at[1], low, high, frac, k) for k in range(g, g + 8)
+        ]
+        out[g : g + 8, :] = row_sums(totals)
 
 
 def call(kernel, out_shape, in_specs, flops, scratch=()):
@@ -353,19 +360,11 @@
         [pltpu.VMEM(beam.shape, beam.dtype), pltpu.SemaphoreType.DMA],
     )(place, beam)
     beam_other = call(beam_kernel, split, [smem(), vmem()], 1 << 22)(place, beam_other)
-    sums = call(rows_kernel, jax.ShapeDtypeStruct((2, 2, psi_width), f32), [vmem()] * 6, 1 << 22)(
-        beam_own, beam_other, sky_coeffs, sky_other, panel, panel_other
-    )
-    rows = (sums + swap(sums, 0, 1)[::-1]).astype(jnp.bfloat16)
-    rows_y = swap(rows, 1, 1)
-    block, phi, psi, frac, _ = lax.optimization_barrier(
-        (sample_block, sample_phi, sample_psi, sample_frac, rows)
-    )
     held = [pltpu.VMEM((groups, LANES), jnp.int32)] * 3 + [pltpu.VMEM((2, groups, LANES), f32)]
     phase, low, high = call(
         sample_kernel,
         (
-            jax.ShapeDtypeStruct((groups, 2, bands, LANES), f32),
+            jax.ShapeDtypeStruct((2, groups, bands, LANES), f32),
             jax.ShapeDtypeStruct((groups, LANES), jnp.int32),
             jax.ShapeDtypeStruct((groups, LANES), jnp.int32),
         ),
@@ -377,27 +376,37 @@
         m_values,
         cycle_table.T,
         jnp.transpose(send_lists[0], (0, 2, 1)),
-        block.reshape(groups, LANES),
-        phi.reshape(groups, LANES),
-        psi.reshape(groups, LANES),
-        frac.reshape(2, groups, LANES),
-    )
-    pair = jnp.stack([rows[0], rows_y[1]])
-    pair_other = jnp.stack([rows[1], rows_y[0]])
-    parts = [pair] + [swap(pair_other, k, 1) for k in range(2, bands, 2)]
+        sample_block.reshape(groups, LANES),
+        sample_phi.reshape(groups, LANES),
+        sample_psi.reshape(groups, LANES),
+        sample_frac.reshape(2, groups, LANES),
+    )
+    beam_own, phase = lax.optimization_barrier((beam_own, phase))
+    sums = call(rows_kernel, jax.ShapeDtypeStruct((2, 2, psi_width), f32), [vmem()] * 6, 1 << 22)(
+        beam_own, beam_other, sky_coeffs, sky_other, panel, panel_other
+    )
+    rows = (sums + swap(sums, 0, 1)[::-1]).astype(jnp.bfloat16)
+    rows_y = swap(rows, 1, 1)
+    pair = jnp.stack([rows, rows_y[::-1]])
+    quad = jnp.concatenate([pair, swap(pair, 2, 1)[:, ::-1]])
+    rest = swap(quad[:, 1], 4, 1)
+    samples = (phase, low, high, sample_frac.reshape(2, groups, LANES))
+    first = call(
+        first_half_kernel,
+        jax.ShapeDtypeStruct((groups, bands, LANES), f32),
+        [vmem()] * 5,
+        1 << 22,
+    )(quad, *samples)
     values = call(
-        final_kernel,
-        jax.ShapeDtypeStruct((groups, LANES), f32),
-        [vmem()] * (len(parts) + 4),
-        1 << 22,
-    )(*parts, phase, low, high, sample_frac.reshape(2, groups, LANES))
+        second_half_kernel, jax.ShapeDtypeStruct((groups, LANES), f32), [vmem()] * 6, 1 << 22
+    )(rest, first, *samples)
     return values.reshape(1, -1)
 
 
 def solution(mesh):
     def per_device(*args):
         cycles = args[2].shape[3]
-        small = mesh.shape["band"] <= 8 and cycles <= 8
+        small = mesh.shape["band"] == 8 and cycles <= 8
         return (by_samples if small else by_blocks)(*args)
 
     return jax.shard_map(

time: 22.5 us -> 21.7 us (0.964)
  starting transfers between devices: 9.38 us -> 8.77 us
  waiting for transfers between devices: 6.11 us -> 5.74 us
    ppermute x8 -> x7, starting transfers between devices: 9.38 us -> 8.77 us  [swap(): return lax.ppermute(x, ('band', 'det'), pairs)]
    ppermute x8 -> x7, waiting for transfers between devices: 6.11 us -> 5.74 us  [swap(): return lax.ppermute(x, ('band', 'det'), pairs)]
    pallas_call x2 -> x3, Pallas kernels: 2.78 us -> 2.77 us  [the longest x1 1.39 us: by_samples(): call(sample_kernel, (jax.ShapeDtypeStruct((2, groups, bands, LANES), f32)...]
  transfers between devices with their start and end apart: 8 -> 7, of which waited for: 4 -> 4; matrix products, arithmetic and copies ran while one was open for 0% -> 0% of each run, Pallas kernels for 14% -> 16%
where the time goes in v3:
time: 21.7 us; the launch traced here: 21.5 us
  starting transfers between devices  8.77 us (40%)
  waiting for transfers between devices  5.74 us (26%)
  Pallas kernels  4.85 us (22%)
  local copies, waits for them, and re-layouts  1.87 us (9%)
    ppermute x7, starting transfers between devices, swap(): return lax.ppermute(x, ('band', 'det'), pairs)  8.77 us
    ppermute x7, waiting for transfers between devices, swap(): return lax.ppermute(x, ('band', 'det'), pairs)  5.74 us
    unnamed x20, local copies, waits for them, and re-layouts  1.84 us
    pallas_call x1, Pallas kernels, by_samples(): call(sample_kernel, (jax.ShapeDtypeStruct((2, groups, bands, LANES), f32)...  1.39 us
    pallas_call x1, Pallas kernels, by_samples(): call(second_half_kernel, jax.ShapeDtypeStruct((groups, LANES), f32), [vme...  1 us
    pallas_call x1, Pallas kernels, by_samples(): call(beam_copy_kernel, split, [smem(), hbm()], 1 << 22, [pltpu.VMEM(beam....  0.91 us
    pallas_call x1, Pallas kernels, by_samples(): call(beam_kernel, split, [smem(), vmem()], 1 << 22)(place, beam_other)  0.68 us
    pallas_call x1, Pallas kernels, by_samples(): call(rows_kernel, jax.ShapeDtypeStruct((2, 2, psi_width), f32), [vmem()]...  0.49 us
  transfers between devices with their start and end apart: 7, of which 4 were waited for; matrix products, arithmetic and copies ran while one was open for 0% of the time, Pallas kernels for 16%

profile of v3, /device:TPU:0, one launch (start us, length us, event | category | flops | bytes accessed | tf_op | source)
XLA Modules:
  0.0 21.5 jit_solution(15819113338085748541)
XLA Ops:
  0.0 0.0 copy-start.6
  0.0 0.1 pad_add_fusion.place
  0.1 0.5 %collective-permute-start = (bf16[3,17,2,2048]{3,2,1,0:T(2,128)(2,1)}, bf16[3,17,2,2048]{3,2,1,0:T(2,128)(2,1)S(1)}, u32[]{:S(2)}, u32[]{:S(2)}) collective-permute-start(bf16[3,17,2,2048]{3,2,1,0:T(2,128)(2,1)} %bitcast.26), channel_id=1, source_target_pairs={{0,1},{1,0},{2,3},{3,2},{4,5},{5,4},{6,7},{7,6},{8,9},{9,8},{10,11... | collective-permute-start | bytes 1253384 | tf_op jit(solution)/shard_map/ppermute | solution.py:346
  0.5 2.6 %collective-permute-start.2 = (bf16[136,512]{1,0:T(8,128)(2,1)}, bf16[136,512]{1,0:T(8,128)(2,1)S(1)}, u32[]{:S(2)}, u32[]{:S(2)}) collective-permute-start(bf16[136,512]{1,0:T(8,128)(2,1)} %bitcast.31), channel_id=1, source_target_pairs={{0,2},{1,3},{2,0},{3,1},{4,6},{5,7},{6,4},{7,5},{8,10},{9,11},{10,... | collective-permute-start | bytes 417800 | tf_op jit(solution)/shard_map/ppermute | solution.py:346
  3.1 0.0 copy-done.6
  3.1 0.5 %collective-permute-start.1 = (f32[3,2,1,512]{3,2,1,0:T(1,128)S(1)}, f32[3,2,1,512]{3,2,1,0:T(1,128)S(1)}, u32[]{:S(2)}, u32[]{:S(2)}) collective-permute-start(f32[3,2,1,512]{3,2,1,0:T(1,128)S(1)} %copy-done.6), channel_id=1, source_target_pairs={{0,2},{1,3},{2,0},{3,1},{4,6},{5,7},{6,4},{7,5},{8,10},{9,11},{10,... | collective-permute-start | bytes 36872 | tf_op jit(solution)/shard_map/ppermute | solution.py:346
  3.6 0.0 copy-start
  3.6 1.0 %copy-done = bf16[1,3,2,17,2048]{4,2,3,1,0:T(2,128)(2,1)S(1)} copy-done((bf16[1,3,2,17,2048]{4,2,3,1,0:T(2,128)(2,1)S(1)}, bf16[1,3,2,17,2048]{4,2,3,1,0:T(2,128)(2,1)}, u32[]{:S(2)}) %copy-start) | copy-done | bytes 417816
  4.7 0.0 copy-start.1
  4.7 0.0 copy-start.3
  4.7 0.0 copy-start.4
  4.7 0.0 copy-start.5
  4.7 0.9 %shard_map.100.beam_own = f32[3,2,24,1024]{3,2,1,0:T(8,128)S(1)} custom-call(s32[2]{0:T(128)S(1)} %pad_add_fusion.place, bf16[3,17,2,2048]{3,2,1,0:T(2,128)(2,1)S(1)} %bitcast.27), custom_call_target="tpu_custom_call" | custom-call | flops 4194304 | bytes 1048576 | tf_op jit(solution)/shard_map/pallas_call | solution.py:355
  5.6 0.0 copy-start.7
  5.6 0.0 copy-start.8
  5.6 0.0 copy-start.9
  5.6 0.0 copy-done.1
  5.6 0.0 copy-done.3
  5.6 0.0 copy-done.4
  5.6 0.0 copy-done.5
  5.7 0.6 %copy-done.7 = s32[1,8,8,2]{2,3,1,0:T(2,128)S(1)} copy-done((s32[1,8,8,2]{2,3,1,0:T(2,128)S(1)}, s32[1,8,8,2]{2,3,1,0:T(2,128)}, u32[]{:S(2)}) %copy-start.7) | copy-done | bytes 536
  6.3 0.0 copy-done.8
  6.3 0.0 copy-done.9
  6.3 1.4 %shard_map.101 = (f32[2,32,8,128]{3,2,1,0:T(8,128)S(1)}, s32[32,128]{1,0:T(8,128)S(1)}, s32[32,128]{1,0:T(8,128)S(1)}) custom-call(s32[2]{0:T(128)S(1)} %pad_add_fusion.place, s32[8]{0:T(128)S(1)} %copy-done.9, s32[3,8]{1,0:T(4,128)S(1)} %bitcast.37, s32[8,2,8]{2,1,0:T(2,128)S(1)} %bitcast.36, s32[32,128]{1,0:T(8,128)S(1)} %bitcast.33, ...), custom_call_target="tpu_custom_call" | custom-call | flops 4194304 | bytes 1048576 | tf_op jit(solution)/shard_map/pallas_call | solution.py:364
  7.7 0.0 copy-start.2
  7.7 0.0 collective-permute-done.source
  7.7 0.7 %shard_map.102.beam_other = f32[3,2,24,1024]{3,2,1,0:T(8,128)S(1)} custom-call(s32[2]{0:T(128)S(1)} %pad_add_fusion.place, bf16[3,17,2,2048]{3,2,1,0:T(2,128)(2,1)S(1)} %collective-permute-done.source), custom_call_target="tpu_custom_call" | custom-call | flops 4194304 | bytes 1048576 | tf_op jit(solution)/shard_map/pallas_call | solution.py:362
  8.4 0.0 collective-permute-done.1.sky_other
  8.4 0.0 collective-permute-done.2.w_other
  8.4 0.2 copy-done.2
  8.6 0.5 %shard_map.103 = f32[2,2,256]{2,1,0:T(2,128)S(1)} custom-call(f32[3,2,24,1024]{3,2,1,0:T(8,128)S(1)} %shard_map.100.beam_own, f32[3,2,24,1024]{3,2,1,0:T(8,128)S(1)} %shard_map.102.beam_other, f32[3,2,1,512]{3,2,1,0:T(1,128)S(1)} %copy-done.6, f32[3,2,1,512]{3,2,1,0:T(1,128)S(1)} %collective-permute-done.1.sky_other, bf16[136,512]{1,0:T(8,128)(2,1)S(1)} %bitcast.32, ...), custom_call_target="tpu_custom_call" | custom-call | flops 4194304 | bytes 1048576 | tf_op jit(solution)/shard_map/pallas_call | solution.py:385
  9.1 0.1 collective-permute-start.3
  9.2 1.2 %collective-permute-done.3 = f32[2,2,256]{2,1,0:T(2,128)S(1)} collective-permute-done((f32[2,2,256]{2,1,0:T(2,128)S(1)}, f32[2,2,256]{2,1,0:T(2,128)S(1)}, u32[]{:S(2)}, u32[]{:S(2)}) %collective-permute-start.3) | collective-permute-done | bytes 4128 | tf_op jit(solution)/shard_map/ppermute | solution.py:346
  10.3 1.3 %collective-permute-start.4 = (bf16[2,2,256]{2,1,0:T(2,128)(2,1)S(1)}, bf16[2,2,256]{2,1,0:T(2,128)(2,1)S(1)}, u32[]{:S(2)}, u32[]{:S(2)}) collective-permute-start(bf16[2,2,256]{2,1,0:T(2,128)(2,1)S(1)} %add_convert_fusion), channel_id=1, source_target_pairs={{0,5},{1,4},{2,7},{3,6},{4,1},{5,0},{6,3},{7,2},{8,13},{9,12},{10,... | collective-permute-start | bytes 6152 | tf_op jit(solution)/shard_map/ppermute | solution.py:346
  11.6 1.7 %collective-permute-done.4 = bf16[2,2,256]{2,1,0:T(2,128)(2,1)S(1)} collective-permute-done((bf16[2,2,256]{2,1,0:T(2,128)(2,1)S(1)}, bf16[2,2,256]{2,1,0:T(2,128)(2,1)S(1)}, u32[]{:S(2)}, u32[]{:S(2)}) %collective-permute-start.4) | collective-permute-done | bytes 2080 | tf_op jit(solution)/shard_map/ppermute | solution.py:346
  13.4 1.4 %collective-permute-start.5 = (bf16[2,2,2,256]{3,2,0,1:T(2,128)(2,1)S(1)}, bf16[2,2,2,256]{3,2,0,1:T(2,128)(2,1)S(1)}, u32[]{:S(2)}, u32[]{:S(2)}) collective-permute-start(bf16[2,2,2,256]{3,2,0,1:T(2,128)(2,1)S(1)} %pad_maximum_fusion.1), channel_id=1, source_target_pairs={{0,9},{1,8},{2,11},{3,10},{4,13},{5,12},{6,15},{7,14},{8,1},{9,0},... | collective-permute-start | bytes 12296 | tf_op jit(solution)/shard_map/ppermute | solution.py:346
  14.8 1.7 %collective-permute-done.5 = bf16[2,2,2,256]{3,2,0,1:T(2,128)(2,1)S(1)} collective-permute-done((bf16[2,2,2,256]{3,2,0,1:T(2,128)(2,1)S(1)}, bf16[2,2,2,256]{3,2,0,1:T(2,128)(2,1)S(1)}, u32[]{:S(2)}, u32[]{:S(2)}) %collective-permute-start.5) | collective-permute-done | bytes 4128 | tf_op jit(solution)/shard_map/ppermute | solution.py:346
  16.5 2.4 %collective-permute-start.6 = (bf16[4,2,256]{2,1,0:T(2,128)(2,1)S(1)}, bf16[4,2,256]{2,1,0:T(2,128)(2,1)S(1)}, u32[]{:S(2)}, u32[]{:S(2)}) collective-permute-start(bf16[4,2,256]{2,1,0:T(2,128)(2,1)S(1)} %slice_bitcast_fusion), channel_id=1, source_target_pairs={{0,17},{1,16},{2,19},{3,18},{4,21},{5,20},{6,23},{7,22},{8,25},{9,... | collective-permute-start | bytes 12296 | tf_op jit(solution)/shard_map/ppermute | solution.py:346
  18.9 0.4 %shard_map.104.first = f32[32,8,128]{2,1,0:T(8,128)S(1)} custom-call(bf16[4,2,2,256]{3,2,1,0:T(2,128)(2,1)S(1)} %copy.15.held, f32[2,32,8,128]{3,2,1,0:T(8,128)S(1)} %get-tuple-element.16.phase, s32[32,128]{1,0:T(8,128)S(1)} %get-tuple-element.17.low, s32[32,128]{1,0:T(8,128)S(1)} %get-tuple-element.18.high, f32[2,32,128]{2,1,0:T(8,128)S(1)} %bitcast.29), custom_call_target="tpu_custom_call" | custom-call | flops 4194304 | bytes 1048576 | tf_op jit(solution)/shard_map/pallas_call | solution.py:394
  19.3 1.2 %collective-permute-done.6.received = bf16[4,2,256]{2,1,0:T(2,128)(2,1)S(1)} collective-permute-done((bf16[4,2,256]{2,1,0:T(2,128)(2,1)S(1)}, bf16[4,2,256]{2,1,0:T(2,128)(2,1)S(1)}, u32[]{:S(2)}, u32[]{:S(2)}) %collective-permute-start.6) | collective-permute-done | bytes 4128 | tf_op jit(solution)/shard_map/ppermute | solution.py:346
  20.5 1.0 %shard_map.105 = f32[32,128]{1,0:T(8,128)} custom-call(bf16[4,2,256]{2,1,0:T(2,128)(2,1)S(1)} %collective-permute-done.6.received, f32[32,8,128]{2,1,0:T(8,128)S(1)} %shard_map.104.first, f32[2,32,8,128]{3,2,1,0:T(8,128)S(1)} %get-tuple-element.16.phase, s32[32,128]{1,0:T(8,128)S(1)} %get-tuple-element.17.low, s32[32,128]{1,0:T(8,128)S(1)} %get-tuple-element.18.high, ...), custom_call_target="tpu_custom_call" | custom-call | flops 4194304 | bytes 1048576 | tf_op jit(solution)/shard_map/pallas_call | solution.py:400
  (7 shorter events, 0.1 us)
Async XLA Ops:
  0.0 3.1 %copy-start.6 = (f32[3,2,1,512]{3,2,1,0:T(1,128)S(1)}, f32[3,2,1,512]{3,2,1,0:T(1,128)}, u32[]{:S(2)}) copy-start(f32[3,2,1,512]{3,2,1,0:T(1,128)} %sky_own.1) | copy-start | bytes 36868
  0.1 7.6 %collective-permute-start = (bf16[3,17,2,2048]{3,2,1,0:T(2,128)(2,1)}, bf16[3,17,2,2048]{3,2,1,0:T(2,128)(2,1)S(1)}, u32[]{:S(2)}, u32[]{:S(2)}) collective-permute-start(bf16[3,17,2,2048]{3,2,1,0:T(2,128)(2,1)} %bitcast.26), channel_id=1, source_target_pairs={{0,1},{1,0},{2,3},{3,2},{4,5},{5,4},{6,7},{7,6},{8,9},{9,8},{10,11... | collective-permute-start | bytes 1253384 | tf_op jit(solution)/shard_map/ppermute | solution.py:346
  0.5 7.9 %collective-permute-start.2 = (bf16[136,512]{1,0:T(8,128)(2,1)}, bf16[136,512]{1,0:T(8,128)(2,1)S(1)}, u32[]{:S(2)}, u32[]{:S(2)}) collective-permute-start(bf16[136,512]{1,0:T(8,128)(2,1)} %bitcast.31), channel_id=1, source_target_pairs={{0,2},{1,3},{2,0},{3,1},{4,6},{5,7},{6,4},{7,5},{8,10},{9,11},{10,... | collective-permute-start | bytes 417800 | tf_op jit(solution)/shard_map/ppermute | solution.py:346
  3.1 5.3 %collective-permute-start.1 = (f32[3,2,1,512]{3,2,1,0:T(1,128)S(1)}, f32[3,2,1,512]{3,2,1,0:T(1,128)S(1)}, u32[]{:S(2)}, u32[]{:S(2)}) collective-permute-start(f32[3,2,1,512]{3,2,1,0:T(1,128)S(1)} %copy-done.6), channel_id=1, source_target_pairs={{0,2},{1,3},{2,0},{3,1},{4,6},{5,7},{6,4},{7,5},{8,10},{9,11},{10,... | collective-permute-start | bytes 36872 | tf_op jit(solution)/shard_map/ppermute | solution.py:346
  3.6 1.0 %copy-start = (bf16[1,3,2,17,2048]{4,2,3,1,0:T(2,128)(2,1)S(1)}, bf16[1,3,2,17,2048]{4,2,3,1,0:T(2,128)(2,1)}, u32[]{:S(2)}) copy-start(bf16[1,3,2,17,2048]{4,2,3,1,0:T(2,128)(2,1)} %param.11) | copy-start | bytes 1253380
  4.7 1.0 %copy-start.1 = (f32[2,1,4096]{2,1,0:T(1,128)S(1)}, f32[2,1,4096]{2,1,0:T(1,128)}, u32[]{:S(2)}) copy-start(f32[2,1,4096]{2,1,0:T(1,128)} %param.19) | copy-start | bytes 98308
  4.7 1.0 %copy-start.3 = (s32[1,4096]{1,0:T(1,128)S(1)}, s32[1,4096]{1,0:T(1,128)}, u32[]{:S(2)}) copy-start(s32[1,4096]{1,0:T(1,128)} %param.16) | copy-start | bytes 49156
  4.7 1.0 %copy-start.4 = (s32[1,4096]{1,0:T(1,128)S(1)}, s32[1,4096]{1,0:T(1,128)}, u32[]{:S(2)}) copy-start(s32[1,4096]{1,0:T(1,128)} %param.17) | copy-start | bytes 49156
  4.7 1.0 %copy-start.5 = (s32[1,4096]{1,0:T(1,128)S(1)}, s32[1,4096]{1,0:T(1,128)}, u32[]{:S(2)}) copy-start(s32[1,4096]{1,0:T(1,128)} %param.18) | copy-start | bytes 49156
  5.6 0.7 %copy-start.7 = (s32[1,8,8,2]{2,3,1,0:T(2,128)S(1)}, s32[1,8,8,2]{2,3,1,0:T(2,128)}, u32[]{:S(2)}) copy-start(s32[1,8,8,2]{2,3,1,0:T(2,128)} %param.15) | copy-start | bytes 1540
  5.6 0.7 %copy-start.8 = (s32[8,3]{0,1:T(4,128)S(1)}, s32[8,3]{0,1:T(4,128)}, u32[]{:S(2)}) copy-start(s32[8,3]{0,1:T(4,128)} %param.14) | copy-start | bytes 292
  5.6 0.7 %copy-start.9 = (s32[8]{0:T(128)S(1)}, s32[8]{0:T(128)}, u32[]{:S(2)}) copy-start(s32[8]{0:T(128)} %m_values.1) | copy-start | bytes 100
  7.7 0.9 %copy-start.2 = (bf16[1,17,512,8]{2,3,1,0:T(8,128)(2,1)S(1)}, bf16[1,17,512,8]{2,3,1,0:T(8,128)(2,1)}, u32[]{:S(2)}) copy-start(bf16[1,17,512,8]{2,3,1,0:T(8,128)(2,1)} %param.12) | copy-start | bytes 417796
  9.1 1.2 %collective-permute-start.3 = (f32[2,2,256]{2,1,0:T(2,128)S(1)}, f32[2,2,256]{2,1,0:T(2,128)S(1)}, u32[]{:S(2)}, u32[]{:S(2)}) collective-permute-start(f32[2,2,256]{2,1,0:T(2,128)S(1)} %shard_map.103), channel_id=1, source_target_pairs={{0,1},{1,0},{2,3},{3,2},{4,5},{5,4},{6,7},{7,6},{8,9},{9,8},{10,11... | collective-permute-start | bytes 12296 | tf_op jit(solution)/shard_map/ppermute | solution.py:346
  10.3 3.0 %collective-permute-start.4 = (bf16[2,2,256]{2,1,0:T(2,128)(2,1)S(1)}, bf16[2,2,256]{2,1,0:T(2,128)(2,1)S(1)}, u32[]{:S(2)}, u32[]{:S(2)}) collective-permute-start(bf16[2,2,256]{2,1,0:T(2,128)(2,1)S(1)} %add_convert_fusion), channel_id=1, source_target_pairs={{0,5},{1,4},{2,7},{3,6},{4,1},{5,0},{6,3},{7,2},{8,13},{9,12},{10,... | collective-permute-start | bytes 6152 | tf_op jit(solution)/shard_map/ppermute | solution.py:346
  13.4 3.1 %collective-permute-start.5 = (bf16[2,2,2,256]{3,2,0,1:T(2,128)(2,1)S(1)}, bf16[2,2,2,256]{3,2,0,1:T(2,128)(2,1)S(1)}, u32[]{:S(2)}, u32[]{:S(2)}) collective-permute-start(bf16[2,2,2,256]{3,2,0,1:T(2,128)(2,1)S(1)} %pad_maximum_fusion.1), channel_id=1, source_target_pairs={{0,9},{1,8},{2,11},{3,10},{4,13},{5,12},{6,15},{7,14},{8,1},{9,0},... | collective-permute-start | bytes 12296 | tf_op jit(solution)/shard_map/ppermute | solution.py:346
  16.5 4.0 %collective-permute-start.6 = (bf16[4,2,256]{2,1,0:T(2,128)(2,1)S(1)}, bf16[4,2,256]{2,1,0:T(2,128)(2,1)S(1)}, u32[]{:S(2)}, u32[]{:S(2)}) collective-permute-start(bf16[4,2,256]{2,1,0:T(2,128)(2,1)S(1)} %slice_bitcast_fusion), channel_id=1, source_target_pairs={{0,17},{1,16},{2,19},{3,18},{4,21},{5,20},{6,23},{7,22},{8,25},{9,... | collective-permute-start | bytes 12296 | tf_op jit(solution)/shard_map/ppermute | solution.py:346

commit v4 on v0

--- a/solution.py
+++ b/solution.py
@@ -3,6 +3,8 @@
 import jax
 import jax.numpy as jnp
 from jax import lax
+from jax.experimental import pallas as pl
+from jax.experimental.pallas import tpu as pltpu
 from jax.sharding import PartitionSpec as P
 
 BMAX = 8
@@ -10,6 +12,8 @@
 NPSI = 32
 NPHI = 4096
 BLOCK_PHI = 128
+LANES = 128
+ROWS = 24
 
 
 def psi_tables():
@@ -61,7 +65,7 @@
     return (1.0 - frac_psi) * low_row + frac_psi * high_row
 
 
-def per_device(
+def by_blocks(
     sky_coeffs,
     beam_coeffs,
     wigner_panel,
@@ -120,7 +124,257 @@
     return values[None, :]
 
 
+def vmem():
+    return pl.BlockSpec(memory_space=pltpu.VMEM)
+
+
+def cosine(turns):
+    x = jnp.abs(turns - jnp.floor(turns) - 0.5) - 0.25
+    y = x * x
+    total = jnp.zeros_like(x)
+    for k in (11, 9, 7, 5, 3, 1):
+        total = total * y + (-1.0) ** (k // 2) * (2.0 * math.pi) ** k / math.factorial(k)
+    return x * total
+
+
+def beam_kernel(source, out):
+    chunk = out.shape[3] // 2
+    det = lax.axis_index("det")
+    for part in range(2):
+        owner = det ^ (2 * part)
+        lanes = pl.ds(pl.multiple_of(owner * chunk, chunk), chunk)
+        for c in range(out.shape[0]):
+            block = source[c, :, :, lanes].astype(jnp.float32)
+            for s in range(2):
+                out[c, s, 0:MPRIME, part * chunk : (part + 1) * chunk] = block[:, s, :]
+    out[:, :, MPRIME:, :] = jnp.zeros_like(out[:, :, MPRIME:, :])
+
+
+def sample_kernel(turns, table, block, phi, psi, frac, phase, *index):
+    scale = 2.0 / math.sqrt(phase.shape[1] * MPRIME)
+    step = turns[...]
+    quarter = (lax.broadcasted_iota(jnp.int32, step.shape, 0) & 1).astype(jnp.float32) * 0.25
+    starts = jnp.broadcast_to(table[0:1, :], step.shape)
+    cycles = jnp.broadcast_to(table[1:2, :], step.shape)
+    eight = step.shape[0]
+    for h in range(0, block.shape[0], eight):
+        blocks = block[h : h + eight, :]
+        start = jnp.take_along_axis(starts, blocks, axis=1, mode="promise_in_bounds")
+        if index:
+            low, high = index
+            cycle = jnp.take_along_axis(cycles, blocks, axis=1, mode="promise_in_bounds")
+            cell = psi[h : h + eight, :]
+            low[h : h + eight, :] = cycle * NPSI + cell
+            high[h : h + eight, :] = cycle * NPSI + ((cell + 1) & (NPSI - 1))
+        first = ((start + phi[h : h + eight, :]) & (NPHI - 1)).astype(jnp.float32)
+        for g in range(eight):
+            f = frac[0, h + g : h + g + 1, :]
+            here = step * first[g : g + 1, :] + quarter
+            at = cosine(here).astype(jnp.bfloat16).astype(jnp.float32)
+            after = cosine(here + step).astype(jnp.bfloat16).astype(jnp.float32)
+            phase[h + g] = (at + f * (after - at)) * scale
+
+
+def psi_weights(width):
+    shape = (2 * ROWS, width)
+    lane = lax.broadcasted_iota(jnp.int32, shape, 1) & (NPSI - 1)
+    line = lax.broadcasted_iota(jnp.int32, shape, 0)
+    imag = line >= ROWS
+    n = jnp.where(imag, line - ROWS, line)
+    turns = ((n - BMAX) * lane).astype(jnp.float32) * (1.0 / NPSI)
+    c, s = cosine(turns), cosine(turns - 0.25)
+    return jnp.where(imag, -s, c), jnp.where(imag, c, s)
+
+
+def multipole_sum(part, beams, sky, w):
+    chunk = w.shape[1]
+    lanes = slice(part * chunk, (part + 1) * chunk)
+    pieces = []
+    for beam in beams:
+        real = imag = 0.0
+        for c in range(sky.shape[0]):
+            sr, si = sky[c, 0], sky[c, 1]
+            br, bi = beam[c, 0, :, lanes], beam[c, 1, :, lanes]
+            real += sr * br + si * bi
+            imag += si * br - sr * bi
+        pieces += [real, imag]
+    mixed = jnp.concatenate(pieces, 0).astype(jnp.bfloat16)
+    return lax.dot_general(
+        mixed, w[...], (((1,), (1,)), ((), ())), preferred_element_type=jnp.float32
+    )
+
+
+def near_kernel(beam_own, beam_other, sky, w, total, weights):
+    total[...] = multipole_sum(0, (beam_own, beam_other), sky, w)
+    weights[0], weights[1] = psi_weights(weights.shape[2])
+
+
+def rows_kernel(beam_own, beam_other, sky, w, near, weights, out):
+    cycles = w.shape[0] // MPRIME
+    total = near[...] + multipole_sum(1, (beam_own, beam_other), sky, w)
+    line = lax.broadcasted_iota(jnp.int32, total.shape, 0)
+    column = lax.broadcasted_iota(jnp.int32, total.shape, 1)
+    kept = jnp.where(lax.rem(line, ROWS) == lax.div(column, cycles), total, 0.0)
+    wide = (w.shape[0], weights.shape[2])
+    spread = (
+        lax.rem(lax.broadcasted_iota(jnp.int32, wide, 0), cycles)
+        == lax.div(lax.broadcasted_iota(jnp.int32, wide, 1), NPSI)
+    ).astype(jnp.bfloat16)
+    coeff = jnp.zeros((total.shape[0], wide[1]), jnp.float32)
+    for _ in range(3):
+        piece = kept.astype(jnp.bfloat16)
+        kept = kept - piece.astype(jnp.float32)
+        coeff += jnp.dot(piece, spread, preferred_element_type=jnp.float32)
+    for side in range(2):
+        held = coeff[side * 2 * ROWS : (side + 1) * 2 * ROWS]
+        for s in range(2):
+            out[side, s : s + 1, :] = jnp.sum(held * weights[s], 0, keepdims=True)
+
+
+def half_sum(part, phase, low, high, frac, g):
+    tiles = [part[:, t : t + LANES] for t in range(0, part.shape[1], LANES)]
+
+    def pick(index):
+        index = jnp.broadcast_to(index, (part.shape[0], LANES))
+        inside = index & (LANES - 1)
+        value = None
+        for t, tile in enumerate(tiles):
+            found = jnp.take_along_axis(tile, inside, axis=1, mode="promise_in_bounds")
+            value = found if value is None else jnp.where(index >= t * LANES, found, value)
+        return value
+
+    at_low, at_high = pick(low[g : g + 1, :]), pick(high[g : g + 1, :])
+    return (at_low + frac[1, g : g + 1, :] * (at_high - at_low)) * phase[g]
+
+
+def first_half_kernel(held, phase, low, high, frac, out):
+    part = jnp.concatenate([held[k, 0].astype(jnp.float32) for k in range(held.shape[0])], 0)
+    for g in range(out.shape[0]):
+        out[g] = half_sum(part, phase, low, high, frac, g)
+
+
+def row_sums(tiles):
+    row = lax.broadcasted_iota(jnp.int32, tiles[0].shape, 0)
+    for step in (1, 2, 4):
+        upper = (row & step) != 0
+        tiles = [
+            jnp.where(upper, b, a) + pltpu.roll(jnp.where(upper, a, b), step, 0)
+            for a, b in zip(tiles[::2], tiles[1::2])
+        ]
+    return tiles[0]
+
+
+def second_half_kernel(received, first, phase, low, high, frac, out):
+    part = jnp.concatenate([received[k].astype(jnp.float32) for k in range(received.shape[0])], 0)
+    for g in range(0, out.shape[0], 8):
+        totals = [
+            first[k] + half_sum(part, phase, low, high, frac, k) for k in range(g, g + 8)
+        ]
+        out[g : g + 8, :] = row_sums(totals)
+
+
+def call(kernel, out_shape, in_specs):
+    return pl.pallas_call(
+        kernel,
+        out_shape=out_shape,
+        in_specs=in_specs,
+        out_specs=jax.tree.map(lambda _: vmem(), out_shape),
+        cost_estimate=pl.CostEstimate(flops=1, bytes_accessed=1, transcendentals=0),
+        compiler_params=pltpu.CompilerParams(vmem_limit_bytes=24 << 20),
+    )
+
+
+def by_samples(
+    sky_coeffs,
+    beam_coeffs,
+    wigner_panel,
+    m_values,
+    cycle_table,
+    send_lists,
+    sample_block,
+    sample_phi,
+    sample_psi,
+    sample_frac,
+):
+    f32 = jnp.float32
+    bands = lax.axis_size("band")
+    band = lax.axis_index("band")
+    chunk, cycles = wigner_panel.shape[2:]
+    groups = sample_block.shape[1] // LANES
+    psi_width = cycles * NPSI
+
+    sizes = (bands, lax.axis_size("det"))
+
+    def swap(x, band_bits, det_bits):
+        pairs = [
+            (b * sizes[1] + d, (b ^ band_bits) * sizes[1] + (d ^ det_bits))
+            for b in range(sizes[0])
+            for d in range(sizes[1])
+        ]
+        return lax.ppermute(x, ("band", "det"), pairs)
+
+    panel = jnp.transpose(wigner_panel[0], (0, 2, 1)).reshape(MPRIME * cycles, chunk)
+    panel_other = swap(panel, 0, 2)
+    sky_other = swap(sky_coeffs, 0, 2)
+    beam = jnp.transpose(beam_coeffs[0], (0, 2, 1, 3))
+    beam_other = swap(beam, 0, 1)
+    split = jax.ShapeDtypeStruct((beam.shape[0], 2, ROWS, 2 * chunk), f32)
+    beam_own = call(beam_kernel, split, [vmem()])(beam)
+    beam_other = call(beam_kernel, split, [vmem()])(beam_other)
+    near_sum, psi = call(
+        near_kernel,
+        (
+            jax.ShapeDtypeStruct((4 * ROWS, MPRIME * cycles), f32),
+            jax.ShapeDtypeStruct((2, 2 * ROWS, psi_width), f32),
+        ),
+        [vmem()] * 4,
+    )(beam_own, beam_other, sky_coeffs, panel)
+    sums = call(rows_kernel, jax.ShapeDtypeStruct((2, 2, psi_width), f32), [vmem()] * 6)(
+        beam_own, beam_other, sky_other, panel_other, near_sum, psi
+    )
+    rows = (sums + swap(sums, 0, 1)[::-1]).astype(jnp.bfloat16)
+    rows_y = swap(rows, 1, 1)
+    here = lax.broadcasted_iota(jnp.int32, (bands, bands), 0) ^ band
+    there = lax.broadcasted_iota(jnp.int32, (bands, bands), 1)
+    turns = jnp.sum(jnp.where(here == there, m_values, 0), 1).astype(f32) * (1.0 / NPHI)
+    turns = jnp.broadcast_to(turns.reshape(2, bands // 2, 1, 1), (2, bands // 2, 2, LANES))
+    turns = turns.reshape(2, bands, LANES)
+    owners = lax.broadcasted_iota(jnp.int32, send_lists.shape[1:], 1)
+    codes = jnp.sum(jnp.where(owners == band, jnp.maximum(send_lists[0], 0), 0), 1)
+    slots = lax.broadcasted_iota(jnp.int32, (*codes.shape, cycle_table.shape[1]), 2)
+    chosen = jnp.where(slots == (codes // NPHI)[..., None], cycle_table[:, None, :], 0)
+    table = jnp.stack([codes % NPHI, jnp.sum(chosen, 2)]).reshape(2, -1)
+    table = jnp.pad(table, ((0, 0), (0, LANES - table.shape[1])))
+    weights = jax.ShapeDtypeStruct((groups, bands, LANES), f32)
+    index = jax.ShapeDtypeStruct((groups, LANES), jnp.int32)
+    frac = sample_frac.reshape(2, groups, LANES)
+    where = (sample_block, sample_phi, sample_psi)
+    samples = (*(a.reshape(groups, LANES) for a in where), frac)
+    table, _ = lax.optimization_barrier((table, rows))
+    near, low, high = call(sample_kernel, (weights, index, index), [vmem()] * 6)(
+        turns[0], table, *samples
+    )
+    rows_y, near = lax.optimization_barrier((rows_y, near))
+    pair = jnp.stack([rows, rows_y[::-1]])
+    pair_z = swap(pair, 2, 1)
+    table, _ = lax.optimization_barrier((table, pair))
+    far = call(sample_kernel, weights, [vmem()] * 6)(turns[1], table, *samples)
+    pair_z, far = lax.optimization_barrier((pair_z, far))
+    quad = jnp.concatenate([pair, pair_z[:, ::-1]])
+    rest = swap(quad[:, 1], 4, 1)
+    first = call(first_half_kernel, weights, [vmem()] * 5)(quad, near, low, high, frac)
+    values = call(
+        second_half_kernel, jax.ShapeDtypeStruct((groups, LANES), f32), [vmem()] * 6
+    )(rest, first, far, low, high, frac)
+    return values.reshape(1, -1)
+
+
 def solution(mesh):
+    def per_device(*args):
+        cycles = args[2].shape[3]
+        small = mesh.shape["band"] == 8 and cycles <= 8
+        return (by_samples if small else by_blocks)(*args)
+
     return jax.shard_map(
         per_device,
         mesh=mesh,

time: 215 us -> 20.9 us (0.10)
  local copies, waits for them, and re-layouts: 141 us -> 4.02 us
  waiting for transfers between devices: 40.9 us -> 4.16 us
  between operations: 13.7 us -> 0.17 us
  other arithmetic: 4.56 us -> 0.42 us
  starting transfers between devices: 13.1 us -> 8.97 us
  Pallas kernels: 0 us -> 2.9 us
    gather x6 -> x0, local copies, waits for them, and re-layouts: 106 us -> none  [the longest x1 25.6 us: interpolate(): value_ll = jnp.take(flat_cells, low_index).astype(jnp.float32)]
    all_to_all x3 -> x0, waiting for transfers between devices: 21 us -> none  [the longest x1 7.34 us: per_device(): lax.all_to_all(beam_coeffs, 'det', split_axis=4, concat_axis=0, tiled=True)]
    reduce_scatter x1 -> x0, waiting for transfers between devices: 19.9 us -> none  [per_device(): lax.psum_scatter(jnp.einsum('dsmnk,mnkr->dsmnr', mixed, wigner_panel, pre...]
    unnamed x20, local copies, waits for them, and re-layouts: 20.7 us -> 3.14 us
    all_to_all x3 -> x0, starting transfers between devices: 13.1 us -> none  [the longest x1 5.51 us: per_device(): lax.all_to_all(payload, 'band', split_axis=0, concat_axis=0, tiled=True)]
    ppermute x0 -> x7, starting transfers between devices: none -> 8.97 us  [swap(): return lax.ppermute(x, ('band', 'det'), pairs)]
    all_to_all x1 -> x0, local copies, waits for them, and re-layouts: 6.12 us -> none  [per_device(): lax.all_to_all(beam_coeffs, 'det', split_axis=4, concat_axis=0, tiled=True)]
    concatenate x3 -> x1, local copies, waits for them, and re-layouts: 4.8 us -> 0.01 us  [by_samples(): quad = jnp.concatenate([pair, pair_z[:, ::-1]])]
  transfers between devices with their start and end apart: 4 -> 7, of which waited for: 4 -> 5; matrix products, arithmetic and copies ran while one was open for 1% -> 6% of each run, Pallas kernels for 0% -> 7%
where the time goes in v4:
time: 20.9 us; the launch traced here: 20.6 us
  starting transfers between devices  8.97 us (43%)
  waiting for transfers between devices  4.16 us (20%)
  local copies, waits for them, and re-layouts  4.02 us (19%)
  Pallas kernels  2.9 us (14%)
  other arithmetic  0.42 us (2%)
    ppermute x7, starting transfers between devices, swap(): return lax.ppermute(x, ('band', 'det'), pairs)  8.97 us
    ppermute x7, waiting for transfers between devices, swap(): return lax.ppermute(x, ('band', 'det'), pairs)  4.16 us
    unnamed x20, local copies, waits for them, and re-layouts  3.14 us
    pallas_call x1, Pallas kernels, by_samples(): call(second_half_kernel, jax.ShapeDtypeStruct((groups, LANES), f32), [vme...  1 us
    broadcast_in_dim x6, local copies, waits for them, and re-layouts, by_samples(): jnp.broadcast_to(turns.reshape(2, bands // 2, 1, 1), (2, bands // 2, 2, L...  0.45 us
  transfers between devices with their start and end apart: 7, of which 5 were waited for; matrix products, arithmetic and copies ran while one was open for 6% of the time, Pallas kernels for 7%

profile of v4, /device:TPU:0, one launch (start us, length us, event | category | flops | bytes accessed | tf_op | source)
XLA Modules:
  0.0 20.6 jit_solution(6011514598899724604)
XLA Ops:
  0.0 0.5 %collective-permute-start = (bf16[3,17,2,2048]{3,2,1,0:T(2,128)(2,1)}, bf16[3,17,2,2048]{3,2,1,0:T(2,128)(2,1)S(1)}, u32[]{:S(2)}, u32[]{:S(2)}) collective-permute-start(bf16[3,17,2,2048]{3,2,1,0:T(2,128)(2,1)} %bitcast.28), channel_id=1, source_target_pairs={{0,1},{1,0},{2,3},{3,2},{4,5},{5,4},{6,7},{7,6},{8,9},{9,8},{10,11... | collective-permute-start | bytes 1253384 | tf_op jit(solution)/shard_map/ppermute | solution.py:314
  0.5 2.5 %collective-permute-start.2 = (bf16[136,512]{1,0:T(8,128)(2,1)}, bf16[136,512]{1,0:T(8,128)(2,1)S(1)}, u32[]{:S(2)}, u32[]{:S(2)}) collective-permute-start(bf16[136,512]{1,0:T(8,128)(2,1)} %bitcast.30), channel_id=1, source_target_pairs={{0,2},{1,3},{2,0},{3,1},{4,6},{5,7},{6,4},{7,5},{8,10},{9,11},{10,... | collective-permute-start | bytes 417800 | tf_op jit(solution)/shard_map/ppermute | solution.py:314
  2.9 0.1 collective-permute-start.1
  3.0 1.0 %copy-done.1 = bf16[1,3,2,17,2048]{4,2,3,1,0:T(2,128)(2,1)S(1)} copy-done((bf16[1,3,2,17,2048]{4,2,3,1,0:T(2,128)(2,1)S(1)}, bf16[1,3,2,17,2048]{4,2,3,1,0:T(2,128)(2,1)}, u32[]{:S(2)}) %copy-start.1) | copy-done | bytes 417816
  4.0 0.1 shard_map.100.beam_own
  4.2 0.0 copy-start.7
  4.2 0.7 %copy-done.7 = s32[1,8,8,2]{2,3,1,0:T(2,128)S(1)} copy-done((s32[1,8,8,2]{2,3,1,0:T(2,128)S(1)}, s32[1,8,8,2]{2,3,1,0:T(2,128)}, u32[]{:S(2)}) %copy-start.7) | copy-done | bytes 536
  4.9 0.1 fusion
  5.0 0.1 copy.29
  5.1 0.1 reduce_sum.31
  5.2 0.6 %copy-done.9 = s32[8]{0:T(128)S(1)} copy-done((s32[8]{0:T(128)S(1)}, s32[8]{0:T(128)}, u32[]{:S(2)}) %copy-start.9) | copy-done | bytes 56
  5.8 0.2 select_reduce_fusion
  5.9 0.1 fusion.3
  6.0 0.0 copy-start.6
  6.0 0.0 collective-permute-done.source
  6.1 0.1 shard_map.101.beam_other
  6.2 0.7 %copy-done.2 = bf16[1,17,512,8]{2,3,1,0:T(8,128)(2,1)S(1)} copy-done((bf16[1,17,512,8]{2,3,1,0:T(8,128)(2,1)S(1)}, bf16[1,17,512,8]{2,3,1,0:T(8,128)(2,1)}, u32[]{:S(2)}) %copy-start.2) | copy-done | bytes 139288
  6.9 0.0 copy-done.6
  6.9 0.2 %shard_map.102 = (f32[96,136]{1,0:T(8,128)S(1)}, f32[2,48,256]{2,1,0:T(8,128)S(1)}) custom-call(f32[3,2,24,1024]{3,2,1,0:T(8,128)S(1)} %shard_map.100.beam_own, f32[3,2,24,1024]{3,2,1,0:T(8,128)S(1)} %shard_map.101.beam_other, f32[3,2,1,512]{3,2,1,0:T(1,128)S(1)} %copy-done.6, bf16[136,512]{1,0:T(8,128)(2,1)S(1)} %bitcast.31), custom_call_target="tpu_custom_call" | custom-call | flops 1 | bytes 1 | tf_op jit(solution)/shard_map/pallas_call | solution.py:324
  7.2 0.6 %collective-permute-done.1.sky = f32[3,2,1,512]{3,2,1,0:T(1,128)S(1)} collective-permute-done((f32[3,2,1,512]{3,2,1,0:T(1,128)}, f32[3,2,1,512]{3,2,1,0:T(1,128)S(1)}, u32[]{:S(2)}, u32[]{:S(2)}) %collective-permute-start.1) | collective-permute-done | bytes 12320 | tf_op jit(solution)/shard_map/ppermute | solution.py:314
  7.8 0.0 collective-permute-done.2.w
  7.8 0.0 copy-start.5
  7.8 0.4 %shard_map.103 = f32[2,2,256]{2,1,0:T(2,128)S(1)} custom-call(f32[3,2,24,1024]{3,2,1,0:T(8,128)S(1)} %shard_map.100.beam_own, f32[3,2,24,1024]{3,2,1,0:T(8,128)S(1)} %shard_map.101.beam_other, f32[3,2,1,512]{3,2,1,0:T(1,128)S(1)} %collective-permute-done.1.sky, bf16[136,512]{1,0:T(8,128)(2,1)S(1)} %collective-permute-done.2.w, ...), custom_call_target="tpu_custom_call" | custom-call | flops 1 | bytes 1 | tf_op jit(solution)/shard_map/pallas_call | solution.py:332
  8.2 0.0 copy-start
  8.2 0.1 collective-permute-start.3
  8.3 0.1 copy-done.8
  8.5 0.1 copy.30
  8.5 0.1 stack.17
  8.6 0.8 %collective-permute-done.3 = f32[2,2,256]{2,1,0:T(2,128)S(1)} collective-permute-done((f32[2,2,256]{2,1,0:T(2,128)S(1)}, f32[2,2,256]{2,1,0:T(2,128)S(1)}, u32[]{:S(2)}, u32[]{:S(2)}) %collective-permute-start.3) | collective-permute-done | bytes 4128 | tf_op jit(solution)/shard_map/ppermute | solution.py:314
  9.5 1.5 %collective-permute-start.4 = (bf16[2,2,256]{2,1,0:T(2,128)(2,1)S(1)}, bf16[2,2,256]{2,1,0:T(2,128)(2,1)S(1)}, u32[]{:S(2)}, u32[]{:S(2)}) collective-permute-start(bf16[2,2,256]{2,1,0:T(2,128)(2,1)S(1)} %add_convert_fusion), channel_id=1, source_target_pairs={{0,5},{1,4},{2,7},{3,6},{4,1},{5,0},{6,3},{7,2},{8,13},{9,12},{10,... | collective-permute-start | bytes 6152 | tf_op jit(solution)/shard_map/ppermute | solution.py:314
  11.0 0.1 broadcast_in_dim.41
  11.1 0.1 broadcast_in_dim.42
  11.2 0.1 broadcast_in_dim.43.turns
  11.2 0.0 copy-done.3
  11.2 0.0 copy-done.4
  11.2 0.0 copy-done.5
  11.3 0.3 %shard_map.104 = (f32[32,8,128]{2,1,0:T(8,128)S(1)}, s32[32,128]{1,0:T(8,128)S(1)}, s32[32,128]{1,0:T(8,128)S(1)}) custom-call(f32[8,128]{1,0:T(8,128)S(1)} %broadcast_in_dim.43.turns, s32[2,128]{1,0:T(2,128)S(1)} %pad.4.table, s32[32,128]{1,0:T(8,128)S(1)} %bitcast.32, s32[32,128]{1,0:T(8,128)S(1)} %bitcast.34, s32[32,128]{1,0:T(8,128)S(1)} %bitcast.36, ...), custom_call_target="tpu_custom_call" | custom-call | flops 1 | bytes 1 | tf_op jit(solution)/shard_map/pallas_call | solution.py:354
  11.6 0.9 %collective-permute-done.4 = bf16[2,2,256]{2,1,0:T(2,128)(2,1)S(1)} collective-permute-done((bf16[2,2,256]{2,1,0:T(2,128)(2,1)S(1)}, bf16[2,2,256]{2,1,0:T(2,128)(2,1)S(1)}, u32[]{:S(2)}, u32[]{:S(2)}) %collective-permute-start.4) | collective-permute-done | bytes 2080 | tf_op jit(solution)/shard_map/ppermute | solution.py:314
  12.5 1.7 %collective-permute-start.5 = (bf16[2,2,2,256]{3,2,0,1:T(2,128)(2,1)S(1)}, bf16[2,2,2,256]{3,2,0,1:T(2,128)(2,1)S(1)}, u32[]{:S(2)}, u32[]{:S(2)}) collective-permute-start(bf16[2,2,2,256]{3,2,0,1:T(2,128)(2,1)S(1)} %pad_maximum_fusion.1), channel_id=1, source_target_pairs={{0,9},{1,8},{2,11},{3,10},{4,13},{5,12},{6,15},{7,14},{8,1},{9,0},... | collective-permute-start | bytes 12296 | tf_op jit(solution)/shard_map/ppermute | solution.py:314
  14.2 0.1 broadcast_in_dim.46
  14.2 0.1 broadcast_in_dim.47
  14.3 0.1 broadcast_in_dim.48.turns
  14.4 0.3 %shard_map.105.phase = f32[32,8,128]{2,1,0:T(8,128)S(1)} custom-call(f32[8,128]{1,0:T(8,128)S(1)} %broadcast_in_dim.48.turns, s32[2,128]{1,0:T(2,128)S(1)} %pad.4.table, s32[32,128]{1,0:T(8,128)S(1)} %bitcast.33, s32[32,128]{1,0:T(8,128)S(1)} %bitcast.35, s32[32,128]{1,0:T(8,128)S(1)} %bitcast.37, f32[2,32,128]{2,1,0:T(8,128)S(1)} %bitcast.25), custom_call_target="tpu_custom_call" | custom-call | flops 1 | bytes 1 | tf_op jit(solution)/shard_map/pallas_call | solution.py:361
  14.7 0.9 %collective-permute-done.5 = bf16[2,2,2,256]{3,2,0,1:T(2,128)(2,1)S(1)} collective-permute-done((bf16[2,2,2,256]{3,2,0,1:T(2,128)(2,1)S(1)}, bf16[2,2,2,256]{3,2,0,1:T(2,128)(2,1)S(1)}, u32[]{:S(2)}, u32[]{:S(2)}) %collective-permute-start.5) | collective-permute-done | bytes 4128 | tf_op jit(solution)/shard_map/ppermute | solution.py:314
  15.6 2.7 %collective-permute-start.6 = (bf16[4,2,256]{2,1,0:T(2,128)(2,1)S(1)}, bf16[4,2,256]{2,1,0:T(2,128)(2,1)S(1)}, u32[]{:S(2)}, u32[]{:S(2)}) collective-permute-start(bf16[4,2,256]{2,1,0:T(2,128)(2,1)S(1)} %slice_bitcast_fusion), channel_id=1, source_target_pairs={{0,17},{1,16},{2,19},{3,18},{4,21},{5,20},{6,23},{7,22},{8,25},{9,... | collective-permute-start | bytes 12296 | tf_op jit(solution)/shard_map/ppermute | solution.py:314
  18.3 0.4 %shard_map.106.first = f32[32,8,128]{2,1,0:T(8,128)S(1)} custom-call(bf16[4,2,2,256]{3,2,1,0:T(2,128)(2,1)S(1)} %copy.33.held, f32[32,8,128]{2,1,0:T(8,128)S(1)} %get-tuple-element.23.phase, s32[32,128]{1,0:T(8,128)S(1)} %get-tuple-element.24.low, s32[32,128]{1,0:T(8,128)S(1)} %get-tuple-element.25.high, f32[2,32,128]{2,1,0:T(8,128)S(1)} %bitcast.26), custom_call_target="tpu_custom_call" | custom-call | flops 1 | bytes 1 | tf_op jit(solution)/shard_map/pallas_call | solution.py:365
  18.7 0.9 %collective-permute-done.6.received = bf16[4,2,256]{2,1,0:T(2,128)(2,1)S(1)} collective-permute-done((bf16[4,2,256]{2,1,0:T(2,128)(2,1)S(1)}, bf16[4,2,256]{2,1,0:T(2,128)(2,1)S(1)}, u32[]{:S(2)}, u32[]{:S(2)}) %collective-permute-start.6) | collective-permute-done | bytes 4128 | tf_op jit(solution)/shard_map/ppermute | solution.py:314
  19.6 1.0 %shard_map.107 = f32[32,128]{1,0:T(8,128)} custom-call(bf16[4,2,256]{2,1,0:T(2,128)(2,1)S(1)} %collective-permute-done.6.received, f32[32,8,128]{2,1,0:T(8,128)S(1)} %shard_map.106.first, f32[32,8,128]{2,1,0:T(8,128)S(1)} %shard_map.105.phase, s32[32,128]{1,0:T(8,128)S(1)} %get-tuple-element.24.low, s32[32,128]{1,0:T(8,128)S(1)} %get-tuple-element.25.high, ...), custom_call_target="tpu_custom_call" | custom-call | flops 1 | bytes 1 | tf_op jit(solution)/shard_map/pallas_call | solution.py:366
  (22 shorter events, 0.1 us)
Async XLA Ops:
  0.0 6.1 %collective-permute-start = (bf16[3,17,2,2048]{3,2,1,0:T(2,128)(2,1)}, bf16[3,17,2,2048]{3,2,1,0:T(2,128)(2,1)S(1)}, u32[]{:S(2)}, u32[]{:S(2)}) collective-permute-start(bf16[3,17,2,2048]{3,2,1,0:T(2,128)(2,1)} %bitcast.28), channel_id=1, source_target_pairs={{0,1},{1,0},{2,3},{3,2},{4,5},{5,4},{6,7},{7,6},{8,9},{9,8},{10,11... | collective-permute-start | bytes 1253384 | tf_op jit(solution)/shard_map/ppermute | solution.py:314
  0.5 7.3 %collective-permute-start.2 = (bf16[136,512]{1,0:T(8,128)(2,1)}, bf16[136,512]{1,0:T(8,128)(2,1)S(1)}, u32[]{:S(2)}, u32[]{:S(2)}) collective-permute-start(bf16[136,512]{1,0:T(8,128)(2,1)} %bitcast.30), channel_id=1, source_target_pairs={{0,2},{1,3},{2,0},{3,1},{4,6},{5,7},{6,4},{7,5},{8,10},{9,11},{10,... | collective-permute-start | bytes 417800 | tf_op jit(solution)/shard_map/ppermute | solution.py:314
  2.9 4.8 %collective-permute-start.1 = (f32[3,2,1,512]{3,2,1,0:T(1,128)}, f32[3,2,1,512]{3,2,1,0:T(1,128)S(1)}, u32[]{:S(2)}, u32[]{:S(2)}) collective-permute-start(f32[3,2,1,512]{3,2,1,0:T(1,128)} %sky.1), channel_id=1, source_target_pairs={{0,2},{1,3},{2,0},{3,1},{4,6},{5,7},{6,4},{7,5},{8,10},{9,11},{10,... | collective-permute-start | bytes 36872 | tf_op jit(solution)/shard_map/ppermute | solution.py:314
  3.0 1.0 %copy-start.1 = (bf16[1,3,2,17,2048]{4,2,3,1,0:T(2,128)(2,1)S(1)}, bf16[1,3,2,17,2048]{4,2,3,1,0:T(2,128)(2,1)}, u32[]{:S(2)}) copy-start(bf16[1,3,2,17,2048]{4,2,3,1,0:T(2,128)(2,1)} %param.11) | copy-start | bytes 1253380
  4.2 0.7 %copy-start.7 = (s32[1,8,8,2]{2,3,1,0:T(2,128)S(1)}, s32[1,8,8,2]{2,3,1,0:T(2,128)}, u32[]{:S(2)}) copy-start(s32[1,8,8,2]{2,3,1,0:T(2,128)} %param.15) | copy-start | bytes 1540
  5.1 0.7 %copy-start.9 = (s32[8]{0:T(128)S(1)}, s32[8]{0:T(128)}, u32[]{:S(2)}) copy-start(s32[8]{0:T(128)} %param.13) | copy-start | bytes 100
  6.0 0.9 %copy-start.2 = (bf16[1,17,512,8]{2,3,1,0:T(8,128)(2,1)S(1)}, bf16[1,17,512,8]{2,3,1,0:T(8,128)(2,1)}, u32[]{:S(2)}) copy-start(bf16[1,17,512,8]{2,3,1,0:T(8,128)(2,1)} %param.12) | copy-start | bytes 417796
  6.0 0.9 %copy-start.6 = (f32[3,2,1,512]{3,2,1,0:T(1,128)S(1)}, f32[3,2,1,512]{3,2,1,0:T(1,128)}, u32[]{:S(2)}) copy-start(f32[3,2,1,512]{3,2,1,0:T(1,128)} %sky.1) | copy-start | bytes 36868
  7.8 0.7 %copy-start.8 = (s32[8,3]{0,1:T(4,128)S(1)}, s32[8,3]{0,1:T(4,128)}, u32[]{:S(2)}) copy-start(s32[8,3]{0,1:T(4,128)} %param.14) | copy-start | bytes 292
  7.8 3.5 %copy-start.3 = (s32[1,4096]{1,0:T(1,128)S(1)}, s32[1,4096]{1,0:T(1,128)}, u32[]{:S(2)}) copy-start(s32[1,4096]{1,0:T(1,128)} %param.16) | copy-start | bytes 49156
  7.8 3.5 %copy-start.4 = (s32[1,4096]{1,0:T(1,128)S(1)}, s32[1,4096]{1,0:T(1,128)}, u32[]{:S(2)}) copy-start(s32[1,4096]{1,0:T(1,128)} %param.17) | copy-start | bytes 49156
  7.8 3.5 %copy-start.5 = (s32[1,4096]{1,0:T(1,128)S(1)}, s32[1,4096]{1,0:T(1,128)}, u32[]{:S(2)}) copy-start(s32[1,4096]{1,0:T(1,128)} %param.18) | copy-start | bytes 49156
  8.2 3.0 %copy-start = (f32[2,1,4096]{2,1,0:T(1,128)S(1)}, f32[2,1,4096]{2,1,0:T(1,128)}, u32[]{:S(2)}) copy-start(f32[2,1,4096]{2,1,0:T(1,128)} %param.19) | copy-start | bytes 98308
  8.2 1.2 %collective-permute-start.3 = (f32[2,2,256]{2,1,0:T(2,128)S(1)}, f32[2,2,256]{2,1,0:T(2,128)S(1)}, u32[]{:S(2)}, u32[]{:S(2)}) collective-permute-start(f32[2,2,256]{2,1,0:T(2,128)S(1)} %shard_map.103), channel_id=1, source_target_pairs={{0,1},{1,0},{2,3},{3,2},{4,5},{5,4},{6,7},{7,6},{8,9},{9,8},{10,11... | collective-permute-start | bytes 12296 | tf_op jit(solution)/shard_map/ppermute | solution.py:314
  9.5 3.0 %collective-permute-start.4 = (bf16[2,2,256]{2,1,0:T(2,128)(2,1)S(1)}, bf16[2,2,256]{2,1,0:T(2,128)(2,1)S(1)}, u32[]{:S(2)}, u32[]{:S(2)}) collective-permute-start(bf16[2,2,256]{2,1,0:T(2,128)(2,1)S(1)} %add_convert_fusion), channel_id=1, source_target_pairs={{0,5},{1,4},{2,7},{3,6},{4,1},{5,0},{6,3},{7,2},{8,13},{9,12},{10,... | collective-permute-start | bytes 6152 | tf_op jit(solution)/shard_map/ppermute | solution.py:314
  12.5 3.1 %collective-permute-start.5 = (bf16[2,2,2,256]{3,2,0,1:T(2,128)(2,1)S(1)}, bf16[2,2,2,256]{3,2,0,1:T(2,128)(2,1)S(1)}, u32[]{:S(2)}, u32[]{:S(2)}) collective-permute-start(bf16[2,2,2,256]{3,2,0,1:T(2,128)(2,1)S(1)} %pad_maximum_fusion.1), channel_id=1, source_target_pairs={{0,9},{1,8},{2,11},{3,10},{4,13},{5,12},{6,15},{7,14},{8,1},{9,0},... | collective-permute-start | bytes 12296 | tf_op jit(solution)/shard_map/ppermute | solution.py:314
  15.6 4.0 %collective-permute-start.6 = (bf16[4,2,256]{2,1,0:T(2,128)(2,1)S(1)}, bf16[4,2,256]{2,1,0:T(2,128)(2,1)S(1)}, u32[]{:S(2)}, u32[]{:S(2)}) collective-permute-start(bf16[4,2,256]{2,1,0:T(2,128)(2,1)S(1)} %slice_bitcast_fusion), channel_id=1, source_target_pairs={{0,17},{1,16},{2,19},{3,18},{4,21},{5,20},{6,23},{7,22},{8,25},{9,... | collective-permute-start | bytes 12296 | tf_op jit(solution)/shard_map/ppermute | solution.py:314

commit v5 on v4

--- a/solution.py
+++ b/solution.py
@@ -175,6 +175,19 @@
             phase[h + g] = (at + f * (after - at)) * scale
 
 
+def pick_lanes(values, column):
+    inside = column & (LANES - 1)
+    picked = None
+    for first in range(0, values.shape[1], LANES):
+        tile = values[:, first : first + LANES]
+        spare = LANES - tile.shape[1]
+        if spare:
+            tile = jnp.concatenate([tile, jnp.zeros((tile.shape[0], spare), tile.dtype)], 1)
+        found = jnp.take_along_axis(tile, inside, axis=1, mode="promise_in_bounds")
+        picked = found if picked is None else jnp.where(column >= first, found, picked)
+    return picked
+
+
 def psi_weights(width):
     shape = (2 * ROWS, width)
     lane = lax.broadcasted_iota(jnp.int32, shape, 1) & (NPSI - 1)
@@ -212,19 +225,13 @@
 def rows_kernel(beam_own, beam_other, sky, w, near, weights, out):
     cycles = w.shape[0] // MPRIME
     total = near[...] + multipole_sum(1, (beam_own, beam_other), sky, w)
-    line = lax.broadcasted_iota(jnp.int32, total.shape, 0)
-    column = lax.broadcasted_iota(jnp.int32, total.shape, 1)
-    kept = jnp.where(lax.rem(line, ROWS) == lax.div(column, cycles), total, 0.0)
-    wide = (w.shape[0], weights.shape[2])
-    spread = (
-        lax.rem(lax.broadcasted_iota(jnp.int32, wide, 0), cycles)
-        == lax.div(lax.broadcasted_iota(jnp.int32, wide, 1), NPSI)
-    ).astype(jnp.bfloat16)
-    coeff = jnp.zeros((total.shape[0], wide[1]), jnp.float32)
-    for _ in range(3):
-        piece = kept.astype(jnp.bfloat16)
-        kept = kept - piece.astype(jnp.float32)
-        coeff += jnp.dot(piece, spread, preferred_element_type=jnp.float32)
+    shape = (total.shape[0], weights.shape[2])
+    order = lax.rem(lax.broadcasted_iota(jnp.int32, shape, 0), ROWS)
+    cycle = lax.div(lax.broadcasted_iota(jnp.int32, shape, 1), NPSI)
+    column = jnp.minimum(order, MPRIME - 1) * cycles + cycle
+    coeff = jnp.concatenate(
+        [pick_lanes(total, column[:, t : t + LANES]) for t in range(0, shape[1], LANES)], 1
+    )
     for side in range(2):
         held = coeff[side * 2 * ROWS : (side + 1) * 2 * ROWS]
         for s in range(2):
@@ -232,18 +239,9 @@
 
 
 def half_sum(part, phase, low, high, frac, g):
-    tiles = [part[:, t : t + LANES] for t in range(0, part.shape[1], LANES)]
-
-    def pick(index):
-        index = jnp.broadcast_to(index, (part.shape[0], LANES))
-        inside = index & (LANES - 1)
-        value = None
-        for t, tile in enumerate(tiles):
-            found = jnp.take_along_axis(tile, inside, axis=1, mode="promise_in_bounds")
-            value = found if value is None else jnp.where(index >= t * LANES, found, value)
-        return value
-
-    at_low, at_high = pick(low[g : g + 1, :]), pick(high[g : g + 1, :])
+    shape = (part.shape[0], LANES)
+    at_low = pick_lanes(part, jnp.broadcast_to(low[g : g + 1, :], shape))
+    at_high = pick_lanes(part, jnp.broadcast_to(high[g : g + 1, :], shape))
     return (at_low + frac[1, g : g + 1, :] * (at_high - at_low)) * phase[g]
 
 

time: 20.9 us -> 20.9 us (level)
  no operation moved by 1% of the time
where the time goes in v5:
time: 20.9 us; the launch traced here: 20.6 us
  starting transfers between devices  8.97 us (43%)
  waiting for transfers between devices  4.12 us (20%)
  local copies, waits for them, and re-layouts  4.06 us (19%)
  Pallas kernels  2.85 us (14%)
  other arithmetic  0.42 us (2%)
    ppermute x7, starting transfers between devices, swap(): return lax.ppermute(x, ('band', 'det'), pairs)  8.97 us
    ppermute x7, waiting for transfers between devices, swap(): return lax.ppermute(x, ('band', 'det'), pairs)  4.12 us
    unnamed x20, local copies, waits for them, and re-layouts  3.18 us
    pallas_call x1, Pallas kernels, by_samples(): call(second_half_kernel, jax.ShapeDtypeStruct((groups, LANES), f32), [vme...  1 us
    broadcast_in_dim x6, local copies, waits for them, and re-layouts, by_samples(): jnp.broadcast_to(turns.reshape(2, bands // 2, 1, 1), (2, bands // 2, 2, L...  0.45 us
  transfers between devices with their start and end apart: 7, of which 5 were waited for; matrix products, arithmetic and copies ran while one was open for 6% of the time, Pallas kernels for 7%

profile of v5, /device:TPU:0, one launch (start us, length us, event | category | flops | bytes accessed | tf_op | source)
XLA Modules:
  0.0 20.6 jit_solution(6083092499659702009)
XLA Ops:
  0.0 0.5 %collective-permute-start = (bf16[3,17,2,2048]{3,2,1,0:T(2,128)(2,1)}, bf16[3,17,2,2048]{3,2,1,0:T(2,128)(2,1)S(1)}, u32[]{:S(2)}, u32[]{:S(2)}) collective-permute-start(bf16[3,17,2,2048]{3,2,1,0:T(2,128)(2,1)} %bitcast.28), channel_id=1, source_target_pairs={{0,1},{1,0},{2,3},{3,2},{4,5},{5,4},{6,7},{7,6},{8,9},{9,8},{10,11... | collective-permute-start | bytes 1253384 | tf_op jit(solution)/shard_map/ppermute | solution.py:312
  0.5 2.5 %collective-permute-start.2 = (bf16[136,512]{1,0:T(8,128)(2,1)}, bf16[136,512]{1,0:T(8,128)(2,1)S(1)}, u32[]{:S(2)}, u32[]{:S(2)}) collective-permute-start(bf16[136,512]{1,0:T(8,128)(2,1)} %bitcast.30), channel_id=1, source_target_pairs={{0,2},{1,3},{2,0},{3,1},{4,6},{5,7},{6,4},{7,5},{8,10},{9,11},{10,... | collective-permute-start | bytes 417800 | tf_op jit(solution)/shard_map/ppermute | solution.py:312
  2.9 0.1 collective-permute-start.1
  3.0 1.0 %copy-done.1 = bf16[1,3,2,17,2048]{4,2,3,1,0:T(2,128)(2,1)S(1)} copy-done((bf16[1,3,2,17,2048]{4,2,3,1,0:T(2,128)(2,1)S(1)}, bf16[1,3,2,17,2048]{4,2,3,1,0:T(2,128)(2,1)}, u32[]{:S(2)}) %copy-start.1) | copy-done | bytes 417816
  4.0 0.1 shard_map.100.beam_own
  4.2 0.0 copy-start.7
  4.2 0.7 %copy-done.7 = s32[1,8,8,2]{2,3,1,0:T(2,128)S(1)} copy-done((s32[1,8,8,2]{2,3,1,0:T(2,128)S(1)}, s32[1,8,8,2]{2,3,1,0:T(2,128)}, u32[]{:S(2)}) %copy-start.7) | copy-done | bytes 536
  4.9 0.1 fusion
  5.0 0.1 copy.29
  5.1 0.1 reduce_sum.31
  5.2 0.6 %copy-done.9 = s32[8]{0:T(128)S(1)} copy-done((s32[8]{0:T(128)S(1)}, s32[8]{0:T(128)}, u32[]{:S(2)}) %copy-start.9) | copy-done | bytes 56
  5.8 0.2 select_reduce_fusion
  5.9 0.1 fusion.3
  6.0 0.0 copy-start.6
  6.0 0.0 collective-permute-done.source
  6.1 0.1 shard_map.101.beam_other
  6.2 0.7 %copy-done.2 = bf16[1,17,512,8]{2,3,1,0:T(8,128)(2,1)S(1)} copy-done((bf16[1,17,512,8]{2,3,1,0:T(8,128)(2,1)S(1)}, bf16[1,17,512,8]{2,3,1,0:T(8,128)(2,1)}, u32[]{:S(2)}) %copy-start.2) | copy-done | bytes 139288
  6.9 0.0 copy-done.6
  6.9 0.2 %shard_map.102 = (f32[96,136]{1,0:T(8,128)S(1)}, f32[2,48,256]{2,1,0:T(8,128)S(1)}) custom-call(f32[3,2,24,1024]{3,2,1,0:T(8,128)S(1)} %shard_map.100.beam_own, f32[3,2,24,1024]{3,2,1,0:T(8,128)S(1)} %shard_map.101.beam_other, f32[3,2,1,512]{3,2,1,0:T(1,128)S(1)} %copy-done.6, bf16[136,512]{1,0:T(8,128)(2,1)S(1)} %bitcast.31), custom_call_target="tpu_custom_call" | custom-call | flops 1 | bytes 1 | tf_op jit(solution)/shard_map/pallas_call | solution.py:322
  7.2 0.6 %collective-permute-done.1.sky = f32[3,2,1,512]{3,2,1,0:T(1,128)S(1)} collective-permute-done((f32[3,2,1,512]{3,2,1,0:T(1,128)}, f32[3,2,1,512]{3,2,1,0:T(1,128)S(1)}, u32[]{:S(2)}, u32[]{:S(2)}) %collective-permute-start.1) | collective-permute-done | bytes 12320 | tf_op jit(solution)/shard_map/ppermute | solution.py:312
  7.8 0.0 collective-permute-done.2.w
  7.8 0.0 copy-start.5
  7.8 0.4 %shard_map.103 = f32[2,2,256]{2,1,0:T(2,128)S(1)} custom-call(f32[3,2,24,1024]{3,2,1,0:T(8,128)S(1)} %shard_map.100.beam_own, f32[3,2,24,1024]{3,2,1,0:T(8,128)S(1)} %shard_map.101.beam_other, f32[3,2,1,512]{3,2,1,0:T(1,128)S(1)} %collective-permute-done.1.sky, bf16[136,512]{1,0:T(8,128)(2,1)S(1)} %collective-permute-done.2.w, ...), custom_call_target="tpu_custom_call" | custom-call | flops 1 | bytes 1 | tf_op jit(solution)/shard_map/pallas_call | solution.py:330
  8.2 0.0 copy-start
  8.2 0.1 collective-permute-start.3
  8.3 0.2 copy-done.8
  8.5 0.1 copy.30
  8.5 0.1 stack.17
  8.6 0.8 %collective-permute-done.3 = f32[2,2,256]{2,1,0:T(2,128)S(1)} collective-permute-done((f32[2,2,256]{2,1,0:T(2,128)S(1)}, f32[2,2,256]{2,1,0:T(2,128)S(1)}, u32[]{:S(2)}, u32[]{:S(2)}) %collective-permute-start.3) | collective-permute-done | bytes 4128 | tf_op jit(solution)/shard_map/ppermute | solution.py:312
  9.4 1.5 %collective-permute-start.4 = (bf16[2,2,256]{2,1,0:T(2,128)(2,1)S(1)}, bf16[2,2,256]{2,1,0:T(2,128)(2,1)S(1)}, u32[]{:S(2)}, u32[]{:S(2)}) collective-permute-start(bf16[2,2,256]{2,1,0:T(2,128)(2,1)S(1)} %add_convert_fusion), channel_id=1, source_target_pairs={{0,5},{1,4},{2,7},{3,6},{4,1},{5,0},{6,3},{7,2},{8,13},{9,12},{10,... | collective-permute-start | bytes 6152 | tf_op jit(solution)/shard_map/ppermute | solution.py:312
  11.0 0.1 broadcast_in_dim.41
  11.0 0.1 broadcast_in_dim.42
  11.1 0.1 broadcast_in_dim.43.turns
  11.2 0.0 copy-done.3
  11.2 0.0 copy-done.4
  11.2 0.0 copy-done.5
  11.2 0.3 %shard_map.104 = (f32[32,8,128]{2,1,0:T(8,128)S(1)}, s32[32,128]{1,0:T(8,128)S(1)}, s32[32,128]{1,0:T(8,128)S(1)}) custom-call(f32[8,128]{1,0:T(8,128)S(1)} %broadcast_in_dim.43.turns, s32[2,128]{1,0:T(2,128)S(1)} %pad.4.table, s32[32,128]{1,0:T(8,128)S(1)} %bitcast.32, s32[32,128]{1,0:T(8,128)S(1)} %bitcast.34, s32[32,128]{1,0:T(8,128)S(1)} %bitcast.36, ...), custom_call_target="tpu_custom_call" | custom-call | flops 1 | bytes 1 | tf_op jit(solution)/shard_map/pallas_call | solution.py:352
  11.5 0.9 %collective-permute-done.4 = bf16[2,2,256]{2,1,0:T(2,128)(2,1)S(1)} collective-permute-done((bf16[2,2,256]{2,1,0:T(2,128)(2,1)S(1)}, bf16[2,2,256]{2,1,0:T(2,128)(2,1)S(1)}, u32[]{:S(2)}, u32[]{:S(2)}) %collective-permute-start.4) | collective-permute-done | bytes 2080 | tf_op jit(solution)/shard_map/ppermute | solution.py:312
  12.4 1.7 %collective-permute-start.5 = (bf16[2,2,2,256]{3,2,0,1:T(2,128)(2,1)S(1)}, bf16[2,2,2,256]{3,2,0,1:T(2,128)(2,1)S(1)}, u32[]{:S(2)}, u32[]{:S(2)}) collective-permute-start(bf16[2,2,2,256]{3,2,0,1:T(2,128)(2,1)S(1)} %pad_maximum_fusion.1), channel_id=1, source_target_pairs={{0,9},{1,8},{2,11},{3,10},{4,13},{5,12},{6,15},{7,14},{8,1},{9,0},... | collective-permute-start | bytes 12296 | tf_op jit(solution)/shard_map/ppermute | solution.py:312
  14.1 0.1 broadcast_in_dim.46
  14.2 0.1 broadcast_in_dim.47
  14.3 0.1 broadcast_in_dim.48.turns
  14.3 0.3 %shard_map.105.phase = f32[32,8,128]{2,1,0:T(8,128)S(1)} custom-call(f32[8,128]{1,0:T(8,128)S(1)} %broadcast_in_dim.48.turns, s32[2,128]{1,0:T(2,128)S(1)} %pad.4.table, s32[32,128]{1,0:T(8,128)S(1)} %bitcast.33, s32[32,128]{1,0:T(8,128)S(1)} %bitcast.35, s32[32,128]{1,0:T(8,128)S(1)} %bitcast.37, f32[2,32,128]{2,1,0:T(8,128)S(1)} %bitcast.25), custom_call_target="tpu_custom_call" | custom-call | flops 1 | bytes 1 | tf_op jit(solution)/shard_map/pallas_call | solution.py:359
  14.6 0.9 %collective-permute-done.5 = bf16[2,2,2,256]{3,2,0,1:T(2,128)(2,1)S(1)} collective-permute-done((bf16[2,2,2,256]{3,2,0,1:T(2,128)(2,1)S(1)}, bf16[2,2,2,256]{3,2,0,1:T(2,128)(2,1)S(1)}, u32[]{:S(2)}, u32[]{:S(2)}) %collective-permute-start.5) | collective-permute-done | bytes 4128 | tf_op jit(solution)/shard_map/ppermute | solution.py:312
  15.6 2.7 %collective-permute-start.6 = (bf16[4,2,256]{2,1,0:T(2,128)(2,1)S(1)}, bf16[4,2,256]{2,1,0:T(2,128)(2,1)S(1)}, u32[]{:S(2)}, u32[]{:S(2)}) collective-permute-start(bf16[4,2,256]{2,1,0:T(2,128)(2,1)S(1)} %slice_bitcast_fusion), channel_id=1, source_target_pairs={{0,17},{1,16},{2,19},{3,18},{4,21},{5,20},{6,23},{7,22},{8,25},{9,... | collective-permute-start | bytes 12296 | tf_op jit(solution)/shard_map/ppermute | solution.py:312
  18.3 0.4 %shard_map.106.first = f32[32,8,128]{2,1,0:T(8,128)S(1)} custom-call(bf16[4,2,2,256]{3,2,1,0:T(2,128)(2,1)S(1)} %copy.33.held, f32[32,8,128]{2,1,0:T(8,128)S(1)} %get-tuple-element.23.phase, s32[32,128]{1,0:T(8,128)S(1)} %get-tuple-element.24.low, s32[32,128]{1,0:T(8,128)S(1)} %get-tuple-element.25.high, f32[2,32,128]{2,1,0:T(8,128)S(1)} %bitcast.26), custom_call_target="tpu_custom_call" | custom-call | flops 1 | bytes 1 | tf_op jit(solution)/shard_map/pallas_call | solution.py:363
  18.7 0.9 %collective-permute-done.6.received = bf16[4,2,256]{2,1,0:T(2,128)(2,1)S(1)} collective-permute-done((bf16[4,2,256]{2,1,0:T(2,128)(2,1)S(1)}, bf16[4,2,256]{2,1,0:T(2,128)(2,1)S(1)}, u32[]{:S(2)}, u32[]{:S(2)}) %collective-permute-start.6) | collective-permute-done | bytes 4128 | tf_op jit(solution)/shard_map/ppermute | solution.py:312
  19.6 1.0 %shard_map.107 = f32[32,128]{1,0:T(8,128)} custom-call(bf16[4,2,256]{2,1,0:T(2,128)(2,1)S(1)} %collective-permute-done.6.received, f32[32,8,128]{2,1,0:T(8,128)S(1)} %shard_map.106.first, f32[32,8,128]{2,1,0:T(8,128)S(1)} %shard_map.105.phase, s32[32,128]{1,0:T(8,128)S(1)} %get-tuple-element.24.low, s32[32,128]{1,0:T(8,128)S(1)} %get-tuple-element.25.high, ...), custom_call_target="tpu_custom_call" | custom-call | flops 1 | bytes 1 | tf_op jit(solution)/shard_map/pallas_call | solution.py:364
  (22 shorter events, 0.1 us)
Async XLA Ops:
  0.0 6.1 %collective-permute-start = (bf16[3,17,2,2048]{3,2,1,0:T(2,128)(2,1)}, bf16[3,17,2,2048]{3,2,1,0:T(2,128)(2,1)S(1)}, u32[]{:S(2)}, u32[]{:S(2)}) collective-permute-start(bf16[3,17,2,2048]{3,2,1,0:T(2,128)(2,1)} %bitcast.28), channel_id=1, source_target_pairs={{0,1},{1,0},{2,3},{3,2},{4,5},{5,4},{6,7},{7,6},{8,9},{9,8},{10,11... | collective-permute-start | bytes 1253384 | tf_op jit(solution)/shard_map/ppermute | solution.py:312
  0.5 7.3 %collective-permute-start.2 = (bf16[136,512]{1,0:T(8,128)(2,1)}, bf16[136,512]{1,0:T(8,128)(2,1)S(1)}, u32[]{:S(2)}, u32[]{:S(2)}) collective-permute-start(bf16[136,512]{1,0:T(8,128)(2,1)} %bitcast.30), channel_id=1, source_target_pairs={{0,2},{1,3},{2,0},{3,1},{4,6},{5,7},{6,4},{7,5},{8,10},{9,11},{10,... | collective-permute-start | bytes 417800 | tf_op jit(solution)/shard_map/ppermute | solution.py:312
  2.9 4.8 %collective-permute-start.1 = (f32[3,2,1,512]{3,2,1,0:T(1,128)}, f32[3,2,1,512]{3,2,1,0:T(1,128)S(1)}, u32[]{:S(2)}, u32[]{:S(2)}) collective-permute-start(f32[3,2,1,512]{3,2,1,0:T(1,128)} %sky.1), channel_id=1, source_target_pairs={{0,2},{1,3},{2,0},{3,1},{4,6},{5,7},{6,4},{7,5},{8,10},{9,11},{10,... | collective-permute-start | bytes 36872 | tf_op jit(solution)/shard_map/ppermute | solution.py:312
  3.0 1.0 %copy-start.1 = (bf16[1,3,2,17,2048]{4,2,3,1,0:T(2,128)(2,1)S(1)}, bf16[1,3,2,17,2048]{4,2,3,1,0:T(2,128)(2,1)}, u32[]{:S(2)}) copy-start(bf16[1,3,2,17,2048]{4,2,3,1,0:T(2,128)(2,1)} %param.11) | copy-start | bytes 1253380
  4.2 0.7 %copy-start.7 = (s32[1,8,8,2]{2,3,1,0:T(2,128)S(1)}, s32[1,8,8,2]{2,3,1,0:T(2,128)}, u32[]{:S(2)}) copy-start(s32[1,8,8,2]{2,3,1,0:T(2,128)} %param.15) | copy-start | bytes 1540
  5.1 0.7 %copy-start.9 = (s32[8]{0:T(128)S(1)}, s32[8]{0:T(128)}, u32[]{:S(2)}) copy-start(s32[8]{0:T(128)} %param.13) | copy-start | bytes 100
  6.0 0.9 %copy-start.2 = (bf16[1,17,512,8]{2,3,1,0:T(8,128)(2,1)S(1)}, bf16[1,17,512,8]{2,3,1,0:T(8,128)(2,1)}, u32[]{:S(2)}) copy-start(bf16[1,17,512,8]{2,3,1,0:T(8,128)(2,1)} %param.12) | copy-start | bytes 417796
  6.0 0.9 %copy-start.6 = (f32[3,2,1,512]{3,2,1,0:T(1,128)S(1)}, f32[3,2,1,512]{3,2,1,0:T(1,128)}, u32[]{:S(2)}) copy-start(f32[3,2,1,512]{3,2,1,0:T(1,128)} %sky.1) | copy-start | bytes 36868
  7.8 0.7 %copy-start.8 = (s32[8,3]{0,1:T(4,128)S(1)}, s32[8,3]{0,1:T(4,128)}, u32[]{:S(2)}) copy-start(s32[8,3]{0,1:T(4,128)} %param.14) | copy-start | bytes 292
  7.8 3.4 %copy-start.3 = (s32[1,4096]{1,0:T(1,128)S(1)}, s32[1,4096]{1,0:T(1,128)}, u32[]{:S(2)}) copy-start(s32[1,4096]{1,0:T(1,128)} %param.16) | copy-start | bytes 49156
  7.8 3.4 %copy-start.4 = (s32[1,4096]{1,0:T(1,128)S(1)}, s32[1,4096]{1,0:T(1,128)}, u32[]{:S(2)}) copy-start(s32[1,4096]{1,0:T(1,128)} %param.17) | copy-start | bytes 49156
  7.8 3.4 %copy-start.5 = (s32[1,4096]{1,0:T(1,128)S(1)}, s32[1,4096]{1,0:T(1,128)}, u32[]{:S(2)}) copy-start(s32[1,4096]{1,0:T(1,128)} %param.18) | copy-start | bytes 49156
  8.2 3.0 %copy-start = (f32[2,1,4096]{2,1,0:T(1,128)S(1)}, f32[2,1,4096]{2,1,0:T(1,128)}, u32[]{:S(2)}) copy-start(f32[2,1,4096]{2,1,0:T(1,128)} %param.19) | copy-start | bytes 98308
  8.2 1.2 %collective-permute-start.3 = (f32[2,2,256]{2,1,0:T(2,128)S(1)}, f32[2,2,256]{2,1,0:T(2,128)S(1)}, u32[]{:S(2)}, u32[]{:S(2)}) collective-permute-start(f32[2,2,256]{2,1,0:T(2,128)S(1)} %shard_map.103), channel_id=1, source_target_pairs={{0,1},{1,0},{2,3},{3,2},{4,5},{5,4},{6,7},{7,6},{8,9},{9,8},{10,11... | collective-permute-start | bytes 12296 | tf_op jit(solution)/shard_map/ppermute | solution.py:312
  9.4 3.0 %collective-permute-start.4 = (bf16[2,2,256]{2,1,0:T(2,128)(2,1)S(1)}, bf16[2,2,256]{2,1,0:T(2,128)(2,1)S(1)}, u32[]{:S(2)}, u32[]{:S(2)}) collective-permute-start(bf16[2,2,256]{2,1,0:T(2,128)(2,1)S(1)} %add_convert_fusion), channel_id=1, source_target_pairs={{0,5},{1,4},{2,7},{3,6},{4,1},{5,0},{6,3},{7,2},{8,13},{9,12},{10,... | collective-permute-start | bytes 6152 | tf_op jit(solution)/shard_map/ppermute | solution.py:312
  12.4 3.1 %collective-permute-start.5 = (bf16[2,2,2,256]{3,2,0,1:T(2,128)(2,1)S(1)}, bf16[2,2,2,256]{3,2,0,1:T(2,128)(2,1)S(1)}, u32[]{:S(2)}, u32[]{:S(2)}) collective-permute-start(bf16[2,2,2,256]{3,2,0,1:T(2,128)(2,1)S(1)} %pad_maximum_fusion.1), channel_id=1, source_target_pairs={{0,9},{1,8},{2,11},{3,10},{4,13},{5,12},{6,15},{7,14},{8,1},{9,0},... | collective-permute-start | bytes 12296 | tf_op jit(solution)/shard_map/ppermute | solution.py:312
  15.6 4.0 %collective-permute-start.6 = (bf16[4,2,256]{2,1,0:T(2,128)(2,1)S(1)}, bf16[4,2,256]{2,1,0:T(2,128)(2,1)S(1)}, u32[]{:S(2)}, u32[]{:S(2)}) collective-permute-start(bf16[4,2,256]{2,1,0:T(2,128)(2,1)S(1)} %slice_bitcast_fusion), channel_id=1, source_target_pairs={{0,17},{1,16},{2,19},{3,18},{4,21},{5,20},{6,23},{7,22},{8,25},{9,... | collective-permute-start | bytes 12296 | tf_op jit(solution)/shard_map/ppermute | solution.py:312

commit v6 on v5

--- a/solution.py
+++ b/solution.py
@@ -141,7 +141,7 @@
     chunk = out.shape[3] // 2
     det = lax.axis_index("det")
     for part in range(2):
-        owner = det ^ (2 * part)
+        owner = det ^ (3 * part)
         lanes = pl.ds(pl.multiple_of(owner * chunk, chunk), chunk)
         for c in range(out.shape[0]):
             block = source[c, :, :, lanes].astype(jnp.float32)
@@ -312,8 +312,8 @@
         return lax.ppermute(x, ("band", "det"), pairs)
 
     panel = jnp.transpose(wigner_panel[0], (0, 2, 1)).reshape(MPRIME * cycles, chunk)
-    panel_other = swap(panel, 0, 2)
-    sky_other = swap(sky_coeffs, 0, 2)
+    panel_other = swap(panel, 0, 3)
+    sky_other = swap(sky_coeffs, 0, 3)
     beam = jnp.transpose(beam_coeffs[0], (0, 2, 1, 3))
     beam_other = swap(beam, 0, 1)
     split = jax.ShapeDtypeStruct((beam.shape[0], 2, ROWS, 2 * chunk), f32)

time: 20.9 us -> 20.7 us (level)
  no operation moved by 1% of the time
where the time goes in v6:
time: 20.7 us; the launch traced here: 20.4 us
  starting transfers between devices  8.89 us (43%)
  waiting for transfers between devices  4.11 us (20%)
  local copies, waits for them, and re-layouts  3.96 us (19%)
  Pallas kernels  2.86 us (14%)
  other arithmetic  0.42 us (2%)
    ppermute x7, starting transfers between devices, swap(): return lax.ppermute(x, ('band', 'det'), pairs)  8.89 us
    ppermute x7, waiting for transfers between devices, swap(): return lax.ppermute(x, ('band', 'det'), pairs)  4.11 us
    unnamed x20, local copies, waits for them, and re-layouts  3.08 us
    pallas_call x1, Pallas kernels, by_samples(): call(second_half_kernel, jax.ShapeDtypeStruct((groups, LANES), f32), [vme...  1 us
    broadcast_in_dim x6, local copies, waits for them, and re-layouts, by_samples(): jnp.broadcast_to(turns.reshape(2, bands // 2, 1, 1), (2, bands // 2, 2, L...  0.45 us
  transfers between devices with their start and end apart: 7, of which 5 were waited for; matrix products, arithmetic and copies ran while one was open for 6% of the time, Pallas kernels for 7%

profile of v6, /device:TPU:0, one launch (start us, length us, event | category | flops | bytes accessed | tf_op | source)
XLA Modules:
  0.0 20.4 jit_solution(16615211213822869366)
XLA Ops:
  0.0 0.5 %collective-permute-start = (bf16[3,17,2,2048]{3,2,1,0:T(2,128)(2,1)}, bf16[3,17,2,2048]{3,2,1,0:T(2,128)(2,1)S(1)}, u32[]{:S(2)}, u32[]{:S(2)}) collective-permute-start(bf16[3,17,2,2048]{3,2,1,0:T(2,128)(2,1)} %bitcast.28), channel_id=1, source_target_pairs={{0,1},{1,0},{2,3},{3,2},{4,5},{5,4},{6,7},{7,6},{8,9},{9,8},{10,11... | collective-permute-start | bytes 1253384 | tf_op jit(solution)/shard_map/ppermute | solution.py:312
  0.5 2.6 %collective-permute-start.2 = (bf16[136,512]{1,0:T(8,128)(2,1)}, bf16[136,512]{1,0:T(8,128)(2,1)S(1)}, u32[]{:S(2)}, u32[]{:S(2)}) collective-permute-start(bf16[136,512]{1,0:T(8,128)(2,1)} %bitcast.30), channel_id=1, source_target_pairs={{0,3},{1,2},{2,1},{3,0},{4,7},{5,6},{6,5},{7,4},{8,11},{9,10},{10,... | collective-permute-start | bytes 417800 | tf_op jit(solution)/shard_map/ppermute | solution.py:312
  3.1 0.0 collective-permute-start.1
  3.1 1.0 %copy-done.1 = bf16[1,3,2,17,2048]{4,2,3,1,0:T(2,128)(2,1)S(1)} copy-done((bf16[1,3,2,17,2048]{4,2,3,1,0:T(2,128)(2,1)S(1)}, bf16[1,3,2,17,2048]{4,2,3,1,0:T(2,128)(2,1)}, u32[]{:S(2)}) %copy-start.1) | copy-done | bytes 417816
  4.1 0.1 shard_map.100.beam_own
  4.2 0.0 copy-start.7
  4.3 0.7 %copy-done.7 = s32[1,8,8,2]{2,3,1,0:T(2,128)S(1)} copy-done((s32[1,8,8,2]{2,3,1,0:T(2,128)S(1)}, s32[1,8,8,2]{2,3,1,0:T(2,128)}, u32[]{:S(2)}) %copy-start.7) | copy-done | bytes 536
  4.9 0.1 fusion
  5.1 0.1 copy.29
  5.2 0.1 reduce_sum.31
  5.2 0.6 %copy-done.9 = s32[8]{0:T(128)S(1)} copy-done((s32[8]{0:T(128)S(1)}, s32[8]{0:T(128)}, u32[]{:S(2)}) %copy-start.9) | copy-done | bytes 56
  5.8 0.2 select_reduce_fusion
  6.0 0.1 fusion.3
  6.1 0.0 copy-start.6
  6.1 0.0 collective-permute-done.source
  6.1 0.1 shard_map.101.beam_other
  6.3 0.7 %copy-done.2 = bf16[1,17,512,8]{2,3,1,0:T(8,128)(2,1)S(1)} copy-done((bf16[1,17,512,8]{2,3,1,0:T(8,128)(2,1)S(1)}, bf16[1,17,512,8]{2,3,1,0:T(8,128)(2,1)}, u32[]{:S(2)}) %copy-start.2) | copy-done | bytes 139288
  7.0 0.0 copy-done.6
  7.0 0.2 %shard_map.102 = (f32[96,136]{1,0:T(8,128)S(1)}, f32[2,48,256]{2,1,0:T(8,128)S(1)}) custom-call(f32[3,2,24,1024]{3,2,1,0:T(8,128)S(1)} %shard_map.100.beam_own, f32[3,2,24,1024]{3,2,1,0:T(8,128)S(1)} %shard_map.101.beam_other, f32[3,2,1,512]{3,2,1,0:T(1,128)S(1)} %copy-done.6, bf16[136,512]{1,0:T(8,128)(2,1)S(1)} %bitcast.31), custom_call_target="tpu_custom_call" | custom-call | flops 1 | bytes 1 | tf_op jit(solution)/shard_map/pallas_call | solution.py:322
  7.2 0.3 %collective-permute-done.1.sky = f32[3,2,1,512]{3,2,1,0:T(1,128)S(1)} collective-permute-done((f32[3,2,1,512]{3,2,1,0:T(1,128)}, f32[3,2,1,512]{3,2,1,0:T(1,128)S(1)}, u32[]{:S(2)}, u32[]{:S(2)}) %collective-permute-start.1) | collective-permute-done | bytes 12320 | tf_op jit(solution)/shard_map/ppermute | solution.py:312
  7.6 0.0 collective-permute-done.2.w
  7.6 0.0 copy-start.5
  7.6 0.4 %shard_map.103 = f32[2,2,256]{2,1,0:T(2,128)S(1)} custom-call(f32[3,2,24,1024]{3,2,1,0:T(8,128)S(1)} %shard_map.100.beam_own, f32[3,2,24,1024]{3,2,1,0:T(8,128)S(1)} %shard_map.101.beam_other, f32[3,2,1,512]{3,2,1,0:T(1,128)S(1)} %collective-permute-done.1.sky, bf16[136,512]{1,0:T(8,128)(2,1)S(1)} %collective-permute-done.2.w, ...), custom_call_target="tpu_custom_call" | custom-call | flops 1 | bytes 1 | tf_op jit(solution)/shard_map/pallas_call | solution.py:330
  8.0 0.0 copy-start
  8.0 0.2 collective-permute-start.3
  8.2 0.1 copy-done.8
  8.3 0.1 copy.30
  8.4 0.1 stack.17
  8.4 0.8 %collective-permute-done.3 = f32[2,2,256]{2,1,0:T(2,128)S(1)} collective-permute-done((f32[2,2,256]{2,1,0:T(2,128)S(1)}, f32[2,2,256]{2,1,0:T(2,128)S(1)}, u32[]{:S(2)}, u32[]{:S(2)}) %collective-permute-start.3) | collective-permute-done | bytes 4128 | tf_op jit(solution)/shard_map/ppermute | solution.py:312
  9.2 1.5 %collective-permute-start.4 = (bf16[2,2,256]{2,1,0:T(2,128)(2,1)S(1)}, bf16[2,2,256]{2,1,0:T(2,128)(2,1)S(1)}, u32[]{:S(2)}, u32[]{:S(2)}) collective-permute-start(bf16[2,2,256]{2,1,0:T(2,128)(2,1)S(1)} %add_convert_fusion), channel_id=1, source_target_pairs={{0,5},{1,4},{2,7},{3,6},{4,1},{5,0},{6,3},{7,2},{8,13},{9,12},{10,... | collective-permute-start | bytes 6152 | tf_op jit(solution)/shard_map/ppermute | solution.py:312
  10.7 0.1 broadcast_in_dim.41
  10.8 0.1 broadcast_in_dim.42
  10.8 0.1 broadcast_in_dim.43.turns
  10.9 0.0 copy-done.3
  10.9 0.0 copy-done.4
  10.9 0.0 copy-done.5
  10.9 0.3 %shard_map.104 = (f32[32,8,128]{2,1,0:T(8,128)S(1)}, s32[32,128]{1,0:T(8,128)S(1)}, s32[32,128]{1,0:T(8,128)S(1)}) custom-call(f32[8,128]{1,0:T(8,128)S(1)} %broadcast_in_dim.43.turns, s32[2,128]{1,0:T(2,128)S(1)} %pad.4.table, s32[32,128]{1,0:T(8,128)S(1)} %bitcast.32, s32[32,128]{1,0:T(8,128)S(1)} %bitcast.34, s32[32,128]{1,0:T(8,128)S(1)} %bitcast.36, ...), custom_call_target="tpu_custom_call" | custom-call | flops 1 | bytes 1 | tf_op jit(solution)/shard_map/pallas_call | solution.py:352
  11.2 1.0 %collective-permute-done.4 = bf16[2,2,256]{2,1,0:T(2,128)(2,1)S(1)} collective-permute-done((bf16[2,2,256]{2,1,0:T(2,128)(2,1)S(1)}, bf16[2,2,256]{2,1,0:T(2,128)(2,1)S(1)}, u32[]{:S(2)}, u32[]{:S(2)}) %collective-permute-start.4) | collective-permute-done | bytes 2080 | tf_op jit(solution)/shard_map/ppermute | solution.py:312
  12.3 1.6 %collective-permute-start.5 = (bf16[2,2,2,256]{3,2,0,1:T(2,128)(2,1)S(1)}, bf16[2,2,2,256]{3,2,0,1:T(2,128)(2,1)S(1)}, u32[]{:S(2)}, u32[]{:S(2)}) collective-permute-start(bf16[2,2,2,256]{3,2,0,1:T(2,128)(2,1)S(1)} %pad_maximum_fusion.1), channel_id=1, source_target_pairs={{0,9},{1,8},{2,11},{3,10},{4,13},{5,12},{6,15},{7,14},{8,1},{9,0},... | collective-permute-start | bytes 12296 | tf_op jit(solution)/shard_map/ppermute | solution.py:312
  13.8 0.1 broadcast_in_dim.46
  13.9 0.1 broadcast_in_dim.47
  14.0 0.1 broadcast_in_dim.48.turns
  14.1 0.3 %shard_map.105.phase = f32[32,8,128]{2,1,0:T(8,128)S(1)} custom-call(f32[8,128]{1,0:T(8,128)S(1)} %broadcast_in_dim.48.turns, s32[2,128]{1,0:T(2,128)S(1)} %pad.4.table, s32[32,128]{1,0:T(8,128)S(1)} %bitcast.33, s32[32,128]{1,0:T(8,128)S(1)} %bitcast.35, s32[32,128]{1,0:T(8,128)S(1)} %bitcast.37, f32[2,32,128]{2,1,0:T(8,128)S(1)} %bitcast.25), custom_call_target="tpu_custom_call" | custom-call | flops 1 | bytes 1 | tf_op jit(solution)/shard_map/pallas_call | solution.py:359
  14.4 1.0 %collective-permute-done.5 = bf16[2,2,2,256]{3,2,0,1:T(2,128)(2,1)S(1)} collective-permute-done((bf16[2,2,2,256]{3,2,0,1:T(2,128)(2,1)S(1)}, bf16[2,2,2,256]{3,2,0,1:T(2,128)(2,1)S(1)}, u32[]{:S(2)}, u32[]{:S(2)}) %collective-permute-start.5) | collective-permute-done | bytes 4128 | tf_op jit(solution)/shard_map/ppermute | solution.py:312
  15.4 2.6 %collective-permute-start.6 = (bf16[4,2,256]{2,1,0:T(2,128)(2,1)S(1)}, bf16[4,2,256]{2,1,0:T(2,128)(2,1)S(1)}, u32[]{:S(2)}, u32[]{:S(2)}) collective-permute-start(bf16[4,2,256]{2,1,0:T(2,128)(2,1)S(1)} %slice_bitcast_fusion), channel_id=1, source_target_pairs={{0,17},{1,16},{2,19},{3,18},{4,21},{5,20},{6,23},{7,22},{8,25},{9,... | collective-permute-start | bytes 12296 | tf_op jit(solution)/shard_map/ppermute | solution.py:312
  18.0 0.4 %shard_map.106.first = f32[32,8,128]{2,1,0:T(8,128)S(1)} custom-call(bf16[4,2,2,256]{3,2,1,0:T(2,128)(2,1)S(1)} %copy.33.held, f32[32,8,128]{2,1,0:T(8,128)S(1)} %get-tuple-element.23.phase, s32[32,128]{1,0:T(8,128)S(1)} %get-tuple-element.24.low, s32[32,128]{1,0:T(8,128)S(1)} %get-tuple-element.25.high, f32[2,32,128]{2,1,0:T(8,128)S(1)} %bitcast.26), custom_call_target="tpu_custom_call" | custom-call | flops 1 | bytes 1 | tf_op jit(solution)/shard_map/pallas_call | solution.py:363
  18.4 1.0 %collective-permute-done.6.received = bf16[4,2,256]{2,1,0:T(2,128)(2,1)S(1)} collective-permute-done((bf16[4,2,256]{2,1,0:T(2,128)(2,1)S(1)}, bf16[4,2,256]{2,1,0:T(2,128)(2,1)S(1)}, u32[]{:S(2)}, u32[]{:S(2)}) %collective-permute-start.6) | collective-permute-done | bytes 4128 | tf_op jit(solution)/shard_map/ppermute | solution.py:312
  19.4 1.0 %shard_map.107 = f32[32,128]{1,0:T(8,128)} custom-call(bf16[4,2,256]{2,1,0:T(2,128)(2,1)S(1)} %collective-permute-done.6.received, f32[32,8,128]{2,1,0:T(8,128)S(1)} %shard_map.106.first, f32[32,8,128]{2,1,0:T(8,128)S(1)} %shard_map.105.phase, s32[32,128]{1,0:T(8,128)S(1)} %get-tuple-element.24.low, s32[32,128]{1,0:T(8,128)S(1)} %get-tuple-element.25.high, ...), custom_call_target="tpu_custom_call" | custom-call | flops 1 | bytes 1 | tf_op jit(solution)/shard_map/pallas_call | solution.py:364
  (22 shorter events, 0.1 us)
Async XLA Ops:
  0.0 6.1 %collective-permute-start = (bf16[3,17,2,2048]{3,2,1,0:T(2,128)(2,1)}, bf16[3,17,2,2048]{3,2,1,0:T(2,128)(2,1)S(1)}, u32[]{:S(2)}, u32[]{:S(2)}) collective-permute-start(bf16[3,17,2,2048]{3,2,1,0:T(2,128)(2,1)} %bitcast.28), channel_id=1, source_target_pairs={{0,1},{1,0},{2,3},{3,2},{4,5},{5,4},{6,7},{7,6},{8,9},{9,8},{10,11... | collective-permute-start | bytes 1253384 | tf_op jit(solution)/shard_map/ppermute | solution.py:312
  0.5 7.1 %collective-permute-start.2 = (bf16[136,512]{1,0:T(8,128)(2,1)}, bf16[136,512]{1,0:T(8,128)(2,1)S(1)}, u32[]{:S(2)}, u32[]{:S(2)}) collective-permute-start(bf16[136,512]{1,0:T(8,128)(2,1)} %bitcast.30), channel_id=1, source_target_pairs={{0,3},{1,2},{2,1},{3,0},{4,7},{5,6},{6,5},{7,4},{8,11},{9,10},{10,... | collective-permute-start | bytes 417800 | tf_op jit(solution)/shard_map/ppermute | solution.py:312
  3.1 4.5 %collective-permute-start.1 = (f32[3,2,1,512]{3,2,1,0:T(1,128)}, f32[3,2,1,512]{3,2,1,0:T(1,128)S(1)}, u32[]{:S(2)}, u32[]{:S(2)}) collective-permute-start(f32[3,2,1,512]{3,2,1,0:T(1,128)} %sky.1), channel_id=1, source_target_pairs={{0,3},{1,2},{2,1},{3,0},{4,7},{5,6},{6,5},{7,4},{8,11},{9,10},{10,... | collective-permute-start | bytes 36872 | tf_op jit(solution)/shard_map/ppermute | solution.py:312
  3.1 1.0 %copy-start.1 = (bf16[1,3,2,17,2048]{4,2,3,1,0:T(2,128)(2,1)S(1)}, bf16[1,3,2,17,2048]{4,2,3,1,0:T(2,128)(2,1)}, u32[]{:S(2)}) copy-start(bf16[1,3,2,17,2048]{4,2,3,1,0:T(2,128)(2,1)} %param.11) | copy-start | bytes 1253380
  4.2 0.7 %copy-start.7 = (s32[1,8,8,2]{2,3,1,0:T(2,128)S(1)}, s32[1,8,8,2]{2,3,1,0:T(2,128)}, u32[]{:S(2)}) copy-start(s32[1,8,8,2]{2,3,1,0:T(2,128)} %param.15) | copy-start | bytes 1540
  5.2 0.7 %copy-start.9 = (s32[8]{0:T(128)S(1)}, s32[8]{0:T(128)}, u32[]{:S(2)}) copy-start(s32[8]{0:T(128)} %param.13) | copy-start | bytes 100
  6.1 0.9 %copy-start.2 = (bf16[1,17,512,8]{2,3,1,0:T(8,128)(2,1)S(1)}, bf16[1,17,512,8]{2,3,1,0:T(8,128)(2,1)}, u32[]{:S(2)}) copy-start(bf16[1,17,512,8]{2,3,1,0:T(8,128)(2,1)} %param.12) | copy-start | bytes 417796
  6.1 0.9 %copy-start.6 = (f32[3,2,1,512]{3,2,1,0:T(1,128)S(1)}, f32[3,2,1,512]{3,2,1,0:T(1,128)}, u32[]{:S(2)}) copy-start(f32[3,2,1,512]{3,2,1,0:T(1,128)} %sky.1) | copy-start | bytes 36868
  7.6 0.7 %copy-start.8 = (s32[8,3]{0,1:T(4,128)S(1)}, s32[8,3]{0,1:T(4,128)}, u32[]{:S(2)}) copy-start(s32[8,3]{0,1:T(4,128)} %param.14) | copy-start | bytes 292
  7.6 3.3 %copy-start.3 = (s32[1,4096]{1,0:T(1,128)S(1)}, s32[1,4096]{1,0:T(1,128)}, u32[]{:S(2)}) copy-start(s32[1,4096]{1,0:T(1,128)} %param.16) | copy-start | bytes 49156
  7.6 3.3 %copy-start.4 = (s32[1,4096]{1,0:T(1,128)S(1)}, s32[1,4096]{1,0:T(1,128)}, u32[]{:S(2)}) copy-start(s32[1,4096]{1,0:T(1,128)} %param.17) | copy-start | bytes 49156
  7.6 3.3 %copy-start.5 = (s32[1,4096]{1,0:T(1,128)S(1)}, s32[1,4096]{1,0:T(1,128)}, u32[]{:S(2)}) copy-start(s32[1,4096]{1,0:T(1,128)} %param.18) | copy-start | bytes 49156
  8.0 3.0 %copy-start = (f32[2,1,4096]{2,1,0:T(1,128)S(1)}, f32[2,1,4096]{2,1,0:T(1,128)}, u32[]{:S(2)}) copy-start(f32[2,1,4096]{2,1,0:T(1,128)} %param.19) | copy-start | bytes 98308
  8.0 1.2 %collective-permute-start.3 = (f32[2,2,256]{2,1,0:T(2,128)S(1)}, f32[2,2,256]{2,1,0:T(2,128)S(1)}, u32[]{:S(2)}, u32[]{:S(2)}) collective-permute-start(f32[2,2,256]{2,1,0:T(2,128)S(1)} %shard_map.103), channel_id=1, source_target_pairs={{0,1},{1,0},{2,3},{3,2},{4,5},{5,4},{6,7},{7,6},{8,9},{9,8},{10,11... | collective-permute-start | bytes 12296 | tf_op jit(solution)/shard_map/ppermute | solution.py:312
  9.2 3.0 %collective-permute-start.4 = (bf16[2,2,256]{2,1,0:T(2,128)(2,1)S(1)}, bf16[2,2,256]{2,1,0:T(2,128)(2,1)S(1)}, u32[]{:S(2)}, u32[]{:S(2)}) collective-permute-start(bf16[2,2,256]{2,1,0:T(2,128)(2,1)S(1)} %add_convert_fusion), channel_id=1, source_target_pairs={{0,5},{1,4},{2,7},{3,6},{4,1},{5,0},{6,3},{7,2},{8,13},{9,12},{10,... | collective-permute-start | bytes 6152 | tf_op jit(solution)/shard_map/ppermute | solution.py:312
  12.3 3.1 %collective-permute-start.5 = (bf16[2,2,2,256]{3,2,0,1:T(2,128)(2,1)S(1)}, bf16[2,2,2,256]{3,2,0,1:T(2,128)(2,1)S(1)}, u32[]{:S(2)}, u32[]{:S(2)}) collective-permute-start(bf16[2,2,2,256]{3,2,0,1:T(2,128)(2,1)S(1)} %pad_maximum_fusion.1), channel_id=1, source_target_pairs={{0,9},{1,8},{2,11},{3,10},{4,13},{5,12},{6,15},{7,14},{8,1},{9,0},... | collective-permute-start | bytes 12296 | tf_op jit(solution)/shard_map/ppermute | solution.py:312
  15.4 4.0 %collective-permute-start.6 = (bf16[4,2,256]{2,1,0:T(2,128)(2,1)S(1)}, bf16[4,2,256]{2,1,0:T(2,128)(2,1)S(1)}, u32[]{:S(2)}, u32[]{:S(2)}) collective-permute-start(bf16[4,2,256]{2,1,0:T(2,128)(2,1)S(1)} %slice_bitcast_fusion), channel_id=1, source_target_pairs={{0,17},{1,16},{2,19},{3,18},{4,21},{5,20},{6,23},{7,22},{8,25},{9,... | collective-permute-start | bytes 12296 | tf_op jit(solution)/shard_map/ppermute | solution.py:312

commit v7 on v6

--- a/solution.py
+++ b/solution.py
@@ -1,3 +1,4 @@
+import functools
 import math
 
 import jax
@@ -150,19 +151,39 @@
     out[:, :, MPRIME:, :] = jnp.zeros_like(out[:, :, MPRIME:, :])
 
 
-def sample_kernel(turns, table, block, phi, psi, frac, phase, *index):
+def own_lanes(values, column):
+    spare = jnp.zeros((values.shape[0], LANES - values.shape[1]), values.dtype)
+    wide = jnp.concatenate([values, spare], 1)
+    return jnp.take_along_axis(wide, column, axis=1, mode="promise_in_bounds")
+
+
+def sample_kernel(half, orders, cycles, lists, block, phi, psi, frac, phase, *index):
     scale = 2.0 / math.sqrt(phase.shape[1] * MPRIME)
-    step = turns[...]
-    quarter = (lax.broadcasted_iota(jnp.int32, step.shape, 0) & 1).astype(jnp.float32) * 0.25
-    starts = jnp.broadcast_to(table[0:1, :], step.shape)
-    cycles = jnp.broadcast_to(table[1:2, :], step.shape)
-    eight = step.shape[0]
+    band = lax.axis_index("band")
+    eight = phase.shape[1]
+    row = lax.broadcasted_iota(jnp.int32, (eight, LANES), 0)
+    orders = jnp.broadcast_to(orders[...], (eight, orders.shape[1]))
+    order = own_lanes(orders, band ^ (half * (eight // 2) + row // 2))
+    step = order.astype(jnp.float32) * (1.0 / NPHI)
+    quarter = (row & 1).astype(jnp.float32) * 0.25
+    sources, entries = lists.shape[:2]
+    codes = jnp.concatenate([lists[source] for source in range(sources)], 0)
+    codes = jnp.maximum(own_lanes(codes, jnp.full((codes.shape[0], LANES), band)), 0)
     for h in range(0, block.shape[0], eight):
         blocks = block[h : h + eight, :]
-        start = jnp.take_along_axis(starts, blocks, axis=1, mode="promise_in_bounds")
+        start = jnp.zeros_like(blocks)
+        cycle = jnp.zeros_like(blocks)
+        for entry in range(sources * entries):
+            code = codes[entry : entry + 1, :]
+            here = blocks == entry
+            start = jnp.where(here, code & (NPHI - 1), start)
+            if index:
+                source = entry // entries
+                for slot in range(cycles.shape[0]):
+                    kept = here & (code >= slot * NPHI)
+                    cycle = jnp.where(kept, cycles[slot : slot + 1, source : source + 1], cycle)
         if index:
             low, high = index
-            cycle = jnp.take_along_axis(cycles, blocks, axis=1, mode="promise_in_bounds")
             cell = psi[h : h + eight, :]
             low[h : h + eight, :] = cycle * NPSI + cell
             high[h : h + eight, :] = cycle * NPSI + ((cell + 1) & (NPSI - 1))
@@ -296,7 +317,6 @@
 ):
     f32 = jnp.float32
     bands = lax.axis_size("band")
-    band = lax.axis_index("band")
     chunk, cycles = wigner_panel.shape[2:]
     groups = sample_block.shape[1] // LANES
     psi_width = cycles * NPSI
@@ -332,31 +352,21 @@
     )
     rows = (sums + swap(sums, 0, 1)[::-1]).astype(jnp.bfloat16)
     rows_y = swap(rows, 1, 1)
-    here = lax.broadcasted_iota(jnp.int32, (bands, bands), 0) ^ band
-    there = lax.broadcasted_iota(jnp.int32, (bands, bands), 1)
-    turns = jnp.sum(jnp.where(here == there, m_values, 0), 1).astype(f32) * (1.0 / NPHI)
-    turns = jnp.broadcast_to(turns.reshape(2, bands // 2, 1, 1), (2, bands // 2, 2, LANES))
-    turns = turns.reshape(2, bands, LANES)
-    owners = lax.broadcasted_iota(jnp.int32, send_lists.shape[1:], 1)
-    codes = jnp.sum(jnp.where(owners == band, jnp.maximum(send_lists[0], 0), 0), 1)
-    slots = lax.broadcasted_iota(jnp.int32, (*codes.shape, cycle_table.shape[1]), 2)
-    chosen = jnp.where(slots == (codes // NPHI)[..., None], cycle_table[:, None, :], 0)
-    table = jnp.stack([codes % NPHI, jnp.sum(chosen, 2)]).reshape(2, -1)
-    table = jnp.pad(table, ((0, 0), (0, LANES - table.shape[1])))
     weights = jax.ShapeDtypeStruct((groups, bands, LANES), f32)
     index = jax.ShapeDtypeStruct((groups, LANES), jnp.int32)
     frac = sample_frac.reshape(2, groups, LANES)
     where = (sample_block, sample_phi, sample_psi)
-    samples = (*(a.reshape(groups, LANES) for a in where), frac)
-    table, _ = lax.optimization_barrier((table, rows))
-    near, low, high = call(sample_kernel, (weights, index, index), [vmem()] * 6)(
-        turns[0], table, *samples
-    )
+    lists = (m_values.reshape(1, -1), cycle_table.T, jnp.transpose(send_lists[0], (0, 2, 1)))
+    samples = (*lists, *(a.reshape(groups, LANES) for a in where), frac)
+    late, _ = lax.optimization_barrier((samples[0], rows))
+    near, low, high = call(
+        functools.partial(sample_kernel, 0), (weights, index, index), [vmem()] * 7
+    )(late, *samples[1:])
     rows_y, near = lax.optimization_barrier((rows_y, near))
     pair = jnp.stack([rows, rows_y[::-1]])
     pair_z = swap(pair, 2, 1)
-    table, _ = lax.optimization_barrier((table, pair))
-    far = call(sample_kernel, weights, [vmem()] * 6)(turns[1], table, *samples)
+    late, _ = lax.optimization_barrier((samples[0], pair))
+    far = call(functools.partial(sample_kernel, 1), weights, [vmem()] * 7)(late, *samples[1:])
     pair_z, far = lax.optimization_barrier((pair_z, far))
     quad = jnp.concatenate([pair, pair_z[:, ::-1]])
     rest = swap(quad[:, 1], 4, 1)

time: 20.7 us -> 20.6 us (level)
  waiting for transfers between devices: 4.11 us -> 6.35 us
  local copies, waits for them, and re-layouts: 3.96 us -> 2.43 us
  starting transfers between devices: 8.89 us -> 8.34 us
  other arithmetic: 0.42 us -> 0.04 us
  Pallas kernels: 2.86 us -> 3.12 us
    ppermute x7, waiting for transfers between devices: 4.11 us -> 6.35 us  [swap(): return lax.ppermute(x, ('band', 'det'), pairs)]
    unnamed x20, local copies, waits for them, and re-layouts: 3.08 us -> 2.4 us
    ppermute x7, starting transfers between devices: 8.89 us -> 8.34 us  [swap(): return lax.ppermute(x, ('band', 'det'), pairs)]
    broadcast_in_dim x6 -> x0, local copies, waits for them, and re-layouts: 0.45 us -> none  [by_samples(): jnp.broadcast_to(turns.reshape(2, bands // 2, 1, 1), (2, bands // 2, 2, L...]
    reduce_sum x3 -> x0, other arithmetic: 0.33 us -> none  [the longest x1 0.18 us: by_samples(): jnp.sum(jnp.where(here == there, m_values, 0), 1).astype(f32) * (1.0 / NPHI)]
    pallas_call x2, Pallas kernels: 0.6 us -> 0.86 us  [the longest x1 0.53 us: by_samples(): call(functools.partial(sample_kernel, 0), (weights, index, index), [vmem(...]
    reduce_sum x3 -> x0, local copies, waits for them, and re-layouts: 0.25 us -> none  [the longest x2 0.16 us: by_samples(): jnp.sum(jnp.where(owners == band, jnp.maximum(send_lists[0], 0), 0), 1)]
  transfers between devices with their start and end apart: 7 -> 7, of which waited for: 5 -> 5; matrix products, arithmetic and copies ran while one was open for 6% -> 0% of each run, Pallas kernels for 7% -> 9%
where the time goes in v7:
time: 20.6 us; the launch traced here: 20.4 us
  starting transfers between devices  8.34 us (40%)
  waiting for transfers between devices  6.35 us (31%)
  Pallas kernels  3.12 us (15%)
  local copies, waits for them, and re-layouts  2.43 us (12%)
    ppermute x7, starting transfers between devices, swap(): return lax.ppermute(x, ('band', 'det'), pairs)  8.34 us
    ppermute x7, waiting for transfers between devices, swap(): return lax.ppermute(x, ('band', 'det'), pairs)  6.35 us
    unnamed x20, local copies, waits for them, and re-layouts  2.4 us
    pallas_call x1, Pallas kernels, by_samples(): call(second_half_kernel, jax.ShapeDtypeStruct((groups, LANES), f32), [vme...  1 us
    pallas_call x1, Pallas kernels, by_samples(): call(functools.partial(sample_kernel, 0), (weights, index, index), [vmem(...  0.53 us
  transfers between devices with their start and end apart: 7, of which 5 were waited for; matrix products, arithmetic and copies ran while one was open for 0% of the time, Pallas kernels for 9%

profile of v7, /device:TPU:0, one launch (start us, length us, event | category | flops | bytes accessed | tf_op | source)
XLA Modules:
  0.0 20.4 jit_solution(4599536669640936650)
XLA Ops:
  0.0 0.5 %collective-permute-start = (bf16[3,17,2,2048]{3,2,1,0:T(2,128)(2,1)}, bf16[3,17,2,2048]{3,2,1,0:T(2,128)(2,1)S(1)}, u32[]{:S(2)}, u32[]{:S(2)}) collective-permute-start(bf16[3,17,2,2048]{3,2,1,0:T(2,128)(2,1)} %bitcast.29), channel_id=1, source_target_pairs={{0,1},{1,0},{2,3},{3,2},{4,5},{5,4},{6,7},{7,6},{8,9},{9,8},{10,11... | collective-permute-start | bytes 1253384 | tf_op jit(solution)/shard_map/ppermute | solution.py:332
  0.5 2.6 %collective-permute-start.2 = (bf16[136,512]{1,0:T(8,128)(2,1)}, bf16[136,512]{1,0:T(8,128)(2,1)S(1)}, u32[]{:S(2)}, u32[]{:S(2)}) collective-permute-start(bf16[136,512]{1,0:T(8,128)(2,1)} %bitcast.31), channel_id=1, source_target_pairs={{0,3},{1,2},{2,1},{3,0},{4,7},{5,6},{6,5},{7,4},{8,11},{9,10},{10,... | collective-permute-start | bytes 417800 | tf_op jit(solution)/shard_map/ppermute | solution.py:332
  3.1 0.0 collective-permute-start.1
  3.1 0.0 copy-start.1
  3.1 1.0 %copy-done.1 = bf16[1,3,2,17,2048]{4,2,3,1,0:T(2,128)(2,1)S(1)} copy-done((bf16[1,3,2,17,2048]{4,2,3,1,0:T(2,128)(2,1)S(1)}, bf16[1,3,2,17,2048]{4,2,3,1,0:T(2,128)(2,1)}, u32[]{:S(2)}) %copy-start.1) | copy-done | bytes 417816
  4.1 0.1 shard_map.100.beam_own
  4.2 0.0 copy-start.2
  4.3 0.0 copy-start.7
  4.3 0.0 collective-permute-done.source
  4.3 0.1 shard_map.101.beam_other
  4.4 0.7 %copy-done.2 = bf16[1,17,512,8]{2,3,1,0:T(8,128)(2,1)S(1)} copy-done((bf16[1,17,512,8]{2,3,1,0:T(8,128)(2,1)S(1)}, bf16[1,17,512,8]{2,3,1,0:T(8,128)(2,1)}, u32[]{:S(2)}) %copy-start.2) | copy-done | bytes 139288
  5.1 0.0 copy-done.7
  5.2 0.2 %shard_map.102 = (f32[96,136]{1,0:T(8,128)S(1)}, f32[2,48,256]{2,1,0:T(8,128)S(1)}) custom-call(f32[3,2,24,1024]{3,2,1,0:T(8,128)S(1)} %shard_map.100.beam_own, f32[3,2,24,1024]{3,2,1,0:T(8,128)S(1)} %shard_map.101.beam_other, f32[3,2,1,512]{3,2,1,0:T(1,128)S(1)} %copy-done.7, bf16[136,512]{1,0:T(8,128)(2,1)S(1)} %bitcast.32), custom_call_target="tpu_custom_call" | custom-call | flops 1 | bytes 1 | tf_op jit(solution)/shard_map/pallas_call | solution.py:342
  5.4 2.2 %collective-permute-done.1.sky = f32[3,2,1,512]{3,2,1,0:T(1,128)S(1)} collective-permute-done((f32[3,2,1,512]{3,2,1,0:T(1,128)}, f32[3,2,1,512]{3,2,1,0:T(1,128)S(1)}, u32[]{:S(2)}, u32[]{:S(2)}) %collective-permute-start.1) | collective-permute-done | bytes 12320 | tf_op jit(solution)/shard_map/ppermute | solution.py:332
  7.6 0.0 collective-permute-done.2.w
  7.6 0.0 copy-start
  7.6 0.0 copy-start.4
  7.6 0.0 copy-start.5
  7.6 0.0 copy-start.6
  7.6 0.4 %shard_map.103 = f32[2,2,256]{2,1,0:T(2,128)S(1)} custom-call(f32[3,2,24,1024]{3,2,1,0:T(8,128)S(1)} %shard_map.100.beam_own, f32[3,2,24,1024]{3,2,1,0:T(8,128)S(1)} %shard_map.101.beam_other, f32[3,2,1,512]{3,2,1,0:T(1,128)S(1)} %collective-permute-done.1.sky, bf16[136,512]{1,0:T(8,128)(2,1)S(1)} %collective-permute-done.2.w, ...), custom_call_target="tpu_custom_call" | custom-call | flops 1 | bytes 1 | tf_op jit(solution)/shard_map/pallas_call | solution.py:350
  8.0 0.0 copy-start.3
  8.0 0.2 collective-permute-start.3
  8.2 1.1 %collective-permute-done.3 = f32[2,2,256]{2,1,0:T(2,128)S(1)} collective-permute-done((f32[2,2,256]{2,1,0:T(2,128)S(1)}, f32[2,2,256]{2,1,0:T(2,128)S(1)}, u32[]{:S(2)}, u32[]{:S(2)}) %collective-permute-start.3) | collective-permute-done | bytes 4128 | tf_op jit(solution)/shard_map/ppermute | solution.py:332
  9.2 1.3 %collective-permute-start.4 = (bf16[2,2,256]{2,1,0:T(2,128)(2,1)S(1)}, bf16[2,2,256]{2,1,0:T(2,128)(2,1)S(1)}, u32[]{:S(2)}, u32[]{:S(2)}) collective-permute-start(bf16[2,2,256]{2,1,0:T(2,128)(2,1)S(1)} %add_convert_fusion), channel_id=1, source_target_pairs={{0,5},{1,4},{2,7},{3,6},{4,1},{5,0},{6,3},{7,2},{8,13},{9,12},{10,... | collective-permute-start | bytes 6152 | tf_op jit(solution)/shard_map/ppermute | solution.py:332
  10.5 0.0 copy-start.8
  10.5 0.0 copy-start.9
  10.5 0.0 copy-done
  10.5 0.0 copy-done.4
  10.5 0.0 copy-done.5
  10.5 0.0 copy-done.6
  10.5 0.0 copy-done.3
  10.5 0.6 %copy-done.8 = s32[8,3]{0,1:T(4,128)S(1)} copy-done((s32[8,3]{0,1:T(4,128)S(1)}, s32[8,3]{0,1:T(4,128)}, u32[]{:S(2)}) %copy-start.8) | copy-done | bytes 120
  11.2 0.0 copy-done.9
  11.2 0.5 %shard_map.104 = (f32[32,8,128]{2,1,0:T(8,128)S(1)}, s32[32,128]{1,0:T(8,128)S(1)}, s32[32,128]{1,0:T(8,128)S(1)}) custom-call(s32[1,8]{1,0:T(1,128)S(1)} %bitcast.43, s32[3,8]{1,0:T(4,128)S(1)} %bitcast.41, s32[8,2,8]{2,1,0:T(2,128)S(1)} %bitcast.39, s32[32,128]{1,0:T(8,128)S(1)} %bitcast.33, s32[32,128]{1,0:T(8,128)S(1)} %bitcast.35, ...), custom_call_target="tpu_custom_call" | custom-call | flops 1 | bytes 1 | tf_op jit(solution)/shard_map/pallas_call | solution.py:362
  11.7 0.5 %collective-permute-done.4 = bf16[2,2,256]{2,1,0:T(2,128)(2,1)S(1)} collective-permute-done((bf16[2,2,256]{2,1,0:T(2,128)(2,1)S(1)}, bf16[2,2,256]{2,1,0:T(2,128)(2,1)S(1)}, u32[]{:S(2)}, u32[]{:S(2)}) %collective-permute-start.4) | collective-permute-done | bytes 2080 | tf_op jit(solution)/shard_map/ppermute | solution.py:332
  12.3 1.4 %collective-permute-start.5 = (bf16[2,2,2,256]{3,2,0,1:T(2,128)(2,1)S(1)}, bf16[2,2,2,256]{3,2,0,1:T(2,128)(2,1)S(1)}, u32[]{:S(2)}, u32[]{:S(2)}) collective-permute-start(bf16[2,2,2,256]{3,2,0,1:T(2,128)(2,1)S(1)} %pad_maximum_fusion.1), channel_id=1, source_target_pairs={{0,9},{1,8},{2,11},{3,10},{4,13},{5,12},{6,15},{7,14},{8,1},{9,0},... | collective-permute-start | bytes 12296 | tf_op jit(solution)/shard_map/ppermute | solution.py:332
  13.7 0.3 %shard_map.105.phase = f32[32,8,128]{2,1,0:T(8,128)S(1)} custom-call(s32[1,8]{1,0:T(1,128)S(1)} %bitcast.44, s32[3,8]{1,0:T(4,128)S(1)} %bitcast.42, s32[8,2,8]{2,1,0:T(2,128)S(1)} %bitcast.40, s32[32,128]{1,0:T(8,128)S(1)} %bitcast.34, s32[32,128]{1,0:T(8,128)S(1)} %bitcast.36, s32[32,128]{1,0:T(8,128)S(1)} %bitcast.38, f32[2,32,128]{2,1,0:T(8,128)S(1)} %bitcast.26), custom_call_target="tpu_custom_call" | custom-call | flops 1 | bytes 1 | tf_op jit(solution)/shard_map/pallas_call | solution.py:369
  14.0 1.4 %collective-permute-done.5 = bf16[2,2,2,256]{3,2,0,1:T(2,128)(2,1)S(1)} collective-permute-done((bf16[2,2,2,256]{3,2,0,1:T(2,128)(2,1)S(1)}, bf16[2,2,2,256]{3,2,0,1:T(2,128)(2,1)S(1)}, u32[]{:S(2)}, u32[]{:S(2)}) %collective-permute-start.5) | collective-permute-done | bytes 4128 | tf_op jit(solution)/shard_map/ppermute | solution.py:332
  15.4 2.4 %collective-permute-start.6 = (bf16[4,2,256]{2,1,0:T(2,128)(2,1)S(1)}, bf16[4,2,256]{2,1,0:T(2,128)(2,1)S(1)}, u32[]{:S(2)}, u32[]{:S(2)}) collective-permute-start(bf16[4,2,256]{2,1,0:T(2,128)(2,1)S(1)} %slice_bitcast_fusion), channel_id=1, source_target_pairs={{0,17},{1,16},{2,19},{3,18},{4,21},{5,20},{6,23},{7,22},{8,25},{9,... | collective-permute-start | bytes 12296 | tf_op jit(solution)/shard_map/ppermute | solution.py:332
  17.8 0.4 %shard_map.106.first = f32[32,8,128]{2,1,0:T(8,128)S(1)} custom-call(bf16[4,2,2,256]{3,2,1,0:T(2,128)(2,1)S(1)} %copy.15.held, f32[32,8,128]{2,1,0:T(8,128)S(1)} %get-tuple-element.23.phase, s32[32,128]{1,0:T(8,128)S(1)} %get-tuple-element.24.low, s32[32,128]{1,0:T(8,128)S(1)} %get-tuple-element.25.high, f32[2,32,128]{2,1,0:T(8,128)S(1)} %bitcast.27), custom_call_target="tpu_custom_call" | custom-call | flops 1 | bytes 1 | tf_op jit(solution)/shard_map/pallas_call | solution.py:373
  18.2 1.2 %collective-permute-done.6.received = bf16[4,2,256]{2,1,0:T(2,128)(2,1)S(1)} collective-permute-done((bf16[4,2,256]{2,1,0:T(2,128)(2,1)S(1)}, bf16[4,2,256]{2,1,0:T(2,128)(2,1)S(1)}, u32[]{:S(2)}, u32[]{:S(2)}) %collective-permute-start.6) | collective-permute-done | bytes 4128 | tf_op jit(solution)/shard_map/ppermute | solution.py:332
  19.4 1.0 %shard_map.107 = f32[32,128]{1,0:T(8,128)} custom-call(bf16[4,2,256]{2,1,0:T(2,128)(2,1)S(1)} %collective-permute-done.6.received, f32[32,8,128]{2,1,0:T(8,128)S(1)} %shard_map.106.first, f32[32,8,128]{2,1,0:T(8,128)S(1)} %shard_map.105.phase, s32[32,128]{1,0:T(8,128)S(1)} %get-tuple-element.24.low, s32[32,128]{1,0:T(8,128)S(1)} %get-tuple-element.25.high, ...), custom_call_target="tpu_custom_call" | custom-call | flops 1 | bytes 1 | tf_op jit(solution)/shard_map/pallas_call | solution.py:374
  (7 shorter events, 0.1 us)
Async XLA Ops:
  0.0 4.3 %collective-permute-start = (bf16[3,17,2,2048]{3,2,1,0:T(2,128)(2,1)}, bf16[3,17,2,2048]{3,2,1,0:T(2,128)(2,1)S(1)}, u32[]{:S(2)}, u32[]{:S(2)}) collective-permute-start(bf16[3,17,2,2048]{3,2,1,0:T(2,128)(2,1)} %bitcast.29), channel_id=1, source_target_pairs={{0,1},{1,0},{2,3},{3,2},{4,5},{5,4},{6,7},{7,6},{8,9},{9,8},{10,11... | collective-permute-start | bytes 1253384 | tf_op jit(solution)/shard_map/ppermute | solution.py:332
  0.5 7.1 %collective-permute-start.2 = (bf16[136,512]{1,0:T(8,128)(2,1)}, bf16[136,512]{1,0:T(8,128)(2,1)S(1)}, u32[]{:S(2)}, u32[]{:S(2)}) collective-permute-start(bf16[136,512]{1,0:T(8,128)(2,1)} %bitcast.31), channel_id=1, source_target_pairs={{0,3},{1,2},{2,1},{3,0},{4,7},{5,6},{6,5},{7,4},{8,11},{9,10},{10,... | collective-permute-start | bytes 417800 | tf_op jit(solution)/shard_map/ppermute | solution.py:332
  3.1 4.5 %collective-permute-start.1 = (f32[3,2,1,512]{3,2,1,0:T(1,128)}, f32[3,2,1,512]{3,2,1,0:T(1,128)S(1)}, u32[]{:S(2)}, u32[]{:S(2)}) collective-permute-start(f32[3,2,1,512]{3,2,1,0:T(1,128)} %sky.1), channel_id=1, source_target_pairs={{0,3},{1,2},{2,1},{3,0},{4,7},{5,6},{6,5},{7,4},{8,11},{9,10},{10,... | collective-permute-start | bytes 36872 | tf_op jit(solution)/shard_map/ppermute | solution.py:332
  3.1 1.0 %copy-start.1 = (bf16[1,3,2,17,2048]{4,2,3,1,0:T(2,128)(2,1)S(1)}, bf16[1,3,2,17,2048]{4,2,3,1,0:T(2,128)(2,1)}, u32[]{:S(2)}) copy-start(bf16[1,3,2,17,2048]{4,2,3,1,0:T(2,128)(2,1)} %param.11) | copy-start | bytes 1253380
  4.2 0.9 %copy-start.2 = (bf16[1,17,512,8]{2,3,1,0:T(8,128)(2,1)S(1)}, bf16[1,17,512,8]{2,3,1,0:T(8,128)(2,1)}, u32[]{:S(2)}) copy-start(bf16[1,17,512,8]{2,3,1,0:T(8,128)(2,1)} %param.12) | copy-start | bytes 417796
  4.3 0.9 %copy-start.7 = (f32[3,2,1,512]{3,2,1,0:T(1,128)S(1)}, f32[3,2,1,512]{3,2,1,0:T(1,128)}, u32[]{:S(2)}) copy-start(f32[3,2,1,512]{3,2,1,0:T(1,128)} %sky.1) | copy-start | bytes 36868
  7.6 2.9 %copy-start = (f32[2,1,4096]{2,1,0:T(1,128)S(1)}, f32[2,1,4096]{2,1,0:T(1,128)}, u32[]{:S(2)}) copy-start(f32[2,1,4096]{2,1,0:T(1,128)} %param.19) | copy-start | bytes 98308
  7.6 2.9 %copy-start.4 = (s32[1,4096]{1,0:T(1,128)S(1)}, s32[1,4096]{1,0:T(1,128)}, u32[]{:S(2)}) copy-start(s32[1,4096]{1,0:T(1,128)} %param.17) | copy-start | bytes 49156
  7.6 2.9 %copy-start.5 = (s32[1,4096]{1,0:T(1,128)S(1)}, s32[1,4096]{1,0:T(1,128)}, u32[]{:S(2)}) copy-start(s32[1,4096]{1,0:T(1,128)} %param.18) | copy-start | bytes 49156
  7.6 2.9 %copy-start.6 = (s32[1,8,8,2]{2,3,1,0:T(2,128)S(1)}, s32[1,8,8,2]{2,3,1,0:T(2,128)}, u32[]{:S(2)}) copy-start(s32[1,8,8,2]{2,3,1,0:T(2,128)} %param.15) | copy-start | bytes 1540
  8.0 2.6 %copy-start.3 = (s32[1,4096]{1,0:T(1,128)S(1)}, s32[1,4096]{1,0:T(1,128)}, u32[]{:S(2)}) copy-start(s32[1,4096]{1,0:T(1,128)} %param.16) | copy-start | bytes 49156
  8.0 1.2 %collective-permute-start.3 = (f32[2,2,256]{2,1,0:T(2,128)S(1)}, f32[2,2,256]{2,1,0:T(2,128)S(1)}, u32[]{:S(2)}, u32[]{:S(2)}) collective-permute-start(f32[2,2,256]{2,1,0:T(2,128)S(1)} %shard_map.103), channel_id=1, source_target_pairs={{0,1},{1,0},{2,3},{3,2},{4,5},{5,4},{6,7},{7,6},{8,9},{9,8},{10,11... | collective-permute-start | bytes 12296 | tf_op jit(solution)/shard_map/ppermute | solution.py:332
  9.2 3.0 %collective-permute-start.4 = (bf16[2,2,256]{2,1,0:T(2,128)(2,1)S(1)}, bf16[2,2,256]{2,1,0:T(2,128)(2,1)S(1)}, u32[]{:S(2)}, u32[]{:S(2)}) collective-permute-start(bf16[2,2,256]{2,1,0:T(2,128)(2,1)S(1)} %add_convert_fusion), channel_id=1, source_target_pairs={{0,5},{1,4},{2,7},{3,6},{4,1},{5,0},{6,3},{7,2},{8,13},{9,12},{10,... | collective-permute-start | bytes 6152 | tf_op jit(solution)/shard_map/ppermute | solution.py:332
  10.5 0.7 %copy-start.8 = (s32[8,3]{0,1:T(4,128)S(1)}, s32[8,3]{0,1:T(4,128)}, u32[]{:S(2)}) copy-start(s32[8,3]{0,1:T(4,128)} %param.14) | copy-start | bytes 292
  10.5 0.7 %copy-start.9 = (s32[8]{0:T(128)S(1)}, s32[8]{0:T(128)}, u32[]{:S(2)}) copy-start(s32[8]{0:T(128)} %param.13) | copy-start | bytes 100
  12.3 3.1 %collective-permute-start.5 = (bf16[2,2,2,256]{3,2,0,1:T(2,128)(2,1)S(1)}, bf16[2,2,2,256]{3,2,0,1:T(2,128)(2,1)S(1)}, u32[]{:S(2)}, u32[]{:S(2)}) collective-permute-start(bf16[2,2,2,256]{3,2,0,1:T(2,128)(2,1)S(1)} %pad_maximum_fusion.1), channel_id=1, source_target_pairs={{0,9},{1,8},{2,11},{3,10},{4,13},{5,12},{6,15},{7,14},{8,1},{9,0},... | collective-permute-start | bytes 12296 | tf_op jit(solution)/shard_map/ppermute | solution.py:332
  15.4 4.0 %collective-permute-start.6 = (bf16[4,2,256]{2,1,0:T(2,128)(2,1)S(1)}, bf16[4,2,256]{2,1,0:T(2,128)(2,1)S(1)}, u32[]{:S(2)}, u32[]{:S(2)}) collective-permute-start(bf16[4,2,256]{2,1,0:T(2,128)(2,1)S(1)} %slice_bitcast_fusion), channel_id=1, source_target_pairs={{0,17},{1,16},{2,19},{3,18},{4,21},{5,20},{6,23},{7,22},{8,25},{9,... | collective-permute-start | bytes 12296 | tf_op jit(solution)/shard_map/ppermute | solution.py:332

commit v8 on v7

--- a/solution.py
+++ b/solution.py
@@ -266,8 +266,9 @@
     return (at_low + frac[1, g : g + 1, :] * (at_high - at_low)) * phase[g]
 
 
-def first_half_kernel(held, phase, low, high, frac, out):
-    part = jnp.concatenate([held[k, 0].astype(jnp.float32) for k in range(held.shape[0])], 0)
+def first_half_kernel(held, received, phase, low, high, frac, out):
+    parts = (held[0, 0], held[1, 1], received[0, 1], received[1, 0])
+    part = jnp.concatenate([rows.astype(jnp.float32) for rows in parts], 0)
     for g in range(out.shape[0]):
         out[g] = half_sum(part, phase, low, high, frac, g)
 
@@ -363,14 +364,13 @@
         functools.partial(sample_kernel, 0), (weights, index, index), [vmem()] * 7
     )(late, *samples[1:])
     rows_y, near = lax.optimization_barrier((rows_y, near))
-    pair = jnp.stack([rows, rows_y[::-1]])
+    pair = jnp.stack([rows, rows_y])
     pair_z = swap(pair, 2, 1)
     late, _ = lax.optimization_barrier((samples[0], pair))
     far = call(functools.partial(sample_kernel, 1), weights, [vmem()] * 7)(late, *samples[1:])
     pair_z, far = lax.optimization_barrier((pair_z, far))
-    quad = jnp.concatenate([pair, pair_z[:, ::-1]])
-    rest = swap(quad[:, 1], 4, 1)
-    first = call(first_half_kernel, weights, [vmem()] * 5)(quad, near, low, high, frac)
+    rest = swap(jnp.stack([pair[0, 1], pair[1, 0], pair_z[0, 0], pair_z[1, 1]]), 4, 1)
+    first = call(first_half_kernel, weights, [vmem()] * 6)(pair, pair_z, near, low, high, frac)
     values = call(
         second_half_kernel, jax.ShapeDtypeStruct((groups, LANES), f32), [vmem()] * 6
     )(rest, first, far, low, high, frac)

time: 20.6 us -> 20.6 us (level)
  no operation moved by 1% of the time
where the time goes in v8:
time: 20.6 us; the launch traced here: 20.4 us
  starting transfers between devices  8.34 us (40%)
  waiting for transfers between devices  6.34 us (31%)
  Pallas kernels  3.12 us (15%)
  local copies, waits for them, and re-layouts  2.41 us (12%)
    ppermute x7, starting transfers between devices, swap(): return lax.ppermute(x, ('band', 'det'), pairs)  8.34 us
    ppermute x7, waiting for transfers between devices, swap(): return lax.ppermute(x, ('band', 'det'), pairs)  6.34 us
    unnamed x20, local copies, waits for them, and re-layouts  2.4 us
    pallas_call x1, Pallas kernels, by_samples(): call(second_half_kernel, jax.ShapeDtypeStruct((groups, LANES), f32), [vme...  1 us
    pallas_call x1, Pallas kernels, by_samples(): call(functools.partial(sample_kernel, 0), (weights, index, index), [vmem(...  0.53 us
  transfers between devices with their start and end apart: 7, of which 5 were waited for; matrix products, arithmetic and copies ran while one was open for 0% of the time, Pallas kernels for 9%

profile of v8, /device:TPU:0, one launch (start us, length us, event | category | flops | bytes accessed | tf_op | source)
XLA Modules:
  0.0 20.4 jit_solution(16536047799201642797)
XLA Ops:
  0.0 0.5 %collective-permute-start = (bf16[3,17,2,2048]{3,2,1,0:T(2,128)(2,1)}, bf16[3,17,2,2048]{3,2,1,0:T(2,128)(2,1)S(1)}, u32[]{:S(2)}, u32[]{:S(2)}) collective-permute-start(bf16[3,17,2,2048]{3,2,1,0:T(2,128)(2,1)} %bitcast.32), channel_id=1, source_target_pairs={{0,1},{1,0},{2,3},{3,2},{4,5},{5,4},{6,7},{7,6},{8,9},{9,8},{10,11... | collective-permute-start | bytes 1253384 | tf_op jit(solution)/shard_map/ppermute | solution.py:333
  0.5 2.6 %collective-permute-start.2 = (bf16[136,512]{1,0:T(8,128)(2,1)}, bf16[136,512]{1,0:T(8,128)(2,1)S(1)}, u32[]{:S(2)}, u32[]{:S(2)}) collective-permute-start(bf16[136,512]{1,0:T(8,128)(2,1)} %bitcast.34), channel_id=1, source_target_pairs={{0,3},{1,2},{2,1},{3,0},{4,7},{5,6},{6,5},{7,4},{8,11},{9,10},{10,... | collective-permute-start | bytes 417800 | tf_op jit(solution)/shard_map/ppermute | solution.py:333
  3.1 0.0 collective-permute-start.1
  3.1 0.0 copy-start.1
  3.1 1.0 %copy-done.1 = bf16[1,3,2,17,2048]{4,2,3,1,0:T(2,128)(2,1)S(1)} copy-done((bf16[1,3,2,17,2048]{4,2,3,1,0:T(2,128)(2,1)S(1)}, bf16[1,3,2,17,2048]{4,2,3,1,0:T(2,128)(2,1)}, u32[]{:S(2)}) %copy-start.1) | copy-done | bytes 417816
  4.1 0.1 shard_map.100.beam_own
  4.2 0.0 copy-start.2
  4.3 0.0 copy-start.7
  4.3 0.0 collective-permute-done.source
  4.3 0.1 shard_map.101.beam_other
  4.4 0.7 %copy-done.2 = bf16[1,17,512,8]{2,3,1,0:T(8,128)(2,1)S(1)} copy-done((bf16[1,17,512,8]{2,3,1,0:T(8,128)(2,1)S(1)}, bf16[1,17,512,8]{2,3,1,0:T(8,128)(2,1)}, u32[]{:S(2)}) %copy-start.2) | copy-done | bytes 139288
  5.1 0.0 copy-done.7
  5.2 0.2 %shard_map.102 = (f32[96,136]{1,0:T(8,128)S(1)}, f32[2,48,256]{2,1,0:T(8,128)S(1)}) custom-call(f32[3,2,24,1024]{3,2,1,0:T(8,128)S(1)} %shard_map.100.beam_own, f32[3,2,24,1024]{3,2,1,0:T(8,128)S(1)} %shard_map.101.beam_other, f32[3,2,1,512]{3,2,1,0:T(1,128)S(1)} %copy-done.7, bf16[136,512]{1,0:T(8,128)(2,1)S(1)} %bitcast.35), custom_call_target="tpu_custom_call" | custom-call | flops 1 | bytes 1 | tf_op jit(solution)/shard_map/pallas_call | solution.py:343
  5.4 2.2 %collective-permute-done.1.sky = f32[3,2,1,512]{3,2,1,0:T(1,128)S(1)} collective-permute-done((f32[3,2,1,512]{3,2,1,0:T(1,128)}, f32[3,2,1,512]{3,2,1,0:T(1,128)S(1)}, u32[]{:S(2)}, u32[]{:S(2)}) %collective-permute-start.1) | collective-permute-done | bytes 12320 | tf_op jit(solution)/shard_map/ppermute | solution.py:333
  7.6 0.0 collective-permute-done.2.w
  7.6 0.0 copy-start
  7.6 0.0 copy-start.4
  7.6 0.0 copy-start.5
  7.6 0.4 %shard_map.103 = f32[2,2,256]{2,1,0:T(2,128)S(1)} custom-call(f32[3,2,24,1024]{3,2,1,0:T(8,128)S(1)} %shard_map.100.beam_own, f32[3,2,24,1024]{3,2,1,0:T(8,128)S(1)} %shard_map.101.beam_other, f32[3,2,1,512]{3,2,1,0:T(1,128)S(1)} %collective-permute-done.1.sky, bf16[136,512]{1,0:T(8,128)(2,1)S(1)} %collective-permute-done.2.w, ...), custom_call_target="tpu_custom_call" | custom-call | flops 1 | bytes 1 | tf_op jit(solution)/shard_map/pallas_call | solution.py:351
  8.0 0.0 copy-start.3
  8.0 0.2 collective-permute-start.3
  8.2 1.1 %collective-permute-done.3 = f32[2,2,256]{2,1,0:T(2,128)S(1)} collective-permute-done((f32[2,2,256]{2,1,0:T(2,128)S(1)}, f32[2,2,256]{2,1,0:T(2,128)S(1)}, u32[]{:S(2)}, u32[]{:S(2)}) %collective-permute-start.3) | collective-permute-done | bytes 4128 | tf_op jit(solution)/shard_map/ppermute | solution.py:333
  9.2 1.3 %collective-permute-start.4 = (bf16[2,2,256]{2,1,0:T(2,128)(2,1)S(1)}, bf16[2,2,256]{2,1,0:T(2,128)(2,1)S(1)}, u32[]{:S(2)}, u32[]{:S(2)}) collective-permute-start(bf16[2,2,256]{2,1,0:T(2,128)(2,1)S(1)} %add_convert_fusion), channel_id=1, source_target_pairs={{0,5},{1,4},{2,7},{3,6},{4,1},{5,0},{6,3},{7,2},{8,13},{9,12},{10,... | collective-permute-start | bytes 6152 | tf_op jit(solution)/shard_map/ppermute | solution.py:333
  10.5 0.0 copy-start.6
  10.5 0.0 copy-start.8
  10.5 0.0 copy-start.9
  10.5 0.0 copy-done
  10.5 0.0 copy-done.4
  10.5 0.0 copy-done.5
  10.5 0.0 copy-done.3
  10.5 0.6 %copy-done.6 = s32[1,8,8,2]{2,3,1,0:T(2,128)S(1)} copy-done((s32[1,8,8,2]{2,3,1,0:T(2,128)S(1)}, s32[1,8,8,2]{2,3,1,0:T(2,128)}, u32[]{:S(2)}) %copy-start.6) | copy-done | bytes 536
  11.2 0.0 copy-done.8
  11.2 0.0 copy-done.9
  11.2 0.5 %shard_map.104 = (f32[32,8,128]{2,1,0:T(8,128)S(1)}, s32[32,128]{1,0:T(8,128)S(1)}, s32[32,128]{1,0:T(8,128)S(1)}) custom-call(s32[1,8]{1,0:T(1,128)S(1)} %bitcast.46, s32[3,8]{1,0:T(4,128)S(1)} %bitcast.44, s32[8,2,8]{2,1,0:T(2,128)S(1)} %bitcast.42, s32[32,128]{1,0:T(8,128)S(1)} %bitcast.36, s32[32,128]{1,0:T(8,128)S(1)} %bitcast.38, ...), custom_call_target="tpu_custom_call" | custom-call | flops 1 | bytes 1 | tf_op jit(solution)/shard_map/pallas_call | solution.py:363
  11.7 0.5 %collective-permute-done.4 = bf16[2,2,256]{2,1,0:T(2,128)(2,1)S(1)} collective-permute-done((bf16[2,2,256]{2,1,0:T(2,128)(2,1)S(1)}, bf16[2,2,256]{2,1,0:T(2,128)(2,1)S(1)}, u32[]{:S(2)}, u32[]{:S(2)}) %collective-permute-start.4) | collective-permute-done | bytes 2080 | tf_op jit(solution)/shard_map/ppermute | solution.py:333
  12.2 1.4 %collective-permute-start.5 = (bf16[2,2,2,256]{3,2,1,0:T(2,128)(2,1)S(1)}, bf16[2,2,2,256]{3,2,1,0:T(2,128)(2,1)S(1)}, u32[]{:S(2)}, u32[]{:S(2)}) collective-permute-start(bf16[2,2,2,256]{3,2,1,0:T(2,128)(2,1)S(1)} %pad_maximum_fusion.held), channel_id=1, source_target_pairs={{0,9},{1,8},{2,11},{3,10},{4,13},{5,12},{6,15},{7,14},{8,1},{9,0},... | collective-permute-start | bytes 12296 | tf_op jit(solution)/shard_map/ppermute | solution.py:333
  13.6 0.3 %shard_map.105.phase = f32[32,8,128]{2,1,0:T(8,128)S(1)} custom-call(s32[1,8]{1,0:T(1,128)S(1)} %bitcast.47, s32[3,8]{1,0:T(4,128)S(1)} %bitcast.45, s32[8,2,8]{2,1,0:T(2,128)S(1)} %bitcast.43, s32[32,128]{1,0:T(8,128)S(1)} %bitcast.37, s32[32,128]{1,0:T(8,128)S(1)} %bitcast.39, s32[32,128]{1,0:T(8,128)S(1)} %bitcast.41, f32[2,32,128]{2,1,0:T(8,128)S(1)} %bitcast.29), custom_call_target="tpu_custom_call" | custom-call | flops 1 | bytes 1 | tf_op jit(solution)/shard_map/pallas_call | solution.py:370
  14.0 1.4 %collective-permute-done.5.received = bf16[2,2,2,256]{3,2,1,0:T(2,128)(2,1)S(1)} collective-permute-done((bf16[2,2,2,256]{3,2,1,0:T(2,128)(2,1)S(1)}, bf16[2,2,2,256]{3,2,1,0:T(2,128)(2,1)S(1)}, u32[]{:S(2)}, u32[]{:S(2)}) %collective-permute-start.5) | collective-permute-done | bytes 4128 | tf_op jit(solution)/shard_map/ppermute | solution.py:333
  15.4 2.4 %collective-permute-start.6 = (bf16[4,2,256]{2,1,0:T(2,128)(2,1)S(1)}, bf16[4,2,256]{2,1,0:T(2,128)(2,1)S(1)}, u32[]{:S(2)}, u32[]{:S(2)}) collective-permute-start(bf16[4,2,256]{2,1,0:T(2,128)(2,1)S(1)} %pad_maximum_fusion.1), channel_id=1, source_target_pairs={{0,17},{1,16},{2,19},{3,18},{4,21},{5,20},{6,23},{7,22},{8,25},{9,... | collective-permute-start | bytes 12296 | tf_op jit(solution)/shard_map/ppermute | solution.py:333
  17.8 0.4 %shard_map.106.first = f32[32,8,128]{2,1,0:T(8,128)S(1)} custom-call(bf16[2,2,2,256]{3,2,1,0:T(2,128)(2,1)S(1)} %pad_maximum_fusion.held, bf16[2,2,2,256]{3,2,1,0:T(2,128)(2,1)S(1)} %collective-permute-done.5.received, f32[32,8,128]{2,1,0:T(8,128)S(1)} %get-tuple-element.23.phase, s32[32,128]{1,0:T(8,128)S(1)} %get-tuple-element.24.low, ...), custom_call_target="tpu_custom_call" | custom-call | flops 1 | bytes 1 | tf_op jit(solution)/shard_map/pallas_call | solution.py:373
  18.1 1.2 %collective-permute-done.6.received = bf16[4,2,256]{2,1,0:T(2,128)(2,1)S(1)} collective-permute-done((bf16[4,2,256]{2,1,0:T(2,128)(2,1)S(1)}, bf16[4,2,256]{2,1,0:T(2,128)(2,1)S(1)}, u32[]{:S(2)}, u32[]{:S(2)}) %collective-permute-start.6) | collective-permute-done | bytes 4128 | tf_op jit(solution)/shard_map/ppermute | solution.py:333
  19.4 1.0 %shard_map.107 = f32[32,128]{1,0:T(8,128)} custom-call(bf16[4,2,256]{2,1,0:T(2,128)(2,1)S(1)} %collective-permute-done.6.received, f32[32,8,128]{2,1,0:T(8,128)S(1)} %shard_map.106.first, f32[32,8,128]{2,1,0:T(8,128)S(1)} %shard_map.105.phase, s32[32,128]{1,0:T(8,128)S(1)} %get-tuple-element.24.low, s32[32,128]{1,0:T(8,128)S(1)} %get-tuple-element.25.high, ...), custom_call_target="tpu_custom_call" | custom-call | flops 1 | bytes 1 | tf_op jit(solution)/shard_map/pallas_call | solution.py:374
  (6 shorter events, 0.0 us)
Async XLA Ops:
  0.0 4.3 %collective-permute-start = (bf16[3,17,2,2048]{3,2,1,0:T(2,128)(2,1)}, bf16[3,17,2,2048]{3,2,1,0:T(2,128)(2,1)S(1)}, u32[]{:S(2)}, u32[]{:S(2)}) collective-permute-start(bf16[3,17,2,2048]{3,2,1,0:T(2,128)(2,1)} %bitcast.32), channel_id=1, source_target_pairs={{0,1},{1,0},{2,3},{3,2},{4,5},{5,4},{6,7},{7,6},{8,9},{9,8},{10,11... | collective-permute-start | bytes 1253384 | tf_op jit(solution)/shard_map/ppermute | solution.py:333
  0.5 7.1 %collective-permute-start.2 = (bf16[136,512]{1,0:T(8,128)(2,1)}, bf16[136,512]{1,0:T(8,128)(2,1)S(1)}, u32[]{:S(2)}, u32[]{:S(2)}) collective-permute-start(bf16[136,512]{1,0:T(8,128)(2,1)} %bitcast.34), channel_id=1, source_target_pairs={{0,3},{1,2},{2,1},{3,0},{4,7},{5,6},{6,5},{7,4},{8,11},{9,10},{10,... | collective-permute-start | bytes 417800 | tf_op jit(solution)/shard_map/ppermute | solution.py:333
  3.1 4.5 %collective-permute-start.1 = (f32[3,2,1,512]{3,2,1,0:T(1,128)}, f32[3,2,1,512]{3,2,1,0:T(1,128)S(1)}, u32[]{:S(2)}, u32[]{:S(2)}) collective-permute-start(f32[3,2,1,512]{3,2,1,0:T(1,128)} %sky.1), channel_id=1, source_target_pairs={{0,3},{1,2},{2,1},{3,0},{4,7},{5,6},{6,5},{7,4},{8,11},{9,10},{10,... | collective-permute-start | bytes 36872 | tf_op jit(solution)/shard_map/ppermute | solution.py:333
  3.1 1.0 %copy-start.1 = (bf16[1,3,2,17,2048]{4,2,3,1,0:T(2,128)(2,1)S(1)}, bf16[1,3,2,17,2048]{4,2,3,1,0:T(2,128)(2,1)}, u32[]{:S(2)}) copy-start(bf16[1,3,2,17,2048]{4,2,3,1,0:T(2,128)(2,1)} %param.11) | copy-start | bytes 1253380
  4.2 0.9 %copy-start.2 = (bf16[1,17,512,8]{2,3,1,0:T(8,128)(2,1)S(1)}, bf16[1,17,512,8]{2,3,1,0:T(8,128)(2,1)}, u32[]{:S(2)}) copy-start(bf16[1,17,512,8]{2,3,1,0:T(8,128)(2,1)} %param.12) | copy-start | bytes 417796
  4.3 0.9 %copy-start.7 = (f32[3,2,1,512]{3,2,1,0:T(1,128)S(1)}, f32[3,2,1,512]{3,2,1,0:T(1,128)}, u32[]{:S(2)}) copy-start(f32[3,2,1,512]{3,2,1,0:T(1,128)} %sky.1) | copy-start | bytes 36868
  7.6 2.9 %copy-start = (f32[2,1,4096]{2,1,0:T(1,128)S(1)}, f32[2,1,4096]{2,1,0:T(1,128)}, u32[]{:S(2)}) copy-start(f32[2,1,4096]{2,1,0:T(1,128)} %param.19) | copy-start | bytes 98308
  7.6 2.9 %copy-start.4 = (s32[1,4096]{1,0:T(1,128)S(1)}, s32[1,4096]{1,0:T(1,128)}, u32[]{:S(2)}) copy-start(s32[1,4096]{1,0:T(1,128)} %param.17) | copy-start | bytes 49156
  7.6 2.9 %copy-start.5 = (s32[1,4096]{1,0:T(1,128)S(1)}, s32[1,4096]{1,0:T(1,128)}, u32[]{:S(2)}) copy-start(s32[1,4096]{1,0:T(1,128)} %param.18) | copy-start | bytes 49156
  8.0 2.6 %copy-start.3 = (s32[1,4096]{1,0:T(1,128)S(1)}, s32[1,4096]{1,0:T(1,128)}, u32[]{:S(2)}) copy-start(s32[1,4096]{1,0:T(1,128)} %param.16) | copy-start | bytes 49156
  8.0 1.2 %collective-permute-start.3 = (f32[2,2,256]{2,1,0:T(2,128)S(1)}, f32[2,2,256]{2,1,0:T(2,128)S(1)}, u32[]{:S(2)}, u32[]{:S(2)}) collective-permute-start(f32[2,2,256]{2,1,0:T(2,128)S(1)} %shard_map.103), channel_id=1, source_target_pairs={{0,1},{1,0},{2,3},{3,2},{4,5},{5,4},{6,7},{7,6},{8,9},{9,8},{10,11... | collective-permute-start | bytes 12296 | tf_op jit(solution)/shard_map/ppermute | solution.py:333
  9.2 3.0 %collective-permute-start.4 = (bf16[2,2,256]{2,1,0:T(2,128)(2,1)S(1)}, bf16[2,2,256]{2,1,0:T(2,128)(2,1)S(1)}, u32[]{:S(2)}, u32[]{:S(2)}) collective-permute-start(bf16[2,2,256]{2,1,0:T(2,128)(2,1)S(1)} %add_convert_fusion), channel_id=1, source_target_pairs={{0,5},{1,4},{2,7},{3,6},{4,1},{5,0},{6,3},{7,2},{8,13},{9,12},{10,... | collective-permute-start | bytes 6152 | tf_op jit(solution)/shard_map/ppermute | solution.py:333
  10.5 0.7 %copy-start.6 = (s32[1,8,8,2]{2,3,1,0:T(2,128)S(1)}, s32[1,8,8,2]{2,3,1,0:T(2,128)}, u32[]{:S(2)}) copy-start(s32[1,8,8,2]{2,3,1,0:T(2,128)} %param.15) | copy-start | bytes 1540
  10.5 0.7 %copy-start.8 = (s32[8,3]{0,1:T(4,128)S(1)}, s32[8,3]{0,1:T(4,128)}, u32[]{:S(2)}) copy-start(s32[8,3]{0,1:T(4,128)} %param.14) | copy-start | bytes 292
  10.5 0.7 %copy-start.9 = (s32[8]{0:T(128)S(1)}, s32[8]{0:T(128)}, u32[]{:S(2)}) copy-start(s32[8]{0:T(128)} %param.13) | copy-start | bytes 100
  12.2 3.1 %collective-permute-start.5 = (bf16[2,2,2,256]{3,2,1,0:T(2,128)(2,1)S(1)}, bf16[2,2,2,256]{3,2,1,0:T(2,128)(2,1)S(1)}, u32[]{:S(2)}, u32[]{:S(2)}) collective-permute-start(bf16[2,2,2,256]{3,2,1,0:T(2,128)(2,1)S(1)} %pad_maximum_fusion.held), channel_id=1, source_target_pairs={{0,9},{1,8},{2,11},{3,10},{4,13},{5,12},{6,15},{7,14},{8,1},{9,0},... | collective-permute-start | bytes 12296 | tf_op jit(solution)/shard_map/ppermute | solution.py:333
  15.4 4.0 %collective-permute-start.6 = (bf16[4,2,256]{2,1,0:T(2,128)(2,1)S(1)}, bf16[4,2,256]{2,1,0:T(2,128)(2,1)S(1)}, u32[]{:S(2)}, u32[]{:S(2)}) collective-permute-start(bf16[4,2,256]{2,1,0:T(2,128)(2,1)S(1)} %pad_maximum_fusion.1), channel_id=1, source_target_pairs={{0,17},{1,16},{2,19},{3,18},{4,21},{5,20},{6,23},{7,22},{8,25},{9,... | collective-permute-start | bytes 12296 | tf_op jit(solution)/shard_map/ppermute | solution.py:333

commit v9 on v8

--- a/solution.py
+++ b/solution.py
@@ -183,10 +183,7 @@
                     kept = here & (code >= slot * NPHI)
                     cycle = jnp.where(kept, cycles[slot : slot + 1, source : source + 1], cycle)
         if index:
-            low, high = index
-            cell = psi[h : h + eight, :]
-            low[h : h + eight, :] = cycle * NPSI + cell
-            high[h : h + eight, :] = cycle * NPSI + ((cell + 1) & (NPSI - 1))
+            index[0][h : h + eight, :] = cycle * NPSI + psi[h : h + eight, :]
         first = ((start + phi[h : h + eight, :]) & (NPHI - 1)).astype(jnp.float32)
         for g in range(eight):
             f = frac[0, h + g : h + g + 1, :]
@@ -259,18 +256,25 @@
             out[side, s : s + 1, :] = jnp.sum(held * weights[s], 0, keepdims=True)
 
 
-def half_sum(part, phase, low, high, frac, g):
-    shape = (part.shape[0], LANES)
-    at_low = pick_lanes(part, jnp.broadcast_to(low[g : g + 1, :], shape))
-    at_high = pick_lanes(part, jnp.broadcast_to(high[g : g + 1, :], shape))
-    return (at_low + frac[1, g : g + 1, :] * (at_high - at_low)) * phase[g]
-
-
-def first_half_kernel(held, received, phase, low, high, frac, out):
+def to_next_psi(part):
+    width = part.shape[1]
+    last = lax.broadcasted_iota(jnp.int32, part.shape, 1) & (NPSI - 1) == NPSI - 1
+    after = jnp.where(last, pltpu.roll(part, NPSI - 1, 1), pltpu.roll(part, width - 1, 1))
+    return after - part
+
+
+def half_sum(part, change, phase, low, frac, g):
+    at = jnp.broadcast_to(low[g : g + 1, :], (part.shape[0], LANES))
+    value = pick_lanes(part, at) + frac[1, g : g + 1, :] * pick_lanes(change, at)
+    return value * phase[g]
+
+
+def first_half_kernel(held, received, phase, low, frac, out):
     parts = (held[0, 0], held[1, 1], received[0, 1], received[1, 0])
     part = jnp.concatenate([rows.astype(jnp.float32) for rows in parts], 0)
+    change = to_next_psi(part)
     for g in range(out.shape[0]):
-        out[g] = half_sum(part, phase, low, high, frac, g)
+        out[g] = half_sum(part, change, phase, low, frac, g)
 
 
 def row_sums(tiles):
@@ -284,11 +288,12 @@
     return tiles[0]
 
 
-def second_half_kernel(received, first, phase, low, high, frac, out):
+def second_half_kernel(received, first, phase, low, frac, out):
     part = jnp.concatenate([received[k].astype(jnp.float32) for k in range(received.shape[0])], 0)
+    change = to_next_psi(part)
     for g in range(0, out.shape[0], 8):
         totals = [
-            first[k] + half_sum(part, phase, low, high, frac, k) for k in range(g, g + 8)
+            first[k] + half_sum(part, change, phase, low, frac, k) for k in range(g, g + 8)
         ]
         out[g : g + 8, :] = row_sums(totals)
 
@@ -360,8 +365,8 @@
     lists = (m_values.reshape(1, -1), cycle_table.T, jnp.transpose(send_lists[0], (0, 2, 1)))
     samples = (*lists, *(a.reshape(groups, LANES) for a in where), frac)
     late, _ = lax.optimization_barrier((samples[0], rows))
-    near, low, high = call(
-        functools.partial(sample_kernel, 0), (weights, index, index), [vmem()] * 7
+    near, low = call(
+        functools.partial(sample_kernel, 0), (weights, index), [vmem()] * 7
     )(late, *samples[1:])
     rows_y, near = lax.optimization_barrier((rows_y, near))
     pair = jnp.stack([rows, rows_y])
@@ -370,10 +375,10 @@
     far = call(functools.partial(sample_kernel, 1), weights, [vmem()] * 7)(late, *samples[1:])
     pair_z, far = lax.optimization_barrier((pair_z, far))
     rest = swap(jnp.stack([pair[0, 1], pair[1, 0], pair_z[0, 0], pair_z[1, 1]]), 4, 1)
-    first = call(first_half_kernel, weights, [vmem()] * 6)(pair, pair_z, near, low, high, frac)
+    first = call(first_half_kernel, weights, [vmem()] * 5)(pair, pair_z, near, low, frac)
     values = call(
-        second_half_kernel, jax.ShapeDtypeStruct((groups, LANES), f32), [vmem()] * 6
-    )(rest, first, far, low, high, frac)
+        second_half_kernel, jax.ShapeDtypeStruct((groups, LANES), f32), [vmem()] * 5
+    )(rest, first, far, low, frac)
     return values.reshape(1, -1)
 
 

time: 20.6 us -> 20.5 us (level)
  transfers between devices with their start and end apart: 7 -> 7, of which waited for: 5 -> 5; matrix products, arithmetic and copies ran while one was open for 0% -> 0% of each run, Pallas kernels for 9% -> 8%
where the time goes in v9:
time: 20.5 us; the launch traced here: 20.3 us
  starting transfers between devices  8.34 us (41%)
  waiting for transfers between devices  6.36 us (31%)
  Pallas kernels  3.07 us (15%)
  local copies, waits for them, and re-layouts  2.41 us (12%)
    ppermute x7, starting transfers between devices, swap(): return lax.ppermute(x, ('band', 'det'), pairs)  8.34 us
    ppermute x7, waiting for transfers between devices, swap(): return lax.ppermute(x, ('band', 'det'), pairs)  6.36 us
    unnamed x20, local copies, waits for them, and re-layouts  2.4 us
    pallas_call x1, Pallas kernels, by_samples(): call(second_half_kernel, jax.ShapeDtypeStruct((groups, LANES), f32), [vme...  0.98 us
    pallas_call x1, Pallas kernels, by_samples(): call(functools.partial(sample_kernel, 0), (weights, index), [vmem()] * 7)  0.53 us
  transfers between devices with their start and end apart: 7, of which 5 were waited for; matrix products, arithmetic and copies ran while one was open for 0% of the time, Pallas kernels for 8%

profile of v9, /device:TPU:0, one launch (start us, length us, event | category | flops | bytes accessed | tf_op | source)
XLA Modules:
  0.0 20.3 jit_solution(13903377586845569416)
XLA Ops:
  0.0 0.5 %collective-permute-start = (bf16[3,17,2,2048]{3,2,1,0:T(2,128)(2,1)}, bf16[3,17,2,2048]{3,2,1,0:T(2,128)(2,1)S(1)}, u32[]{:S(2)}, u32[]{:S(2)}) collective-permute-start(bf16[3,17,2,2048]{3,2,1,0:T(2,128)(2,1)} %bitcast.32), channel_id=1, source_target_pairs={{0,1},{1,0},{2,3},{3,2},{4,5},{5,4},{6,7},{7,6},{8,9},{9,8},{10,11... | collective-permute-start | bytes 1253384 | tf_op jit(solution)/shard_map/ppermute | solution.py:338
  0.5 2.6 %collective-permute-start.2 = (bf16[136,512]{1,0:T(8,128)(2,1)}, bf16[136,512]{1,0:T(8,128)(2,1)S(1)}, u32[]{:S(2)}, u32[]{:S(2)}) collective-permute-start(bf16[136,512]{1,0:T(8,128)(2,1)} %bitcast.34), channel_id=1, source_target_pairs={{0,3},{1,2},{2,1},{3,0},{4,7},{5,6},{6,5},{7,4},{8,11},{9,10},{10,... | collective-permute-start | bytes 417800 | tf_op jit(solution)/shard_map/ppermute | solution.py:338
  3.1 0.0 collective-permute-start.1
  3.1 0.0 copy-start.1
  3.1 1.0 %copy-done.1 = bf16[1,3,2,17,2048]{4,2,3,1,0:T(2,128)(2,1)S(1)} copy-done((bf16[1,3,2,17,2048]{4,2,3,1,0:T(2,128)(2,1)S(1)}, bf16[1,3,2,17,2048]{4,2,3,1,0:T(2,128)(2,1)}, u32[]{:S(2)}) %copy-start.1) | copy-done | bytes 417816
  4.1 0.1 shard_map.100.beam_own
  4.2 0.0 copy-start.2
  4.3 0.0 copy-start.7
  4.3 0.0 collective-permute-done.source
  4.3 0.1 shard_map.101.beam_other
  4.4 0.7 %copy-done.2 = bf16[1,17,512,8]{2,3,1,0:T(8,128)(2,1)S(1)} copy-done((bf16[1,17,512,8]{2,3,1,0:T(8,128)(2,1)S(1)}, bf16[1,17,512,8]{2,3,1,0:T(8,128)(2,1)}, u32[]{:S(2)}) %copy-start.2) | copy-done | bytes 139288
  5.1 0.0 copy-done.7
  5.2 0.2 %shard_map.102 = (f32[96,136]{1,0:T(8,128)S(1)}, f32[2,48,256]{2,1,0:T(8,128)S(1)}) custom-call(f32[3,2,24,1024]{3,2,1,0:T(8,128)S(1)} %shard_map.100.beam_own, f32[3,2,24,1024]{3,2,1,0:T(8,128)S(1)} %shard_map.101.beam_other, f32[3,2,1,512]{3,2,1,0:T(1,128)S(1)} %copy-done.7, bf16[136,512]{1,0:T(8,128)(2,1)S(1)} %bitcast.35), custom_call_target="tpu_custom_call" | custom-call | flops 1 | bytes 1 | tf_op jit(solution)/shard_map/pallas_call | solution.py:348
  5.4 2.2 %collective-permute-done.1.sky = f32[3,2,1,512]{3,2,1,0:T(1,128)S(1)} collective-permute-done((f32[3,2,1,512]{3,2,1,0:T(1,128)}, f32[3,2,1,512]{3,2,1,0:T(1,128)S(1)}, u32[]{:S(2)}, u32[]{:S(2)}) %collective-permute-start.1) | collective-permute-done | bytes 12320 | tf_op jit(solution)/shard_map/ppermute | solution.py:338
  7.6 0.0 collective-permute-done.2.w
  7.6 0.0 copy-start
  7.6 0.0 copy-start.4
  7.6 0.0 copy-start.5
  7.6 0.4 %shard_map.103 = f32[2,2,256]{2,1,0:T(2,128)S(1)} custom-call(f32[3,2,24,1024]{3,2,1,0:T(8,128)S(1)} %shard_map.100.beam_own, f32[3,2,24,1024]{3,2,1,0:T(8,128)S(1)} %shard_map.101.beam_other, f32[3,2,1,512]{3,2,1,0:T(1,128)S(1)} %collective-permute-done.1.sky, bf16[136,512]{1,0:T(8,128)(2,1)S(1)} %collective-permute-done.2.w, ...), custom_call_target="tpu_custom_call" | custom-call | flops 1 | bytes 1 | tf_op jit(solution)/shard_map/pallas_call | solution.py:356
  8.0 0.0 copy-start.3
  8.0 0.2 collective-permute-start.3
  8.2 1.1 %collective-permute-done.3 = f32[2,2,256]{2,1,0:T(2,128)S(1)} collective-permute-done((f32[2,2,256]{2,1,0:T(2,128)S(1)}, f32[2,2,256]{2,1,0:T(2,128)S(1)}, u32[]{:S(2)}, u32[]{:S(2)}) %collective-permute-start.3) | collective-permute-done | bytes 4128 | tf_op jit(solution)/shard_map/ppermute | solution.py:338
  9.2 1.3 %collective-permute-start.4 = (bf16[2,2,256]{2,1,0:T(2,128)(2,1)S(1)}, bf16[2,2,256]{2,1,0:T(2,128)(2,1)S(1)}, u32[]{:S(2)}, u32[]{:S(2)}) collective-permute-start(bf16[2,2,256]{2,1,0:T(2,128)(2,1)S(1)} %add_convert_fusion), channel_id=1, source_target_pairs={{0,5},{1,4},{2,7},{3,6},{4,1},{5,0},{6,3},{7,2},{8,13},{9,12},{10,... | collective-permute-start | bytes 6152 | tf_op jit(solution)/shard_map/ppermute | solution.py:338
  10.5 0.0 copy-start.6
  10.5 0.0 copy-start.8
  10.5 0.0 copy-start.9
  10.5 0.0 copy-done
  10.5 0.0 copy-done.4
  10.5 0.0 copy-done.5
  10.5 0.0 copy-done.3
  10.5 0.6 %copy-done.6 = s32[1,8,8,2]{2,3,1,0:T(2,128)S(1)} copy-done((s32[1,8,8,2]{2,3,1,0:T(2,128)S(1)}, s32[1,8,8,2]{2,3,1,0:T(2,128)}, u32[]{:S(2)}) %copy-start.6) | copy-done | bytes 536
  11.2 0.0 copy-done.8
  11.2 0.0 copy-done.9
  11.2 0.5 %shard_map.104 = (f32[32,8,128]{2,1,0:T(8,128)S(1)}, s32[32,128]{1,0:T(8,128)S(1)}) custom-call(s32[1,8]{1,0:T(1,128)S(1)} %bitcast.46, s32[3,8]{1,0:T(4,128)S(1)} %bitcast.44, s32[8,2,8]{2,1,0:T(2,128)S(1)} %bitcast.42, s32[32,128]{1,0:T(8,128)S(1)} %bitcast.36, s32[32,128]{1,0:T(8,128)S(1)} %bitcast.38, s32[32,128]{1,0:T(8,128)S(1)} %bitcast.40, ...), custom_call_target="tpu_custom_call" | custom-call | flops 1 | bytes 1 | tf_op jit(solution)/shard_map/pallas_call | solution.py:368
  11.7 0.5 %collective-permute-done.4 = bf16[2,2,256]{2,1,0:T(2,128)(2,1)S(1)} collective-permute-done((bf16[2,2,256]{2,1,0:T(2,128)(2,1)S(1)}, bf16[2,2,256]{2,1,0:T(2,128)(2,1)S(1)}, u32[]{:S(2)}, u32[]{:S(2)}) %collective-permute-start.4) | collective-permute-done | bytes 2080 | tf_op jit(solution)/shard_map/ppermute | solution.py:338
  12.2 1.4 %collective-permute-start.5 = (bf16[2,2,2,256]{3,2,1,0:T(2,128)(2,1)S(1)}, bf16[2,2,2,256]{3,2,1,0:T(2,128)(2,1)S(1)}, u32[]{:S(2)}, u32[]{:S(2)}) collective-permute-start(bf16[2,2,2,256]{3,2,1,0:T(2,128)(2,1)S(1)} %pad_maximum_fusion.held), channel_id=1, source_target_pairs={{0,9},{1,8},{2,11},{3,10},{4,13},{5,12},{6,15},{7,14},{8,1},{9,0},... | collective-permute-start | bytes 12296 | tf_op jit(solution)/shard_map/ppermute | solution.py:338
  13.6 0.3 %shard_map.105.phase = f32[32,8,128]{2,1,0:T(8,128)S(1)} custom-call(s32[1,8]{1,0:T(1,128)S(1)} %bitcast.47, s32[3,8]{1,0:T(4,128)S(1)} %bitcast.45, s32[8,2,8]{2,1,0:T(2,128)S(1)} %bitcast.43, s32[32,128]{1,0:T(8,128)S(1)} %bitcast.37, s32[32,128]{1,0:T(8,128)S(1)} %bitcast.39, s32[32,128]{1,0:T(8,128)S(1)} %bitcast.41, f32[2,32,128]{2,1,0:T(8,128)S(1)} %bitcast.29), custom_call_target="tpu_custom_call" | custom-call | flops 1 | bytes 1 | tf_op jit(solution)/shard_map/pallas_call | solution.py:375
  14.0 1.4 %collective-permute-done.5.received = bf16[2,2,2,256]{3,2,1,0:T(2,128)(2,1)S(1)} collective-permute-done((bf16[2,2,2,256]{3,2,1,0:T(2,128)(2,1)S(1)}, bf16[2,2,2,256]{3,2,1,0:T(2,128)(2,1)S(1)}, u32[]{:S(2)}, u32[]{:S(2)}) %collective-permute-start.5) | collective-permute-done | bytes 4128 | tf_op jit(solution)/shard_map/ppermute | solution.py:338
  15.4 2.4 %collective-permute-start.6 = (bf16[4,2,256]{2,1,0:T(2,128)(2,1)S(1)}, bf16[4,2,256]{2,1,0:T(2,128)(2,1)S(1)}, u32[]{:S(2)}, u32[]{:S(2)}) collective-permute-start(bf16[4,2,256]{2,1,0:T(2,128)(2,1)S(1)} %pad_maximum_fusion.1), channel_id=1, source_target_pairs={{0,17},{1,16},{2,19},{3,18},{4,21},{5,20},{6,23},{7,22},{8,25},{9,... | collective-permute-start | bytes 12296 | tf_op jit(solution)/shard_map/ppermute | solution.py:338
  17.8 0.4 %shard_map.106.first = f32[32,8,128]{2,1,0:T(8,128)S(1)} custom-call(bf16[2,2,2,256]{3,2,1,0:T(2,128)(2,1)S(1)} %pad_maximum_fusion.held, bf16[2,2,2,256]{3,2,1,0:T(2,128)(2,1)S(1)} %collective-permute-done.5.received, f32[32,8,128]{2,1,0:T(8,128)S(1)} %get-tuple-element.22.phase, s32[32,128]{1,0:T(8,128)S(1)} %get-tuple-element.23.low, ...), custom_call_target="tpu_custom_call" | custom-call | flops 1 | bytes 1 | tf_op jit(solution)/shard_map/pallas_call | solution.py:378
  18.1 1.2 %collective-permute-done.6.received = bf16[4,2,256]{2,1,0:T(2,128)(2,1)S(1)} collective-permute-done((bf16[4,2,256]{2,1,0:T(2,128)(2,1)S(1)}, bf16[4,2,256]{2,1,0:T(2,128)(2,1)S(1)}, u32[]{:S(2)}, u32[]{:S(2)}) %collective-permute-start.6) | collective-permute-done | bytes 4128 | tf_op jit(solution)/shard_map/ppermute | solution.py:338
  19.4 1.0 %shard_map.107 = f32[32,128]{1,0:T(8,128)} custom-call(bf16[4,2,256]{2,1,0:T(2,128)(2,1)S(1)} %collective-permute-done.6.received, f32[32,8,128]{2,1,0:T(8,128)S(1)} %shard_map.106.first, f32[32,8,128]{2,1,0:T(8,128)S(1)} %shard_map.105.phase, s32[32,128]{1,0:T(8,128)S(1)} %get-tuple-element.23.low, f32[2,32,128]{2,1,0:T(8,128)S(1)} %bitcast.31), custom_call_target="tpu_custom_call" | custom-call | flops 1 | bytes 1 | tf_op jit(solution)/shard_map/pallas_call | solution.py:379
  (6 shorter events, 0.0 us)
Async XLA Ops:
  0.0 4.3 %collective-permute-start = (bf16[3,17,2,2048]{3,2,1,0:T(2,128)(2,1)}, bf16[3,17,2,2048]{3,2,1,0:T(2,128)(2,1)S(1)}, u32[]{:S(2)}, u32[]{:S(2)}) collective-permute-start(bf16[3,17,2,2048]{3,2,1,0:T(2,128)(2,1)} %bitcast.32), channel_id=1, source_target_pairs={{0,1},{1,0},{2,3},{3,2},{4,5},{5,4},{6,7},{7,6},{8,9},{9,8},{10,11... | collective-permute-start | bytes 1253384 | tf_op jit(solution)/shard_map/ppermute | solution.py:338
  0.5 7.1 %collective-permute-start.2 = (bf16[136,512]{1,0:T(8,128)(2,1)}, bf16[136,512]{1,0:T(8,128)(2,1)S(1)}, u32[]{:S(2)}, u32[]{:S(2)}) collective-permute-start(bf16[136,512]{1,0:T(8,128)(2,1)} %bitcast.34), channel_id=1, source_target_pairs={{0,3},{1,2},{2,1},{3,0},{4,7},{5,6},{6,5},{7,4},{8,11},{9,10},{10,... | collective-permute-start | bytes 417800 | tf_op jit(solution)/shard_map/ppermute | solution.py:338
  3.1 4.5 %collective-permute-start.1 = (f32[3,2,1,512]{3,2,1,0:T(1,128)}, f32[3,2,1,512]{3,2,1,0:T(1,128)S(1)}, u32[]{:S(2)}, u32[]{:S(2)}) collective-permute-start(f32[3,2,1,512]{3,2,1,0:T(1,128)} %sky.1), channel_id=1, source_target_pairs={{0,3},{1,2},{2,1},{3,0},{4,7},{5,6},{6,5},{7,4},{8,11},{9,10},{10,... | collective-permute-start | bytes 36872 | tf_op jit(solution)/shard_map/ppermute | solution.py:338
  3.1 1.0 %copy-start.1 = (bf16[1,3,2,17,2048]{4,2,3,1,0:T(2,128)(2,1)S(1)}, bf16[1,3,2,17,2048]{4,2,3,1,0:T(2,128)(2,1)}, u32[]{:S(2)}) copy-start(bf16[1,3,2,17,2048]{4,2,3,1,0:T(2,128)(2,1)} %param.11) | copy-start | bytes 1253380
  4.2 0.9 %copy-start.2 = (bf16[1,17,512,8]{2,3,1,0:T(8,128)(2,1)S(1)}, bf16[1,17,512,8]{2,3,1,0:T(8,128)(2,1)}, u32[]{:S(2)}) copy-start(bf16[1,17,512,8]{2,3,1,0:T(8,128)(2,1)} %param.12) | copy-start | bytes 417796
  4.3 0.9 %copy-start.7 = (f32[3,2,1,512]{3,2,1,0:T(1,128)S(1)}, f32[3,2,1,512]{3,2,1,0:T(1,128)}, u32[]{:S(2)}) copy-start(f32[3,2,1,512]{3,2,1,0:T(1,128)} %sky.1) | copy-start | bytes 36868
  7.6 2.9 %copy-start = (f32[2,1,4096]{2,1,0:T(1,128)S(1)}, f32[2,1,4096]{2,1,0:T(1,128)}, u32[]{:S(2)}) copy-start(f32[2,1,4096]{2,1,0:T(1,128)} %param.19) | copy-start | bytes 98308
  7.6 2.9 %copy-start.4 = (s32[1,4096]{1,0:T(1,128)S(1)}, s32[1,4096]{1,0:T(1,128)}, u32[]{:S(2)}) copy-start(s32[1,4096]{1,0:T(1,128)} %param.17) | copy-start | bytes 49156
  7.6 2.9 %copy-start.5 = (s32[1,4096]{1,0:T(1,128)S(1)}, s32[1,4096]{1,0:T(1,128)}, u32[]{:S(2)}) copy-start(s32[1,4096]{1,0:T(1,128)} %param.18) | copy-start | bytes 49156
  8.0 2.6 %copy-start.3 = (s32[1,4096]{1,0:T(1,128)S(1)}, s32[1,4096]{1,0:T(1,128)}, u32[]{:S(2)}) copy-start(s32[1,4096]{1,0:T(1,128)} %param.16) | copy-start | bytes 49156
  8.0 1.2 %collective-permute-start.3 = (f32[2,2,256]{2,1,0:T(2,128)S(1)}, f32[2,2,256]{2,1,0:T(2,128)S(1)}, u32[]{:S(2)}, u32[]{:S(2)}) collective-permute-start(f32[2,2,256]{2,1,0:T(2,128)S(1)} %shard_map.103), channel_id=1, source_target_pairs={{0,1},{1,0},{2,3},{3,2},{4,5},{5,4},{6,7},{7,6},{8,9},{9,8},{10,11... | collective-permute-start | bytes 12296 | tf_op jit(solution)/shard_map/ppermute | solution.py:338
  9.2 3.0 %collective-permute-start.4 = (bf16[2,2,256]{2,1,0:T(2,128)(2,1)S(1)}, bf16[2,2,256]{2,1,0:T(2,128)(2,1)S(1)}, u32[]{:S(2)}, u32[]{:S(2)}) collective-permute-start(bf16[2,2,256]{2,1,0:T(2,128)(2,1)S(1)} %add_convert_fusion), channel_id=1, source_target_pairs={{0,5},{1,4},{2,7},{3,6},{4,1},{5,0},{6,3},{7,2},{8,13},{9,12},{10,... | collective-permute-start | bytes 6152 | tf_op jit(solution)/shard_map/ppermute | solution.py:338
  10.5 0.7 %copy-start.6 = (s32[1,8,8,2]{2,3,1,0:T(2,128)S(1)}, s32[1,8,8,2]{2,3,1,0:T(2,128)}, u32[]{:S(2)}) copy-start(s32[1,8,8,2]{2,3,1,0:T(2,128)} %param.15) | copy-start | bytes 1540
  10.5 0.7 %copy-start.8 = (s32[8,3]{0,1:T(4,128)S(1)}, s32[8,3]{0,1:T(4,128)}, u32[]{:S(2)}) copy-start(s32[8,3]{0,1:T(4,128)} %param.14) | copy-start | bytes 292
  10.5 0.7 %copy-start.9 = (s32[8]{0:T(128)S(1)}, s32[8]{0:T(128)}, u32[]{:S(2)}) copy-start(s32[8]{0:T(128)} %param.13) | copy-start | bytes 100
  12.2 3.1 %collective-permute-start.5 = (bf16[2,2,2,256]{3,2,1,0:T(2,128)(2,1)S(1)}, bf16[2,2,2,256]{3,2,1,0:T(2,128)(2,1)S(1)}, u32[]{:S(2)}, u32[]{:S(2)}) collective-permute-start(bf16[2,2,2,256]{3,2,1,0:T(2,128)(2,1)S(1)} %pad_maximum_fusion.held), channel_id=1, source_target_pairs={{0,9},{1,8},{2,11},{3,10},{4,13},{5,12},{6,15},{7,14},{8,1},{9,0},... | collective-permute-start | bytes 12296 | tf_op jit(solution)/shard_map/ppermute | solution.py:338
  15.4 4.0 %collective-permute-start.6 = (bf16[4,2,256]{2,1,0:T(2,128)(2,1)S(1)}, bf16[4,2,256]{2,1,0:T(2,128)(2,1)S(1)}, u32[]{:S(2)}, u32[]{:S(2)}) collective-permute-start(bf16[4,2,256]{2,1,0:T(2,128)(2,1)S(1)} %pad_maximum_fusion.1), channel_id=1, source_target_pairs={{0,17},{1,16},{2,19},{3,18},{4,21},{5,20},{6,23},{7,22},{8,25},{9,... | collective-permute-start | bytes 12296 | tf_op jit(solution)/shard_map/ppermute | solution.py:338

commit v10 on v9

--- a/solution.py
+++ b/solution.py
@@ -158,9 +158,9 @@
 
 
 def sample_kernel(half, orders, cycles, lists, block, phi, psi, frac, phase, *index):
-    scale = 2.0 / math.sqrt(phase.shape[1] * MPRIME)
+    scale = 2.0 / math.sqrt(phase.shape[2] * MPRIME)
     band = lax.axis_index("band")
-    eight = phase.shape[1]
+    eight = phase.shape[2]
     row = lax.broadcasted_iota(jnp.int32, (eight, LANES), 0)
     orders = jnp.broadcast_to(orders[...], (eight, orders.shape[1]))
     order = own_lanes(orders, band ^ (half * (eight // 2) + row // 2))
@@ -190,7 +190,9 @@
             here = step * first[g : g + 1, :] + quarter
             at = cosine(here).astype(jnp.bfloat16).astype(jnp.float32)
             after = cosine(here + step).astype(jnp.bfloat16).astype(jnp.float32)
-            phase[h + g] = (at + f * (after - at)) * scale
+            weight = (at + f * (after - at)) * scale
+            phase[0, h + g] = weight
+            phase[1, h + g] = weight * frac[1, h + g : h + g + 1, :]
 
 
 def pick_lanes(values, column):
@@ -263,18 +265,17 @@
     return after - part
 
 
-def half_sum(part, change, phase, low, frac, g):
+def half_sum(part, change, phase, low, g):
     at = jnp.broadcast_to(low[g : g + 1, :], (part.shape[0], LANES))
-    value = pick_lanes(part, at) + frac[1, g : g + 1, :] * pick_lanes(change, at)
-    return value * phase[g]
-
-
-def first_half_kernel(held, received, phase, low, frac, out):
+    return pick_lanes(part, at) * phase[0, g] + pick_lanes(change, at) * phase[1, g]
+
+
+def first_half_kernel(held, received, phase, low, out):
     parts = (held[0, 0], held[1, 1], received[0, 1], received[1, 0])
     part = jnp.concatenate([rows.astype(jnp.float32) for rows in parts], 0)
     change = to_next_psi(part)
     for g in range(out.shape[0]):
-        out[g] = half_sum(part, change, phase, low, frac, g)
+        out[g] = half_sum(part, change, phase, low, g)
 
 
 def row_sums(tiles):
@@ -288,12 +289,12 @@
     return tiles[0]
 
 
-def second_half_kernel(received, first, phase, low, frac, out):
+def second_half_kernel(received, first, phase, low, out):
     part = jnp.concatenate([received[k].astype(jnp.float32) for k in range(received.shape[0])], 0)
     change = to_next_psi(part)
     for g in range(0, out.shape[0], 8):
         totals = [
-            first[k] + half_sum(part, change, phase, low, frac, k) for k in range(g, g + 8)
+            first[k] + half_sum(part, change, phase, low, k) for k in range(g, g + 8)
         ]
         out[g : g + 8, :] = row_sums(totals)
 
@@ -360,25 +361,26 @@
     rows_y = swap(rows, 1, 1)
     weights = jax.ShapeDtypeStruct((groups, bands, LANES), f32)
     index = jax.ShapeDtypeStruct((groups, LANES), jnp.int32)
+    two = jax.ShapeDtypeStruct((2, *weights.shape), f32)
     frac = sample_frac.reshape(2, groups, LANES)
     where = (sample_block, sample_phi, sample_psi)
     lists = (m_values.reshape(1, -1), cycle_table.T, jnp.transpose(send_lists[0], (0, 2, 1)))
     samples = (*lists, *(a.reshape(groups, LANES) for a in where), frac)
     late, _ = lax.optimization_barrier((samples[0], rows))
     near, low = call(
-        functools.partial(sample_kernel, 0), (weights, index), [vmem()] * 7
+        functools.partial(sample_kernel, 0), (two, index), [vmem()] * 7
     )(late, *samples[1:])
     rows_y, near = lax.optimization_barrier((rows_y, near))
     pair = jnp.stack([rows, rows_y])
     pair_z = swap(pair, 2, 1)
     late, _ = lax.optimization_barrier((samples[0], pair))
-    far = call(functools.partial(sample_kernel, 1), weights, [vmem()] * 7)(late, *samples[1:])
+    far = call(functools.partial(sample_kernel, 1), two, [vmem()] * 7)(late, *samples[1:])
     pair_z, far = lax.optimization_barrier((pair_z, far))
     rest = swap(jnp.stack([pair[0, 1], pair[1, 0], pair_z[0, 0], pair_z[1, 1]]), 4, 1)
-    first = call(first_half_kernel, weights, [vmem()] * 5)(pair, pair_z, near, low, frac)
+    first = call(first_half_kernel, weights, [vmem()] * 4)(pair, pair_z, near, low)
     values = call(
-        second_half_kernel, jax.ShapeDtypeStruct((groups, LANES), f32), [vmem()] * 5
-    )(rest, first, far, low, frac)
+        second_half_kernel, jax.ShapeDtypeStruct((groups, LANES), f32), [vmem()] * 4
+    )(rest, first, far, low)
     return values.reshape(1, -1)
 
 

time: 20.5 us -> 20.5 us (level)
  transfers between devices with their start and end apart: 7 -> 7, of which waited for: 5 -> 5; matrix products, arithmetic and copies ran while one was open for 0% -> 0% of each run, Pallas kernels for 8% -> 9%
where the time goes in v10:
time: 20.5 us; the launch traced here: 20.3 us
  starting transfers between devices  8.34 us (41%)
  waiting for transfers between devices  6.34 us (31%)
  Pallas kernels  3.07 us (15%)
  local copies, waits for them, and re-layouts  2.41 us (12%)
    ppermute x7, starting transfers between devices, swap(): return lax.ppermute(x, ('band', 'det'), pairs)  8.34 us
    ppermute x7, waiting for transfers between devices, swap(): return lax.ppermute(x, ('band', 'det'), pairs)  6.34 us
    unnamed x20, local copies, waits for them, and re-layouts  2.4 us
    pallas_call x1, Pallas kernels, by_samples(): call(second_half_kernel, jax.ShapeDtypeStruct((groups, LANES), f32), [vme...  0.97 us
    pallas_call x1, Pallas kernels, by_samples(): call(functools.partial(sample_kernel, 0), (two, index), [vmem()] * 7)  0.54 us
  transfers between devices with their start and end apart: 7, of which 5 were waited for; matrix products, arithmetic and copies ran while one was open for 0% of the time, Pallas kernels for 9%

profile of v10, /device:TPU:0, one launch (start us, length us, event | category | flops | bytes accessed | tf_op | source)
XLA Modules:
  0.0 20.3 jit_solution(535754660797073195)
XLA Ops:
  0.0 0.5 %collective-permute-start = (bf16[3,17,2,2048]{3,2,1,0:T(2,128)(2,1)}, bf16[3,17,2,2048]{3,2,1,0:T(2,128)(2,1)S(1)}, u32[]{:S(2)}, u32[]{:S(2)}) collective-permute-start(bf16[3,17,2,2048]{3,2,1,0:T(2,128)(2,1)} %bitcast.28), channel_id=1, source_target_pairs={{0,1},{1,0},{2,3},{3,2},{4,5},{5,4},{6,7},{7,6},{8,9},{9,8},{10,11... | collective-permute-start | bytes 1253384 | tf_op jit(solution)/shard_map/ppermute | solution.py:339
  0.5 2.6 %collective-permute-start.2 = (bf16[136,512]{1,0:T(8,128)(2,1)}, bf16[136,512]{1,0:T(8,128)(2,1)S(1)}, u32[]{:S(2)}, u32[]{:S(2)}) collective-permute-start(bf16[136,512]{1,0:T(8,128)(2,1)} %bitcast.30), channel_id=1, source_target_pairs={{0,3},{1,2},{2,1},{3,0},{4,7},{5,6},{6,5},{7,4},{8,11},{9,10},{10,... | collective-permute-start | bytes 417800 | tf_op jit(solution)/shard_map/ppermute | solution.py:339
  3.1 0.0 collective-permute-start.1
  3.1 0.0 copy-start
  3.1 1.0 %copy-done = bf16[1,3,2,17,2048]{4,2,3,1,0:T(2,128)(2,1)S(1)} copy-done((bf16[1,3,2,17,2048]{4,2,3,1,0:T(2,128)(2,1)S(1)}, bf16[1,3,2,17,2048]{4,2,3,1,0:T(2,128)(2,1)}, u32[]{:S(2)}) %copy-start) | copy-done | bytes 417816
  4.1 0.1 shard_map.100.beam_own
  4.2 0.0 copy-start.1
  4.3 0.0 copy-start.7
  4.3 0.0 collective-permute-done.source
  4.3 0.1 shard_map.101.beam_other
  4.4 0.7 %copy-done.1 = bf16[1,17,512,8]{2,3,1,0:T(8,128)(2,1)S(1)} copy-done((bf16[1,17,512,8]{2,3,1,0:T(8,128)(2,1)S(1)}, bf16[1,17,512,8]{2,3,1,0:T(8,128)(2,1)}, u32[]{:S(2)}) %copy-start.1) | copy-done | bytes 139288
  5.1 0.0 copy-done.7
  5.2 0.2 %shard_map.102 = (f32[96,136]{1,0:T(8,128)S(1)}, f32[2,48,256]{2,1,0:T(8,128)S(1)}) custom-call(f32[3,2,24,1024]{3,2,1,0:T(8,128)S(1)} %shard_map.100.beam_own, f32[3,2,24,1024]{3,2,1,0:T(8,128)S(1)} %shard_map.101.beam_other, f32[3,2,1,512]{3,2,1,0:T(1,128)S(1)} %copy-done.7, bf16[136,512]{1,0:T(8,128)(2,1)S(1)} %bitcast.31), custom_call_target="tpu_custom_call" | custom-call | flops 1 | bytes 1 | tf_op jit(solution)/shard_map/pallas_call | solution.py:349
  5.4 2.2 %collective-permute-done.1.sky = f32[3,2,1,512]{3,2,1,0:T(1,128)S(1)} collective-permute-done((f32[3,2,1,512]{3,2,1,0:T(1,128)}, f32[3,2,1,512]{3,2,1,0:T(1,128)S(1)}, u32[]{:S(2)}, u32[]{:S(2)}) %collective-permute-start.1) | collective-permute-done | bytes 12320 | tf_op jit(solution)/shard_map/ppermute | solution.py:339
  7.6 0.0 collective-permute-done.2.w
  7.6 0.0 copy-start.2
  7.6 0.0 copy-start.4
  7.6 0.0 copy-start.5
  7.6 0.4 %shard_map.103 = f32[2,2,256]{2,1,0:T(2,128)S(1)} custom-call(f32[3,2,24,1024]{3,2,1,0:T(8,128)S(1)} %shard_map.100.beam_own, f32[3,2,24,1024]{3,2,1,0:T(8,128)S(1)} %shard_map.101.beam_other, f32[3,2,1,512]{3,2,1,0:T(1,128)S(1)} %collective-permute-done.1.sky, bf16[136,512]{1,0:T(8,128)(2,1)S(1)} %collective-permute-done.2.w, ...), custom_call_target="tpu_custom_call" | custom-call | flops 1 | bytes 1 | tf_op jit(solution)/shard_map/pallas_call | solution.py:357
  8.0 0.0 copy-start.3
  8.0 0.2 collective-permute-start.3
  8.2 1.1 %collective-permute-done.3 = f32[2,2,256]{2,1,0:T(2,128)S(1)} collective-permute-done((f32[2,2,256]{2,1,0:T(2,128)S(1)}, f32[2,2,256]{2,1,0:T(2,128)S(1)}, u32[]{:S(2)}, u32[]{:S(2)}) %collective-permute-start.3) | collective-permute-done | bytes 4128 | tf_op jit(solution)/shard_map/ppermute | solution.py:339
  9.2 1.3 %collective-permute-start.4 = (bf16[2,2,256]{2,1,0:T(2,128)(2,1)S(1)}, bf16[2,2,256]{2,1,0:T(2,128)(2,1)S(1)}, u32[]{:S(2)}, u32[]{:S(2)}) collective-permute-start(bf16[2,2,256]{2,1,0:T(2,128)(2,1)S(1)} %add_convert_fusion), channel_id=1, source_target_pairs={{0,5},{1,4},{2,7},{3,6},{4,1},{5,0},{6,3},{7,2},{8,13},{9,12},{10,... | collective-permute-start | bytes 6152 | tf_op jit(solution)/shard_map/ppermute | solution.py:339
  10.5 0.0 copy-start.6
  10.5 0.0 copy-start.8
  10.5 0.0 copy-start.9
  10.5 0.0 copy-done.2
  10.5 0.0 copy-done.4
  10.5 0.0 copy-done.5
  10.5 0.0 copy-done.3
  10.5 0.6 %copy-done.6 = s32[1,8,8,2]{2,3,1,0:T(2,128)S(1)} copy-done((s32[1,8,8,2]{2,3,1,0:T(2,128)S(1)}, s32[1,8,8,2]{2,3,1,0:T(2,128)}, u32[]{:S(2)}) %copy-start.6) | copy-done | bytes 536
  11.2 0.0 copy-done.8
  11.2 0.0 copy-done.9
  11.2 0.5 %shard_map.104 = (f32[2,32,8,128]{3,2,1,0:T(8,128)S(1)}, s32[32,128]{1,0:T(8,128)S(1)}) custom-call(s32[1,8]{1,0:T(1,128)S(1)} %bitcast.44, s32[3,8]{1,0:T(4,128)S(1)} %bitcast.42, s32[8,2,8]{2,1,0:T(2,128)S(1)} %bitcast.40, s32[32,128]{1,0:T(8,128)S(1)} %bitcast.34, s32[32,128]{1,0:T(8,128)S(1)} %bitcast.36, s32[32,128]{1,0:T(8,128)S(1)} %bitcast.38, ...), custom_call_target="tpu_custom_call" | custom-call | flops 1 | bytes 1 | tf_op jit(solution)/shard_map/pallas_call | solution.py:370
  11.7 0.5 %collective-permute-done.4 = bf16[2,2,256]{2,1,0:T(2,128)(2,1)S(1)} collective-permute-done((bf16[2,2,256]{2,1,0:T(2,128)(2,1)S(1)}, bf16[2,2,256]{2,1,0:T(2,128)(2,1)S(1)}, u32[]{:S(2)}, u32[]{:S(2)}) %collective-permute-start.4) | collective-permute-done | bytes 2080 | tf_op jit(solution)/shard_map/ppermute | solution.py:339
  12.2 1.4 %collective-permute-start.5 = (bf16[2,2,2,256]{3,2,1,0:T(2,128)(2,1)S(1)}, bf16[2,2,2,256]{3,2,1,0:T(2,128)(2,1)S(1)}, u32[]{:S(2)}, u32[]{:S(2)}) collective-permute-start(bf16[2,2,2,256]{3,2,1,0:T(2,128)(2,1)S(1)} %pad_maximum_fusion.held), channel_id=1, source_target_pairs={{0,9},{1,8},{2,11},{3,10},{4,13},{5,12},{6,15},{7,14},{8,1},{9,0},... | collective-permute-start | bytes 12296 | tf_op jit(solution)/shard_map/ppermute | solution.py:339
  13.6 0.3 %shard_map.105.phase = f32[2,32,8,128]{3,2,1,0:T(8,128)S(1)} custom-call(s32[1,8]{1,0:T(1,128)S(1)} %bitcast.45, s32[3,8]{1,0:T(4,128)S(1)} %bitcast.43, s32[8,2,8]{2,1,0:T(2,128)S(1)} %bitcast.41, s32[32,128]{1,0:T(8,128)S(1)} %bitcast.35, s32[32,128]{1,0:T(8,128)S(1)} %bitcast.37, s32[32,128]{1,0:T(8,128)S(1)} %bitcast.39, f32[2,32,128]{2,1,0:T(8,128)S(1)} %bitcast.33), custom_call_target="tpu_custom_call" | custom-call | flops 1 | bytes 1 | tf_op jit(solution)/shard_map/pallas_call | solution.py:377
  14.0 1.4 %collective-permute-done.5.received = bf16[2,2,2,256]{3,2,1,0:T(2,128)(2,1)S(1)} collective-permute-done((bf16[2,2,2,256]{3,2,1,0:T(2,128)(2,1)S(1)}, bf16[2,2,2,256]{3,2,1,0:T(2,128)(2,1)S(1)}, u32[]{:S(2)}, u32[]{:S(2)}) %collective-permute-start.5) | collective-permute-done | bytes 4128 | tf_op jit(solution)/shard_map/ppermute | solution.py:339
  15.4 2.4 %collective-permute-start.6 = (bf16[4,2,256]{2,1,0:T(2,128)(2,1)S(1)}, bf16[4,2,256]{2,1,0:T(2,128)(2,1)S(1)}, u32[]{:S(2)}, u32[]{:S(2)}) collective-permute-start(bf16[4,2,256]{2,1,0:T(2,128)(2,1)S(1)} %pad_maximum_fusion.1), channel_id=1, source_target_pairs={{0,17},{1,16},{2,19},{3,18},{4,21},{5,20},{6,23},{7,22},{8,25},{9,... | collective-permute-start | bytes 12296 | tf_op jit(solution)/shard_map/ppermute | solution.py:339
  17.8 0.3 %shard_map.106.first = f32[32,8,128]{2,1,0:T(8,128)S(1)} custom-call(bf16[2,2,2,256]{3,2,1,0:T(2,128)(2,1)S(1)} %pad_maximum_fusion.held, bf16[2,2,2,256]{3,2,1,0:T(2,128)(2,1)S(1)} %collective-permute-done.5.received, f32[2,32,8,128]{3,2,1,0:T(8,128)S(1)} %get-tuple-element.22.phase, s32[32,128]{1,0:T(8,128)S(1)} %get-tuple-element.23.low), custom_call_target="tpu_custom_call" | custom-call | flops 1 | bytes 1 | tf_op jit(solution)/shard_map/pallas_call | solution.py:380
  18.1 1.2 %collective-permute-done.6.received = bf16[4,2,256]{2,1,0:T(2,128)(2,1)S(1)} collective-permute-done((bf16[4,2,256]{2,1,0:T(2,128)(2,1)S(1)}, bf16[4,2,256]{2,1,0:T(2,128)(2,1)S(1)}, u32[]{:S(2)}, u32[]{:S(2)}) %collective-permute-start.6) | collective-permute-done | bytes 4128 | tf_op jit(solution)/shard_map/ppermute | solution.py:339
  19.4 1.0 %shard_map.107 = f32[32,128]{1,0:T(8,128)} custom-call(bf16[4,2,256]{2,1,0:T(2,128)(2,1)S(1)} %collective-permute-done.6.received, f32[32,8,128]{2,1,0:T(8,128)S(1)} %shard_map.106.first, f32[2,32,8,128]{3,2,1,0:T(8,128)S(1)} %shard_map.105.phase, s32[32,128]{1,0:T(8,128)S(1)} %get-tuple-element.23.low), custom_call_target="tpu_custom_call" | custom-call | flops 1 | bytes 1 | tf_op jit(solution)/shard_map/pallas_call | solution.py:381
  (6 shorter events, 0.0 us)
Async XLA Ops:
  0.0 4.3 %collective-permute-start = (bf16[3,17,2,2048]{3,2,1,0:T(2,128)(2,1)}, bf16[3,17,2,2048]{3,2,1,0:T(2,128)(2,1)S(1)}, u32[]{:S(2)}, u32[]{:S(2)}) collective-permute-start(bf16[3,17,2,2048]{3,2,1,0:T(2,128)(2,1)} %bitcast.28), channel_id=1, source_target_pairs={{0,1},{1,0},{2,3},{3,2},{4,5},{5,4},{6,7},{7,6},{8,9},{9,8},{10,11... | collective-permute-start | bytes 1253384 | tf_op jit(solution)/shard_map/ppermute | solution.py:339
  0.5 7.1 %collective-permute-start.2 = (bf16[136,512]{1,0:T(8,128)(2,1)}, bf16[136,512]{1,0:T(8,128)(2,1)S(1)}, u32[]{:S(2)}, u32[]{:S(2)}) collective-permute-start(bf16[136,512]{1,0:T(8,128)(2,1)} %bitcast.30), channel_id=1, source_target_pairs={{0,3},{1,2},{2,1},{3,0},{4,7},{5,6},{6,5},{7,4},{8,11},{9,10},{10,... | collective-permute-start | bytes 417800 | tf_op jit(solution)/shard_map/ppermute | solution.py:339
  3.1 4.5 %collective-permute-start.1 = (f32[3,2,1,512]{3,2,1,0:T(1,128)}, f32[3,2,1,512]{3,2,1,0:T(1,128)S(1)}, u32[]{:S(2)}, u32[]{:S(2)}) collective-permute-start(f32[3,2,1,512]{3,2,1,0:T(1,128)} %sky.1), channel_id=1, source_target_pairs={{0,3},{1,2},{2,1},{3,0},{4,7},{5,6},{6,5},{7,4},{8,11},{9,10},{10,... | collective-permute-start | bytes 36872 | tf_op jit(solution)/shard_map/ppermute | solution.py:339
  3.1 1.0 %copy-start = (bf16[1,3,2,17,2048]{4,2,3,1,0:T(2,128)(2,1)S(1)}, bf16[1,3,2,17,2048]{4,2,3,1,0:T(2,128)(2,1)}, u32[]{:S(2)}) copy-start(bf16[1,3,2,17,2048]{4,2,3,1,0:T(2,128)(2,1)} %param.11) | copy-start | bytes 1253380
  4.2 0.9 %copy-start.1 = (bf16[1,17,512,8]{2,3,1,0:T(8,128)(2,1)S(1)}, bf16[1,17,512,8]{2,3,1,0:T(8,128)(2,1)}, u32[]{:S(2)}) copy-start(bf16[1,17,512,8]{2,3,1,0:T(8,128)(2,1)} %param.12) | copy-start | bytes 417796
  4.3 0.9 %copy-start.7 = (f32[3,2,1,512]{3,2,1,0:T(1,128)S(1)}, f32[3,2,1,512]{3,2,1,0:T(1,128)}, u32[]{:S(2)}) copy-start(f32[3,2,1,512]{3,2,1,0:T(1,128)} %sky.1) | copy-start | bytes 36868
  7.6 2.9 %copy-start.2 = (f32[2,1,4096]{2,1,0:T(1,128)S(1)}, f32[2,1,4096]{2,1,0:T(1,128)}, u32[]{:S(2)}) copy-start(f32[2,1,4096]{2,1,0:T(1,128)} %param.19) | copy-start | bytes 98308
  7.6 2.9 %copy-start.4 = (s32[1,4096]{1,0:T(1,128)S(1)}, s32[1,4096]{1,0:T(1,128)}, u32[]{:S(2)}) copy-start(s32[1,4096]{1,0:T(1,128)} %param.17) | copy-start | bytes 49156
  7.6 2.9 %copy-start.5 = (s32[1,4096]{1,0:T(1,128)S(1)}, s32[1,4096]{1,0:T(1,128)}, u32[]{:S(2)}) copy-start(s32[1,4096]{1,0:T(1,128)} %param.18) | copy-start | bytes 49156
  8.0 2.6 %copy-start.3 = (s32[1,4096]{1,0:T(1,128)S(1)}, s32[1,4096]{1,0:T(1,128)}, u32[]{:S(2)}) copy-start(s32[1,4096]{1,0:T(1,128)} %param.16) | copy-start | bytes 49156
  8.0 1.2 %collective-permute-start.3 = (f32[2,2,256]{2,1,0:T(2,128)S(1)}, f32[2,2,256]{2,1,0:T(2,128)S(1)}, u32[]{:S(2)}, u32[]{:S(2)}) collective-permute-start(f32[2,2,256]{2,1,0:T(2,128)S(1)} %shard_map.103), channel_id=1, source_target_pairs={{0,1},{1,0},{2,3},{3,2},{4,5},{5,4},{6,7},{7,6},{8,9},{9,8},{10,11... | collective-permute-start | bytes 12296 | tf_op jit(solution)/shard_map/ppermute | solution.py:339
  9.2 3.0 %collective-permute-start.4 = (bf16[2,2,256]{2,1,0:T(2,128)(2,1)S(1)}, bf16[2,2,256]{2,1,0:T(2,128)(2,1)S(1)}, u32[]{:S(2)}, u32[]{:S(2)}) collective-permute-start(bf16[2,2,256]{2,1,0:T(2,128)(2,1)S(1)} %add_convert_fusion), channel_id=1, source_target_pairs={{0,5},{1,4},{2,7},{3,6},{4,1},{5,0},{6,3},{7,2},{8,13},{9,12},{10,... | collective-permute-start | bytes 6152 | tf_op jit(solution)/shard_map/ppermute | solution.py:339
  10.5 0.7 %copy-start.6 = (s32[1,8,8,2]{2,3,1,0:T(2,128)S(1)}, s32[1,8,8,2]{2,3,1,0:T(2,128)}, u32[]{:S(2)}) copy-start(s32[1,8,8,2]{2,3,1,0:T(2,128)} %param.15) | copy-start | bytes 1540
  10.5 0.7 %copy-start.8 = (s32[8,3]{0,1:T(4,128)S(1)}, s32[8,3]{0,1:T(4,128)}, u32[]{:S(2)}) copy-start(s32[8,3]{0,1:T(4,128)} %param.14) | copy-start | bytes 292
  10.5 0.7 %copy-start.9 = (s32[8]{0:T(128)S(1)}, s32[8]{0:T(128)}, u32[]{:S(2)}) copy-start(s32[8]{0:T(128)} %param.13) | copy-start | bytes 100
  12.2 3.1 %collective-permute-start.5 = (bf16[2,2,2,256]{3,2,1,0:T(2,128)(2,1)S(1)}, bf16[2,2,2,256]{3,2,1,0:T(2,128)(2,1)S(1)}, u32[]{:S(2)}, u32[]{:S(2)}) collective-permute-start(bf16[2,2,2,256]{3,2,1,0:T(2,128)(2,1)S(1)} %pad_maximum_fusion.held), channel_id=1, source_target_pairs={{0,9},{1,8},{2,11},{3,10},{4,13},{5,12},{6,15},{7,14},{8,1},{9,0},... | collective-permute-start | bytes 12296 | tf_op jit(solution)/shard_map/ppermute | solution.py:339
  15.4 4.0 %collective-permute-start.6 = (bf16[4,2,256]{2,1,0:T(2,128)(2,1)S(1)}, bf16[4,2,256]{2,1,0:T(2,128)(2,1)S(1)}, u32[]{:S(2)}, u32[]{:S(2)}) collective-permute-start(bf16[4,2,256]{2,1,0:T(2,128)(2,1)S(1)} %pad_maximum_fusion.1), channel_id=1, source_target_pairs={{0,17},{1,16},{2,19},{3,18},{4,21},{5,20},{6,23},{7,22},{8,25},{9,... | collective-permute-start | bytes 12296 | tf_op jit(solution)/shard_map/ppermute | solution.py:339
